TPU v7x, 128 devices: a whole 4x4x4 slice. The times are simulated.
128 devices in a mesh: dp: 32 (over y, x, z_hi), pair: 4 (over z_lo, core).
Axes of the slice: x: 4, y: 4, z: 4 (z_hi: 2, z_lo: 2; z = z_hi * 2 + z_lo), core: 2. Of those that a mesh axis runs over, the one named last changes fastest.
Arguments:
- picture_embedding: bfloat16 [16384, 1152], P(('dp', 'pair')), may hold values from -15 to 15
- caption_embedding: bfloat16 [16384, 1152], P(('dp', 'pair')), may hold values from -15 to 15
- logarithmic_scale_factor: float32 [1], replicated, may hold values from 4 to 4.5
- offset_shift: float32 [1], replicated, may hold values from -7 to -5
Outputs:
- image_gradient: float32 [16384, 1152], P(('dp', 'pair'))
- text_grad: float32 [16384, 1152], P(('dp', 'pair'))
- objective_results: float32 [3], replicated
All inputs are finite; a program needn't handle non-finite values.
Results may differ from a plain program's by a relative error of at most 0.0012.
Values may be sent and summed in bfloat16 or wider, within the bound.
No kernel may reach another device: no remote copies, remote signals or barrier semaphores. Data moves between devices by JAX's collectives and lax.ppermute only.
A program may use at most 128 MiB of HBM per device.

v0:
```python
import jax
import jax.numpy as jnp
from jax import lax
from jax.sharding import PartitionSpec as P

EPS = 1e-06


def normalize(embedding):
    widened = embedding.astype(jnp.float32)
    inverse = lax.rsqrt(jnp.sum(widened * widened, axis=1, keepdims=True) + EPS)
    return (widened * inverse, inverse)


def projection_helper(partial_value, unit_rows, inverse):
    radial = jnp.sum(partial_value * unit_rows, axis=1, keepdims=True)
    return (partial_value - radial * unit_rows) * inverse


def per_device(picture_embedding, caption_embedding, logarithmic_scale_factor, offset_shift):
    row_count = picture_embedding.shape[0]
    group_rows = row_count * lax.axis_size("pair")
    example_number = group_rows * lax.axis_size("dp")
    dp_index = lax.axis_index("dp")
    pair_index = lax.axis_index("pair")
    picture_entry, picture_reciprocal_length = normalize(picture_embedding)
    txt32, txt_inv = normalize(caption_embedding)
    img_unit = picture_entry.astype(jnp.bfloat16)
    caption_normalized_vectors = txt32.astype(jnp.bfloat16)
    scale_factor_current = jnp.exp(logarithmic_scale_factor[0])
    trained_offset = offset_shift[0]
    picture_examples = lax.all_gather(img_unit, "pair", axis=0, tiled=True)
    image_index = dp_index * group_rows + jnp.arange(group_rows, dtype=jnp.int32)
    texts = lax.all_gather(caption_normalized_vectors, "dp", axis=0, tiled=True)
    block_rows = texts.shape[0]
    gathered_index = jnp.arange(block_rows, dtype=jnp.int32)
    text_index = (
        gathered_index // row_count * group_rows
        + pair_index * row_count
        + gathered_index % row_count
    )
    couple_similarity = lax.dot_general(
        picture_examples, texts, (((1,), (1,)), ((), ())), preferred_element_type=jnp.float32
    )
    couple_similarity_raw = scale_factor_current * couple_similarity + trained_offset
    matched = image_index[:, None] == text_index[None, :]
    label_sign = jnp.where(matched, 1.0, -1.0).astype(jnp.float32)
    objective_accumulated = jnp.sum(jax.nn.softplus(-label_sign * couple_similarity_raw))
    pair_grads = jax.nn.sigmoid(couple_similarity_raw) - matched.astype(jnp.float32)
    derivative_scale_accum = jnp.sum(pair_grads * couple_similarity)
    derivative_accumulated = jnp.sum(pair_grads)
    couple_factor_matrix = pair_grads.astype(jnp.bfloat16)
    picture_share = jnp.dot(couple_factor_matrix, texts, preferred_element_type=jnp.float32)
    caption_share = scale_factor_current * lax.dot_general(
        couple_factor_matrix,
        picture_examples,
        (((0,), (0,)), ((), ())),
        preferred_element_type=jnp.float32,
    )
    caption_piece = caption_share
    totals = (
        picture_share,
        caption_piece,
        objective_accumulated,
        derivative_scale_accum,
        derivative_accumulated,
    )
    (
        picture_share,
        caption_piece,
        objective_accumulated,
        derivative_scale_accum,
        derivative_accumulated,
    ) = totals
    picture_derivative_accum = lax.psum_scatter(
        picture_share, "pair", scatter_dimension=0, tiled=True
    )
    image_gradient = projection_helper(
        scale_factor_current * picture_derivative_accum, picture_entry, picture_reciprocal_length
    )
    text_total = lax.psum_scatter(caption_piece, "dp", scatter_dimension=0, tiled=True)
    text_grad = projection_helper(text_total, txt32, txt_inv)
    objective_accumulated, derivative_scale_accum, derivative_accumulated = lax.psum(
        (objective_accumulated, derivative_scale_accum, derivative_accumulated), ("dp", "pair")
    )
    objective_results = jnp.stack(
        [
            objective_accumulated / example_number,
            scale_factor_current * derivative_scale_accum / example_number,
            derivative_accumulated / example_number,
        ]
    )
    return (image_gradient, text_grad, objective_results)


def solution(mesh):
    return jax.shard_map(
        per_device,
        mesh=mesh,
        in_specs=(P(("dp", "pair"), None), P(("dp", "pair"), None), P(), P()),
        out_specs=(P(("dp", "pair"), None), P(("dp", "pair"), None), P()),
        check_vma=False,
    )
```

profile of v0, /device:TPU:6, one launch (start us, length us, event | category | flops | bytes accessed | tf_op | source)
XLA Modules:
  0.0 501.9 jit_solution(136134122545390202)
XLA Ops:
  7.2 0.0 all-gather.3.cloned.1.call-start
  7.2 1.1 fusion.16
  8.3 1.8 fusion.12
  10.1 0.0 all-gather.3.cloned.1.call-update
  10.1 0.0 all-gather.5.cloned.1.call-start
  10.2 1.1 fusion.20
  11.3 1.8 fusion.9
  13.1 0.0 all-gather.5.cloned.1.call-update
  13.1 0.0 reduce-scatter.3.cloned.1.call-start
  14.6 19.7 %all-gather.3.cloned.1.call-done = bf16[512,1152]{1,0:T(8,128)(2,1)} async-done(((bf16[128,1152]{1,0:T(8,128)(2,1)}), bf16[512,1152]{1,0:T(8,128)(2,1)}) %all-gather.3.cloned.1.call-update) | async-done | bytes 1179664 | tf_op jit(solution)/shard_map/all_gather | solution.py:32
  34.2 115.8 %all-gather.5.cloned.1.call-done = bf16[4096,1152]{1,0:T(8,128)(2,1)} async-done(((bf16[128,1152]{1,0:T(8,128)(2,1)}), bf16[4096,1152]{1,0:T(8,128)(2,1)}) %all-gather.5.cloned.1.call-update) | async-done | bytes 9437200 | tf_op jit(solution)/shard_map/all_gather | solution.py:34
  150.0 0.0 copy-start.2
  150.0 17.1 %fusion.3 = (f32[]{:T(128)}, f32[]{:T(128)}, f32[]{:T(128)}, f32[512,4096]{1,0:T(8,128)S(1)}) fusion(s32[4096]{0:T(1024)S(1)} %fusion.29, f32[]{:T(128)} %bitcast.10, f32[]{:T(128)} %bitcast, s32[512]{0:T(512)S(1)} %iota_add_fusion, bf16[512,1152]{1,0:T(8,128)(2,1)} %all-gather.3.cloned.1.call-done, bf16[4096,1152]{1,0:T(8,128)(2,1)} %all-gather.5.cloned.1.call-done), kind=kOutput, calls=%fused_computation.7 | convolution fusion | flops 4875878400 | bytes 19023892 | tf_op jit(solution)/shard_map/dot_general | solution.py:42
  167.1 0.0 copy-start.4
  167.1 3.4 copy-done.4
  170.5 0.0 copy-done.2
  170.5 0.0 copy-start.3
  170.5 8.6 %fusion.5 = f32[512,1152]{1,0:T(8,128)} fusion(bf16[4096,1152]{1,0:T(8,128)(2,1)S(1)} %copy-done.2, f32[512,4096]{1,0:T(8,128)S(1)} %get-tuple-element.9, s32[4096]{0:T(1024)S(1)} %fusion.29, f32[]{:T(128)} %bitcast.9, f32[]{:T(128)} %bitcast, s32[512]{0:T(512)S(1)} %iota_add_fusion), kind=kOutput, calls=%fused_computation.11 | convolution fusion | flops 4850712576 | bytes 20203528 | tf_op jit(solution)/shard_map/dot_general | solution.py:53
  179.1 0.0 reduce-scatter.3.cloned.1.call-update
  179.1 0.2 reduce-scatter.5.cloned.1.call-start
  179.3 0.0 copy-done.3
  179.3 13.0 %convolution_multiply_fusion = f32[4096,1152]{1,0:T(8,128)} fusion(bf16[512,1152]{1,0:T(8,128)(2,1)S(1)} %copy-done.3, f32[]{:T(128)} %bitcast, f32[512,4096]{1,0:T(8,128)} %copy-done.4, s32[4096]{0:T(1024)S(1)} %fusion.29, f32[]{:T(128)} %bitcast.11, s32[512]{0:T(512)S(1)} %iota_add_fusion), kind=kOutput, calls=%fused_computation.1 | convolution fusion | flops 4855431168 | bytes 28461064 | tf_op jit(solution)/shard_map/dot_general | solution.py:54
  192.3 0.0 copy-start.1
  192.3 0.0 copy-start
  192.3 0.0 reduce-scatter.5.cloned.1.call-update
  192.3 64.1 %all-reduce = (f32[]{:T(128)}, f32[]{:T(128)}, f32[]{:T(128)}) all-reduce(f32[]{:T(128)} %get-tuple-element.4, f32[]{:T(128)} %get-tuple-element.5, f32[]{:T(128)} %get-tuple-element.3), channel_id=1, replica_groups=mesh['dp'=32,'pair'=4] {'dp','pair'}, use_global_device_ids=true, to_apply=%region_11.12 | all-reduce | flops 3 | bytes 24 | tf_op jit(solution)/shard_map/psum | solution.py:83
  258.4 0.6 pad_maximum_fusion
  259.0 0.0 reduce-scatter.3.cloned.1.call-done
  259.0 0.0 copy-done.1
  259.0 1.3 fusion.13
  260.3 2.1 fusion.15
  262.4 229.6 %reduce-scatter.5.cloned.1.call-done = f32[128,1152]{1,0:T(8,128)} async-done(((f32[4096,1152]{1,0:T(8,128)}), f32[128,1152]{1,0:T(8,128)}) %reduce-scatter.5.cloned.1.call-update) | async-done | bytes 589840 | tf_op jit(solution)/shard_map/reduce_scatter | solution.py:81
  492.0 0.0 copy-done
  492.0 1.3 fusion.17
  493.3 2.1 fusion.19
  (4 shorter events, 0.0 us)
Async XLA Ops:
  7.2 27.1 %all-gather.3.cloned.1.call-start = ((), (), s32[]{:S(2)}) async-start(), calls=%async_computation.2 | async-start | bytes 1474560 | tf_op jit(solution)/shard_map/all_gather | solution.py:32
  10.1 139.9 %all-gather.5.cloned.1.call-start = ((), (), s32[]{:S(2)}) async-start(), calls=%async_computation.3 | async-start | bytes 9732096 | tf_op jit(solution)/shard_map/all_gather | solution.py:34
  13.1 245.8 %reduce-scatter.3.cloned.1.call-start = ((), (), s32[]{:S(2)}) async-start(), calls=%async_computation.4 | async-start | bytes 2949120 | tf_op jit(solution)/shard_map/reduce_scatter | solution.py:75
  150.0 20.5 %copy-start.2 = (bf16[4096,1152]{1,0:T(8,128)(2,1)S(1)}, bf16[4096,1152]{1,0:T(8,128)(2,1)}, u32[]{:S(2)}) copy-start(bf16[4096,1152]{1,0:T(8,128)(2,1)} %all-gather.5.cloned.1.call-done) | copy-start | bytes 28311556
  167.1 3.4 copy-start.4
  170.5 8.8 %copy-start.3 = (bf16[512,1152]{1,0:T(8,128)(2,1)S(1)}, bf16[512,1152]{1,0:T(8,128)(2,1)}, u32[]{:S(2)}) copy-start(bf16[512,1152]{1,0:T(8,128)(2,1)} %all-gather.3.cloned.1.call-done) | copy-start | bytes 3538948
  179.1 312.9 %reduce-scatter.5.cloned.1.call-start = ((), (), s32[]{:S(2)}) async-start(), calls=%async_computation.5 | async-start | bytes 19464192 | tf_op jit(solution)/shard_map/reduce_scatter | solution.py:81
  192.3 66.7 %copy-start.1 = (bf16[128,1152]{1,0:T(8,128)(2,1)S(1)}, bf16[128,1152]{1,0:T(8,128)(2,1)}, u32[]{:S(2)}) copy-start(bf16[128,1152]{1,0:T(8,128)(2,1)} %param.4) | copy-start | bytes 884740
  192.3 299.7 %copy-start = (bf16[128,1152]{1,0:T(8,128)(2,1)S(1)}, bf16[128,1152]{1,0:T(8,128)(2,1)}, u32[]{:S(2)}) copy-start(bf16[128,1152]{1,0:T(8,128)(2,1)} %param.5) | copy-start | bytes 884740
Sparse Core Ops, SparseCore 0:
  10.3 23.9 all-gather.2
  37.8 112.1 all-gather.4
  179.2 28.5 reduce-scatter.2
  213.5 278.4 reduce-scatter.4
where the time goes:
time: 504 us; the launch traced here: 502 us
  waiting for transfers between devices  365 us (72%)
  blocking collectives  64.1 us (13%)
  matrix products  38.7 us (8%)
  between operations  17.1 us (3%)
  other arithmetic  13.2 us (3%)
    reduce_scatter x1, waiting for transfers between devices, per_device(): lax.psum_scatter(caption_piece, 'dp', scatter_dimension=0, tiled=True)  230 us
    all_gather x1, waiting for transfers between devices, per_device(): texts = lax.all_gather(caption_normalized_vectors, 'dp', axis=0, tiled=True)  116 us
    psum x1, blocking collectives, per_device(): lax.psum((objective_accumulated, derivative_scale_accum, derivative_accum...  64.1 us
    all_gather x1, waiting for transfers between devices, per_device(): picture_examples = lax.all_gather(img_unit, 'pair', axis=0, tiled=True)  19.7 us
    dot_general x1, matrix products, per_device(): lax.dot_general(picture_examples, texts, (((1,), (1,)), ((), ())), prefer...  17.1 us
    dot_general x1, matrix products, per_device(): lax.dot_general(couple_factor_matrix, picture_examples, (((0,), (0,)), ((...  13 us
  transfers between devices with their start and end apart: 4, of which 3 were waited for; matrix products, arithmetic and copies ran while one was open for 4% of the time, Pallas kernels for 0%

commit v1 on v0

v1 whole, which is shorter than its diff:
```python
import jax
import jax.numpy as jnp
from jax import lax
from jax.experimental import pallas as pl
from jax.experimental.pallas import tpu as pltpu
from jax.sharding import Mesh, PartitionSpec as P

EPS = 1e-06
AXES = ("y", "x", "zh", "zl", "c")
Z = ("zh", "zl")
Z_IMAGE = [(0, 1), (1, 0), (2, 3), (3, 2)]
Z_TEXT = [(1, 2), (2, 1), (3, 0), (0, 3)]
UP = [(i, (i + 1) % 4) for i in range(4)]
DOWN = [(i, (i - 1) % 4) for i in range(4)]
SWAP = [(0, 1), (1, 0)]
SCALE = 4.0
TILE = 256


def send(value, axis, pairs):
    return lax.ppermute(value, axis, pairs)


def normalize(embedding):
    widened = embedding.astype(jnp.float32)
    inverse = lax.rsqrt(jnp.sum(widened * widened, axis=1, keepdims=True) + EPS)
    return (widened * inverse, inverse)


def projection(total, unit_rows, inverse):
    radial = jnp.sum(total * unit_rows, axis=1, keepdims=True)
    return (total - radial * unit_rows) * inverse


def gather_ring(block, axis):
    from_down = send(block, axis, UP)
    from_up = send(block, axis, DOWN)
    half = block.shape[0] // 2
    far_first = send(from_down[:half], axis, UP)
    far_second = send(from_up[half:], axis, DOWN)
    return from_down, from_up, jnp.concatenate([far_first, far_second], axis=0)


def pair_kernel(scalars, images, texts, weights, sums):
    step = pl.program_id(0)
    temperature = scalars[0]
    offset = scalars[1]

    @pl.when(step == 0)
    def _():
        sums[...] = jnp.zeros_like(sums)

    for m in range(images.shape[0] // TILE):
        rows = pl.ds(m * TILE, TILE)
        scores = lax.dot_general(
            images[rows, :], texts[...], (((1,), (1,)), ((), ())), preferred_element_type=jnp.float32
        )
        logits = scores * temperature + offset
        small = jnp.exp(-jnp.abs(logits))
        inverse = 1.0 / (1.0 + small)
        gradient = jnp.where(logits >= 0.0, inverse, small * inverse)
        signed = logits
        if m == 0:
            row = lax.broadcasted_iota(jnp.int32, (TILE, TILE), 0)
            column = lax.broadcasted_iota(jnp.int32, (TILE, TILE), 1) + step * TILE
            matched = (row == column) & (row < 128)
            signed = jnp.where(matched, -logits, logits)
            gradient = jnp.where(matched, gradient - 1.0, gradient)
        product = small
        while product.shape[0] > 8:
            half = product.shape[0] // 2
            left, right = product[:half], product[half:]
            product = left + right + left * right
        relu = jnp.maximum(signed, 0.0)
        loss = jnp.log1p(product) + jnp.sum(relu.reshape(TILE // 8, 8, TILE), axis=0)
        slope = jnp.sum((gradient * scores).reshape(TILE // 8, 8, TILE), axis=0)
        total = jnp.sum(gradient.reshape(TILE // 8, 8, TILE), axis=0)
        sums[0] += loss
        sums[1] += slope
        sums[2] += total
        weights[rows, :] = gradient.astype(jnp.bfloat16)


def pair_weights(scalars, images, texts):
    n_images, n_texts, width = images.shape[0], texts.shape[0], images.shape[1]
    return pl.pallas_call(
        pair_kernel,
        grid=(n_texts // TILE,),
        in_specs=[
            pl.BlockSpec(memory_space=pltpu.SMEM),
            pl.BlockSpec((n_images, width), lambda j: (0, 0)),
            pl.BlockSpec((TILE, width), lambda j: (j, 0)),
        ],
        out_specs=[
            pl.BlockSpec((n_images, TILE), lambda j: (0, j)),
            pl.BlockSpec((3, 8, TILE), lambda j: (0, 0, 0)),
        ],
        out_shape=[
            jax.ShapeDtypeStruct((n_images, n_texts), jnp.bfloat16),
            jax.ShapeDtypeStruct((3, 8, TILE), jnp.float32),
        ],
        compiler_params=pltpu.CompilerParams(vmem_limit_bytes=32 * 1024 * 1024),
        cost_estimate=pl.CostEstimate(
            flops=2 * n_images * n_texts * width, bytes_accessed=8 << 20, transcendentals=2 * n_images * n_texts
        ),
    )(scalars, images, texts)


def narrow(value):
    return value.astype(jnp.float16)


def wide(value):
    return value.astype(jnp.float32)


def scatter_ring(own, low, high, far, axis):
    half = far.shape[0] // 2
    for_low = send(narrow(far[:half]), axis, DOWN)
    for_high = send(narrow(far[half:]), axis, UP)
    low = jnp.concatenate([low[:half] + wide(for_low), low[half:]], axis=0)
    high = jnp.concatenate([high[:half], high[half:] + wide(for_high)], axis=0)
    from_high = send(narrow(low), axis, DOWN)
    from_low = send(narrow(high), axis, UP)
    return own + wide(from_high) + wide(from_low)


def all_sum(value):
    for axis, pairs in (
        ("c", SWAP),
        ("x", [(0, 1), (1, 0), (2, 3), (3, 2)]),
        ("y", [(0, 1), (1, 0), (2, 3), (3, 2)]),
        (Z, Z_IMAGE),
        ("x", [(1, 2), (2, 1), (3, 0), (0, 3)]),
        ("y", [(1, 2), (2, 1), (3, 0), (0, 3)]),
        (Z, Z_TEXT),
    ):
        value = value + send(value, axis, pairs)
    return value


def per_device(picture_embedding, caption_embedding, logarithmic_scale_factor, offset_shift):
    example_number = picture_embedding.shape[0] * 128
    image32, image_inverse = normalize(picture_embedding)
    text32, text_inverse = normalize(caption_embedding)
    image = image32.astype(jnp.bfloat16)
    text = text32.astype(jnp.bfloat16)
    temperature = jnp.exp(logarithmic_scale_factor[0])
    scalars = jnp.stack([temperature, offset_shift[0]])

    image_own = jnp.concatenate([image, send(image, Z, Z_IMAGE)], axis=0)
    text_own = jnp.concatenate([text, send(text, Z, Z_TEXT)], axis=0)
    images = jnp.concatenate([image_own, *gather_ring(image_own, "x")], axis=0)
    texts_own = jnp.concatenate([text_own, *gather_ring(text_own, "y")], axis=0)
    texts = jnp.concatenate([texts_own, send(texts_own, "c", SWAP)], axis=0)

    weights, sums = pair_weights(scalars, images, texts)
    objective = all_sum(jnp.sum(sums, axis=(1, 2)).reshape(1, 3))[0]
    objective_results = objective * jnp.stack([jnp.float32(1.0), temperature, jnp.float32(1.0)]) / example_number

    block = image_own.shape[0]
    image_parts = [
        SCALE * jnp.dot(weights[i * block : (i + 1) * block], texts, preferred_element_type=jnp.float32)
        for i in range(4)
    ]

    def text_part(first):
        mine = SCALE * lax.dot_general(
            weights[:, first : first + block], images, (((0,), (0,)), ((), ())), preferred_element_type=jnp.float32
        )
        return mine

    text_parts = []
    for i in range(4):
        other = send(narrow(text_part(4 * block + i * block)), "c", SWAP)
        text_parts.append(text_part(i * block) + wide(other))

    def finish(parts, axis, pairs, unit_rows, inverse):
        total = scatter_ring(*parts, axis)
        half = block // 2
        total = total[:half] + wide(send(narrow(total[half:]), Z, pairs))
        return projection(total * (temperature / SCALE), unit_rows, inverse)

    image_gradient = finish(image_parts, "x", Z_IMAGE, image32, image_inverse)
    text_grad = finish(text_parts, "y", Z_TEXT, text32, text_inverse)
    return (image_gradient, text_grad, objective_results)


def solution(mesh):
    mesh = Mesh(mesh.devices.reshape(4, 4, 2, 2, 2), AXES)
    return jax.shard_map(
        per_device,
        mesh=mesh,
        in_specs=(P(AXES, None), P(AXES, None), P(), P()),
        out_specs=(P(AXES, None), P(AXES, None), P()),
        check_vma=False,
    )
```

time: 504 us -> 188 us (0.37)
  waiting for transfers between devices: 365 us -> 110 us
  blocking collectives: 64.1 us -> 0 us
  starting transfers between devices: 0.34 us -> 33.8 us
  matrix products: 38.7 us -> 19.7 us
  between operations: 17.1 us -> 2.42 us
  Pallas kernels: 0 us -> 12.4 us
  other arithmetic: 13.2 us -> 8.01 us
    reduce_scatter x2 -> x0, waiting for transfers between devices: 230 us -> none  [the longest x1 230 us: per_device(): lax.psum_scatter(caption_piece, 'dp', scatter_dimension=0, tiled=True)]
    all_gather x2 -> x0, waiting for transfers between devices: 135 us -> none  [the longest x1 116 us: per_device(): texts = lax.all_gather(caption_normalized_vectors, 'dp', axis=0, tiled=True)]
    ppermute x0 -> x32, waiting for transfers between devices: none -> 110 us  [send(): return lax.ppermute(value, axis, pairs)]
    psum x1 -> x0, blocking collectives: 64.1 us -> none  [per_device(): lax.psum((objective_accumulated, derivative_scale_accum, derivative_accum...]
    ppermute x0 -> x32, starting transfers between devices: none -> 33.8 us  [send(): return lax.ppermute(value, axis, pairs)]
    dot_general x3 -> x12, matrix products: 38.7 us -> 19.7 us  [the longest x8 11.4 us: text_part(): lax.dot_general(weights[:, first:first + block], images, (((0,), (0,)), (...]
    pallas_call x0 -> x1, Pallas kernels: none -> 12.4 us  [pair_weights(): pl.pallas_call(pair_kernel, grid=(n_texts // TILE,), in_specs=[pl.BlockSp...]
  transfers between devices with their start and end apart: 4 -> 32, of which waited for: 3 -> 18; matrix products, arithmetic and copies ran while one was open for 4% -> 6% of each run, Pallas kernels for 0% -> 0%
where the time goes in v1:
time: 188 us; the launch traced here: 187 us
  waiting for transfers between devices  110 us (59%)
  starting transfers between devices  33.8 us (18%)
  matrix products  19.7 us (10%)
  Pallas kernels  12.4 us (7%)
  other arithmetic  8.01 us (4%)
  between operations  2.42 us (1%)
    ppermute x32, waiting for transfers between devices, send(): return lax.ppermute(value, axis, pairs)  110 us
    ppermute x32, starting transfers between devices, send(): return lax.ppermute(value, axis, pairs)  33.8 us
    pallas_call x1, Pallas kernels, pair_weights(): pl.pallas_call(pair_kernel, grid=(n_texts // TILE,), in_specs=[pl.BlockSp...  12.4 us
    dot_general x8, matrix products, text_part(): lax.dot_general(weights[:, first:first + block], images, (((0,), (0,)), (...  11.4 us
    dot_general x4, matrix products, per_device(): jnp.dot(weights[i * block:(i + 1) * block], texts, preferred_element_type...  8.35 us
  transfers between devices with their start and end apart: 32, of which 18 were waited for; matrix products, arithmetic and copies ran while one was open for 6% of the time, Pallas kernels for 0%

profile of v1, /device:TPU:6, one launch (start us, length us, event | category | flops | bytes accessed | tf_op | source)
XLA Modules:
  0.0 187.3 jit_solution(8708448597840063884)
XLA Ops:
  0.6 1.1 fusion.31
  1.7 1.1 constant_dynamic-update-slice_fusion.11
  2.8 4.1 %collective-permute-start.5 = (bf16[128,1152]{1,0:T(8,128)(2,1)S(1)}, bf16[128,1152]{1,0:T(8,128)(2,1)S(1)}, u32[]{:S(2)}, u32[]{:S(2)}) collective-permute-start(bf16[128,1152]{1,0:T(8,128)(2,1)S(1)} %get-tuple-element.10), channel_id=1, source_target_pairs={{2,4},{4,2},{6,0},{0,6},{3,5},{5,3},{7,1},{1,7},{10,12},{12,10},{1... | collective-permute-start | bytes 884744 | tf_op jit(solution)/shard_map/ppermute | solution.py:21
  6.9 1.1 fusion.27
  8.0 5.9 %collective-permute-done.5 = bf16[128,1152]{1,0:T(8,128)(2,1)S(1)} collective-permute-done((bf16[128,1152]{1,0:T(8,128)(2,1)S(1)}, bf16[128,1152]{1,0:T(8,128)(2,1)S(1)}, u32[]{:S(2)}, u32[]{:S(2)}) %collective-permute-start.5) | collective-permute-done | bytes 294944 | tf_op jit(solution)/shard_map/ppermute | solution.py:21
  14.0 1.6 collective-permute-start.6
  15.7 1.7 collective-permute-start.7
  17.4 12.4 %collective-permute-done.6 = bf16[256,1152]{1,0:T(8,128)(2,1)S(1)} collective-permute-done((bf16[256,1152]{1,0:T(8,128)(2,1)S(1)}, bf16[256,1152]{1,0:T(8,128)(2,1)S(1)}, u32[]{:S(2)}, u32[]{:S(2)}) %collective-permute-start.6) | collective-permute-done | bytes 589856 | tf_op jit(solution)/shard_map/ppermute | solution.py:21
  29.9 0.4 collective-permute-start.8
  30.3 3.0 %collective-permute-start.9 = (bf16[128,1152]{1,0:T(8,128)(2,1)S(1)}, bf16[128,1152]{1,0:T(8,128)(2,1)S(1)}, u32[]{:S(2)}, u32[]{:S(2)}) collective-permute-start(bf16[128,1152]{1,0:T(8,128)(2,1)S(1)} %slice.141), channel_id=1, source_target_pairs={{0,96},{32,0},{64,32},{96,64},{1,97},{33,1},{65,33},{97,65},{2,98}... | collective-permute-start | bytes 884744 | tf_op jit(solution)/shard_map/ppermute | solution.py:21
  33.3 0.2 constant_dynamic-update-slice_fusion.9
  33.5 0.2 constant_dynamic-update-slice_fusion.8
  33.6 4.9 %collective-permute-done.8 = bf16[128,1152]{1,0:T(8,128)(2,1)S(1)} collective-permute-done((bf16[128,1152]{1,0:T(8,128)(2,1)S(1)}, bf16[128,1152]{1,0:T(8,128)(2,1)S(1)}, u32[]{:S(2)}, u32[]{:S(2)}) %collective-permute-start.8) | collective-permute-done | bytes 294944 | tf_op jit(solution)/shard_map/ppermute | solution.py:21
  39.0 9.4 %collective-permute-done = bf16[128,1152]{1,0:T(8,128)(2,1)S(1)} collective-permute-done((bf16[128,1152]{1,0:T(8,128)(2,1)S(1)}, bf16[128,1152]{1,0:T(8,128)(2,1)S(1)}, u32[]{:S(2)}, u32[]{:S(2)}) %collective-permute-start) | collective-permute-done | bytes 294944 | tf_op jit(solution)/shard_map/ppermute | solution.py:21
  48.4 0.5 collective-permute-start.1
  48.9 1.5 collective-permute-start.2
  51.9 11.5 %collective-permute-done.1 = bf16[256,1152]{1,0:T(8,128)(2,1)S(1)} collective-permute-done((bf16[256,1152]{1,0:T(8,128)(2,1)S(1)}, bf16[256,1152]{1,0:T(8,128)(2,1)S(1)}, u32[]{:S(2)}, u32[]{:S(2)}) %collective-permute-start.1) | collective-permute-done | bytes 589856 | tf_op jit(solution)/shard_map/ppermute | solution.py:21
  63.4 1.8 collective-permute-start.3
  65.2 0.6 collective-permute-start.4
  66.0 5.3 %collective-permute-done.3 = bf16[128,1152]{1,0:T(8,128)(2,1)S(1)} collective-permute-done((bf16[128,1152]{1,0:T(8,128)(2,1)S(1)}, bf16[128,1152]{1,0:T(8,128)(2,1)S(1)}, u32[]{:S(2)}, u32[]{:S(2)}) %collective-permute-start.3) | collective-permute-done | bytes 294944 | tf_op jit(solution)/shard_map/ppermute | solution.py:21
  71.3 2.9 %collective-permute-done.4 = bf16[128,1152]{1,0:T(8,128)(2,1)S(1)} collective-permute-done((bf16[128,1152]{1,0:T(8,128)(2,1)S(1)}, bf16[128,1152]{1,0:T(8,128)(2,1)S(1)}, u32[]{:S(2)}, u32[]{:S(2)}) %collective-permute-start.4) | collective-permute-done | bytes 294944 | tf_op jit(solution)/shard_map/ppermute | solution.py:21
  74.2 0.4 constant_dynamic-update-slice_fusion.12.texts
  74.6 12.4 %shard_map.67 = (bf16[1024,2048]{1,0:T(8,128)(2,1)S(1)}, f32[3,8,256]{2,1,0:T(8,128)S(1)}) custom-call(f32[2]{0:T(128)S(1)} %pad_maximum_fusion.6.scalars, bf16[1024,1152]{1,0:T(8,128)(2,1)S(1)} %constant_dynamic-update-slice_fusion.images, bf16[2048,1152]{1,0:T(8,128)(2,1)S(1)} %constant_dynamic-update-slice_fusion.12.texts), custom_call_target="tpu_custom_call" | custom-call | flops 4831838208 | bytes 8388608 | tf_op jit(solution)/shard_map/pallas_call | solution.py:86
  87.0 2.2 %fusion.9 = f16[256,1152]{1,0:T(8,128)(2,1)} fusion(bf16[1024,1152]{1,0:T(8,128)(2,1)S(1)} %constant_dynamic-update-slice_fusion.images, bf16[1024,2048]{1,0:T(8,128)(2,1)S(1)} %get-tuple-element.5), kind=kOutput, calls=%fused_computation.21 | convolution fusion | flops 604569600 | bytes 3473408 | tf_op jit(solution)/shard_map/dot_general | solution.py:168
  89.2 1.7 fusion.10
  90.9 1.7 fusion.11
  92.6 2.6 %convolution_multiply_fusion.10 = f32[256,1152]{1,0:T(8,128)} fusion(bf16[2048,1152]{1,0:T(8,128)(2,1)S(1)} %constant_dynamic-update-slice_fusion.12.texts, bf16[1024,2048]{1,0:T(8,128)(2,1)S(1)} %get-tuple-element.5), kind=kOutput, calls=%fused_computation.14 | convolution fusion | flops 1208254464 | bytes 6946816 | tf_op jit(solution)/shard_map/dot_general | solution.py:163
  95.2 1.5 fusion.8
  96.7 2.6 %convolution_multiply_fusion.8 = f32[256,1152]{1,0:T(8,128)} fusion(bf16[2048,1152]{1,0:T(8,128)(2,1)S(1)} %constant_dynamic-update-slice_fusion.12.texts, bf16[1024,2048]{1,0:T(8,128)(2,1)S(1)} %get-tuple-element.5), kind=kOutput, calls=%fused_computation.12 | convolution fusion | flops 1208254464 | bytes 6946816 | tf_op jit(solution)/shard_map/dot_general | solution.py:163
  99.5 0.5 collective-permute-start.16
  100.1 0.4 collective-permute-start.18
  100.7 2.0 %fusion.12 = f16[256,1152]{1,0:T(8,128)(2,1)S(1)} fusion(bf16[1024,1152]{1,0:T(8,128)(2,1)S(1)} %constant_dynamic-update-slice_fusion.images, bf16[1024,2048]{1,0:T(8,128)(2,1)} %copy-done), kind=kOutput, calls=%fused_computation.24 | convolution fusion | flops 604569600 | bytes 3473408 | tf_op jit(solution)/shard_map/dot_general | solution.py:168
  102.7 8.2 %collective-permute-done.11 = f16[128,1152]{1,0:T(8,128)(2,1)S(1)} collective-permute-done((f16[128,1152]{1,0:T(8,128)(2,1)S(1)}, f16[128,1152]{1,0:T(8,128)(2,1)S(1)}, u32[]{:S(2)}, u32[]{:S(2)}) %collective-permute-start.11) | collective-permute-done | bytes 294944 | tf_op jit(solution)/shard_map/ppermute | solution.py:21
  111.0 8.0 %collective-permute-done.13 = f16[128,1152]{1,0:T(8,128)(2,1)S(1)} collective-permute-done((f16[128,1152]{1,0:T(8,128)(2,1)S(1)}, f16[128,1152]{1,0:T(8,128)(2,1)S(1)}, u32[]{:S(2)}, u32[]{:S(2)}) %collective-permute-start.13) | collective-permute-done | bytes 294944 | tf_op jit(solution)/shard_map/ppermute | solution.py:21
  119.2 0.1 pad_maximum_fusion.2
  119.6 0.9 fusion.2
  120.5 3.5 %collective-permute-start.14 = (f16[256,1152]{1,0:T(8,128)(2,1)S(1)}, f16[256,1152]{1,0:T(8,128)(2,1)S(1)}, u32[]{:S(2)}, u32[]{:S(2)}) collective-permute-start(f16[256,1152]{1,0:T(8,128)(2,1)S(1)} %pad_maximum_fusion.3), channel_id=1, source_target_pairs={{0,8},{8,16},{16,24},{24,0},{1,9},{9,17},{17,25},{25,1},{2,10},{10... | collective-permute-start | bytes 1769480 | tf_op jit(solution)/shard_map/ppermute | solution.py:21
  124.0 0.9 fusion.13
  125.1 3.1 %collective-permute-start.19 = (f16[128,1152]{1,0:T(8,128)(2,1)S(1)}, f16[128,1152]{1,0:T(8,128)(2,1)S(1)}, u32[]{:S(2)}, u32[]{:S(2)}) collective-permute-start(f16[128,1152]{1,0:T(8,128)(2,1)S(1)} %get-tuple-element.19), channel_id=1, source_target_pairs={{0,96},{32,0},{64,32},{96,64},{1,97},{33,1},{65,33},{97,65},{2,98}... | collective-permute-start | bytes 884744 | tf_op jit(solution)/shard_map/ppermute | solution.py:21
  128.1 0.9 fusion
  129.0 5.5 %collective-permute-done.19 = f16[128,1152]{1,0:T(8,128)(2,1)S(1)} collective-permute-done((f16[128,1152]{1,0:T(8,128)(2,1)S(1)}, f16[128,1152]{1,0:T(8,128)(2,1)S(1)}, u32[]{:S(2)}, u32[]{:S(2)}) %collective-permute-start.19) | collective-permute-done | bytes 294944 | tf_op jit(solution)/shard_map/ppermute | solution.py:21
  134.7 9.7 %collective-permute-done.22 = f16[128,1152]{1,0:T(8,128)(2,1)S(1)} collective-permute-done((f16[128,1152]{1,0:T(8,128)(2,1)S(1)}, f16[128,1152]{1,0:T(8,128)(2,1)S(1)}, u32[]{:S(2)}, u32[]{:S(2)}) %collective-permute-start.22) | collective-permute-done | bytes 294944 | tf_op jit(solution)/shard_map/ppermute | solution.py:21
  144.4 1.7 collective-permute-start.20
  146.4 0.4 collective-permute-start.23
  146.8 1.7 fusion.7
  148.5 0.8 collective-permute-start.15
  149.4 3.5 %collective-permute-done.26 = f32[1,3]{1,0:T(1,128)S(1)} collective-permute-done((f32[1,3]{1,0:T(1,128)S(1)}, f32[1,3]{1,0:T(1,128)S(1)}, u32[]{:S(2)}, u32[]{:S(2)}) %collective-permute-start.26) | collective-permute-done | bytes 44 | tf_op jit(solution)/shard_map/ppermute | solution.py:21
  153.0 5.2 %collective-permute-done.27 = f32[1,3]{1,0:T(1,128)S(1)} collective-permute-done((f32[1,3]{1,0:T(1,128)S(1)}, f32[1,3]{1,0:T(1,128)S(1)}, u32[]{:S(2)}, u32[]{:S(2)}) %collective-permute-start.27) | collective-permute-done | bytes 44 | tf_op jit(solution)/shard_map/ppermute | solution.py:21
  158.2 0.7 collective-permute-start.28
  158.9 2.8 %collective-permute-done.28 = f32[1,3]{1,0:T(1,128)S(1)} collective-permute-done((f32[1,3]{1,0:T(1,128)S(1)}, f32[1,3]{1,0:T(1,128)S(1)}, u32[]{:S(2)}, u32[]{:S(2)}) %collective-permute-start.28) | collective-permute-done | bytes 44 | tf_op jit(solution)/shard_map/ppermute | solution.py:21
  161.7 0.4 collective-permute-start.29
  162.1 4.4 %collective-permute-done.29 = f32[1,3]{1,0:T(1,128)S(1)} collective-permute-done((f32[1,3]{1,0:T(1,128)S(1)}, f32[1,3]{1,0:T(1,128)S(1)}, u32[]{:S(2)}, u32[]{:S(2)}) %collective-permute-start.29) | collective-permute-done | bytes 44 | tf_op jit(solution)/shard_map/ppermute | solution.py:21
  166.5 1.8 collective-permute-start.30
  168.3 3.0 %collective-permute-done.30 = f32[1,3]{1,0:T(1,128)S(1)} collective-permute-done((f32[1,3]{1,0:T(1,128)S(1)}, f32[1,3]{1,0:T(1,128)S(1)}, u32[]{:S(2)}, u32[]{:S(2)}) %collective-permute-start.30) | collective-permute-done | bytes 44 | tf_op jit(solution)/shard_map/ppermute | solution.py:21
  171.2 2.3 %collective-permute-start.31 = (f32[1,3]{1,0:T(1,128)S(1)}, f32[1,3]{1,0:T(1,128)S(1)}, u32[]{:S(2)}, u32[]{:S(2)}) collective-permute-start(f32[1,3]{1,0:T(1,128)S(1)} %add.100), channel_id=1, source_target_pairs={{2,4},{4,2},{6,0},{0,6},{3,5},{5,3},{7,1},{1,7},{10,12},{12,10},{1... | collective-permute-start | bytes 44 | tf_op jit(solution)/shard_map/ppermute | solution.py:21
  173.6 2.4 %collective-permute-done.31 = f32[1,3]{1,0:T(1,128)S(1)} collective-permute-done((f32[1,3]{1,0:T(1,128)S(1)}, f32[1,3]{1,0:T(1,128)S(1)}, u32[]{:S(2)}, u32[]{:S(2)}) %collective-permute-start.31) | collective-permute-done | bytes 44 | tf_op jit(solution)/shard_map/ppermute | solution.py:21
  176.0 0.6 fusion.46
  176.6 0.3 fusion.24
  176.9 1.1 fusion.5
  178.0 2.4 %collective-permute-start.24 = (f16[128,1152]{1,0:T(8,128)(2,1)S(1)}, f16[128,1152]{1,0:T(8,128)(2,1)S(1)}, u32[]{:S(2)}, u32[]{:S(2)}) collective-permute-start(f16[128,1152]{1,0:T(8,128)(2,1)S(1)} %slice_convert_fusion), channel_id=1, source_target_pairs={{2,4},{4,2},{6,0},{0,6},{3,5},{5,3},{7,1},{1,7},{10,12},{12,10},{1... | collective-permute-start | bytes 884744 | tf_op jit(solution)/shard_map/ppermute | solution.py:21
  180.4 1.1 fusion.26
  181.5 4.5 %collective-permute-done.24 = f16[128,1152]{1,0:T(8,128)(2,1)S(1)} collective-permute-done((f16[128,1152]{1,0:T(8,128)(2,1)S(1)}, f16[128,1152]{1,0:T(8,128)(2,1)S(1)}, u32[]{:S(2)}, u32[]{:S(2)}) %collective-permute-start.24) | collective-permute-done | bytes 294944 | tf_op jit(solution)/shard_map/ppermute | solution.py:21
  186.0 0.3 fusion.28
  186.3 1.1 fusion.30
  (81 shorter events, 2.7 us)
Async XLA Ops:
  2.8 11.1 %collective-permute-start.5 = (bf16[128,1152]{1,0:T(8,128)(2,1)S(1)}, bf16[128,1152]{1,0:T(8,128)(2,1)S(1)}, u32[]{:S(2)}, u32[]{:S(2)}) collective-permute-start(bf16[128,1152]{1,0:T(8,128)(2,1)S(1)} %get-tuple-element.10), channel_id=1, source_target_pairs={{2,4},{4,2},{6,0},{0,6},{3,5},{5,3},{7,1},{1,7},{10,12},{12,10},{1... | collective-permute-start | bytes 884744 | tf_op jit(solution)/shard_map/ppermute | solution.py:21
  14.0 15.9 %collective-permute-start.6 = (bf16[256,1152]{1,0:T(8,128)(2,1)S(1)}, bf16[256,1152]{1,0:T(8,128)(2,1)S(1)}, u32[]{:S(2)}, u32[]{:S(2)}) collective-permute-start(bf16[256,1152]{1,0:T(8,128)(2,1)S(1)} %pad_maximum_fusion.1), channel_id=1, source_target_pairs={{0,32},{32,64},{64,96},{96,0},{1,33},{33,65},{65,97},{97,1},{2,34}... | collective-permute-start | bytes 1769480 | tf_op jit(solution)/shard_map/ppermute | solution.py:21
  15.7 14.6 %collective-permute-start.7 = (bf16[256,1152]{1,0:T(8,128)(2,1)S(1)}, bf16[256,1152]{1,0:T(8,128)(2,1)S(1)}, u32[]{:S(2)}, u32[]{:S(2)}) collective-permute-start(bf16[256,1152]{1,0:T(8,128)(2,1)S(1)} %pad_maximum_fusion.1), channel_id=1, source_target_pairs={{0,96},{32,0},{64,32},{96,64},{1,97},{33,1},{65,33},{97,65},{2,98}... | collective-permute-start | bytes 1769480 | tf_op jit(solution)/shard_map/ppermute | solution.py:21
  29.9 8.6 %collective-permute-start.8 = (bf16[128,1152]{1,0:T(8,128)(2,1)S(1)}, bf16[128,1152]{1,0:T(8,128)(2,1)S(1)}, u32[]{:S(2)}, u32[]{:S(2)}) collective-permute-start(bf16[128,1152]{1,0:T(8,128)(2,1)S(1)} %slice.140), channel_id=1, source_target_pairs={{0,32},{32,64},{64,96},{96,0},{1,33},{33,65},{65,97},{97,1},{2,34}... | collective-permute-start | bytes 884744 | tf_op jit(solution)/shard_map/ppermute | solution.py:21
  30.3 8.3 %collective-permute-start.9 = (bf16[128,1152]{1,0:T(8,128)(2,1)S(1)}, bf16[128,1152]{1,0:T(8,128)(2,1)S(1)}, u32[]{:S(2)}, u32[]{:S(2)}) collective-permute-start(bf16[128,1152]{1,0:T(8,128)(2,1)S(1)} %slice.141), channel_id=1, source_target_pairs={{0,96},{32,0},{64,32},{96,64},{1,97},{33,1},{65,33},{97,65},{2,98}... | collective-permute-start | bytes 884744 | tf_op jit(solution)/shard_map/ppermute | solution.py:21
  33.3 5.4 %copy-start.3 = (bf16[128,1152]{1,0:T(8,128)(2,1)S(1)}, bf16[128,1152]{1,0:T(8,128)(2,1)}, u32[]{:S(2)}) copy-start(bf16[128,1152]{1,0:T(8,128)(2,1)} %param.4) | copy-start | bytes 884740
  38.6 35.5 %collective-permute-start.10 = (bf16[1024,1152]{1,0:T(8,128)(2,1)S(1)}, bf16[1024,1152]{1,0:T(8,128)(2,1)S(1)}, u32[]{:S(2)}, u32[]{:S(2)}) collective-permute-start(bf16[1024,1152]{1,0:T(8,128)(2,1)S(1)} %get-tuple-element.27), channel_id=1, source_target_pairs={{0,1},{1,0},{2,3},{3,2},{4,5},{5,4},{6,7},{7,6},{8,9},{9,8},{10,11... | collective-permute-start | bytes 7077896 | tf_op jit(solution)/shard_map/ppermute | solution.py:21
  38.9 9.5 %collective-permute-start = (bf16[128,1152]{1,0:T(8,128)(2,1)S(1)}, bf16[128,1152]{1,0:T(8,128)(2,1)S(1)}, u32[]{:S(2)}, u32[]{:S(2)}) collective-permute-start(bf16[128,1152]{1,0:T(8,128)(2,1)S(1)} %get-tuple-element.8), channel_id=1, source_target_pairs={{0,2},{2,0},{4,6},{6,4},{1,3},{3,1},{5,7},{7,5},{8,10},{10,8},{12,... | collective-permute-start | bytes 884744 | tf_op jit(solution)/shard_map/ppermute | solution.py:21
  48.4 15.0 %collective-permute-start.1 = (bf16[256,1152]{1,0:T(8,128)(2,1)S(1)}, bf16[256,1152]{1,0:T(8,128)(2,1)S(1)}, u32[]{:S(2)}, u32[]{:S(2)}) collective-permute-start(bf16[256,1152]{1,0:T(8,128)(2,1)S(1)} %pad_maximum_fusion), channel_id=1, source_target_pairs={{0,8},{8,16},{16,24},{24,0},{1,9},{9,17},{17,25},{25,1},{2,10},{10... | collective-permute-start | bytes 1769480 | tf_op jit(solution)/shard_map/ppermute | solution.py:21
  48.9 16.3 %collective-permute-start.2 = (bf16[256,1152]{1,0:T(8,128)(2,1)S(1)}, bf16[256,1152]{1,0:T(8,128)(2,1)S(1)}, u32[]{:S(2)}, u32[]{:S(2)}) collective-permute-start(bf16[256,1152]{1,0:T(8,128)(2,1)S(1)} %pad_maximum_fusion), channel_id=1, source_target_pairs={{0,24},{8,0},{16,8},{24,16},{1,25},{9,1},{17,9},{25,17},{2,26},{10... | collective-permute-start | bytes 1769480 | tf_op jit(solution)/shard_map/ppermute | solution.py:21
  63.4 7.8 %collective-permute-start.3 = (bf16[128,1152]{1,0:T(8,128)(2,1)S(1)}, bf16[128,1152]{1,0:T(8,128)(2,1)S(1)}, u32[]{:S(2)}, u32[]{:S(2)}) collective-permute-start(bf16[128,1152]{1,0:T(8,128)(2,1)S(1)} %slice.138), channel_id=1, source_target_pairs={{0,8},{8,16},{16,24},{24,0},{1,9},{9,17},{17,25},{25,1},{2,10},{10... | collective-permute-start | bytes 884744 | tf_op jit(solution)/shard_map/ppermute | solution.py:21
  65.2 8.9 %collective-permute-start.4 = (bf16[128,1152]{1,0:T(8,128)(2,1)S(1)}, bf16[128,1152]{1,0:T(8,128)(2,1)S(1)}, u32[]{:S(2)}, u32[]{:S(2)}) collective-permute-start(bf16[128,1152]{1,0:T(8,128)(2,1)S(1)} %slice.139), channel_id=1, source_target_pairs={{0,24},{8,0},{16,8},{24,16},{1,25},{9,1},{17,9},{25,17},{2,26},{10... | collective-permute-start | bytes 884744 | tf_op jit(solution)/shard_map/ppermute | solution.py:21
  74.6 22.2 %copy-start.2 = (bf16[2048,1152]{1,0:T(8,128)(2,1)}, bf16[2048,1152]{1,0:T(8,128)(2,1)S(1)}, u32[]{:S(2)}) copy-start(bf16[2048,1152]{1,0:T(8,128)(2,1)S(1)} %constant_dynamic-update-slice_fusion.12.texts) | copy-start | bytes 14155780
  87.0 9.8 %copy-start = (bf16[1024,2048]{1,0:T(8,128)(2,1)}, bf16[1024,2048]{1,0:T(8,128)(2,1)S(1)}, u32[]{:S(2)}) copy-start(bf16[1024,2048]{1,0:T(8,128)(2,1)S(1)} %get-tuple-element.5) | copy-start | bytes 12582916
  99.4 11.5 %copy-start.6 = (f32[256,1152]{1,0:T(8,128)S(1)}, f32[256,1152]{1,0:T(8,128)}, u32[]{:S(2)}) copy-start(f32[256,1152]{1,0:T(8,128)} %convolution_multiply_fusion.10) | copy-start | bytes 3538948
  99.4 49.9 %collective-permute-start.25 = (f32[1,3]{1,0:T(1,128)S(1)}, f32[1,3]{1,0:T(1,128)S(1)}, u32[]{:S(2)}, u32[]{:S(2)}) collective-permute-start(f32[1,3]{1,0:T(1,128)S(1)} %bitcast.19), channel_id=1, source_target_pairs={{0,1},{1,0},{2,3},{3,2},{4,5},{5,4},{6,7},{7,6},{8,9},{9,8},{10,11... | collective-permute-start | bytes 44 | tf_op jit(solution)/shard_map/ppermute | solution.py:21
  99.5 77.4 %collective-permute-start.16 = (f16[256,1152]{1,0:T(8,128)(2,1)}, f16[256,1152]{1,0:T(8,128)(2,1)S(1)}, u32[]{:S(2)}, u32[]{:S(2)}) collective-permute-start(f16[256,1152]{1,0:T(8,128)(2,1)} %fusion.9), channel_id=1, source_target_pairs={{0,1},{1,0},{2,3},{3,2},{4,5},{5,4},{6,7},{7,6},{8,9},{9,8},{10,11... | collective-permute-start | bytes 1769480 | tf_op jit(solution)/shard_map/ppermute | solution.py:21
  100.0 19.5 %collective-permute-start.17 = (f16[256,1152]{1,0:T(8,128)(2,1)}, f16[256,1152]{1,0:T(8,128)(2,1)S(1)}, u32[]{:S(2)}, u32[]{:S(2)}) collective-permute-start(f16[256,1152]{1,0:T(8,128)(2,1)} %fusion.10), channel_id=1, source_target_pairs={{0,1},{1,0},{2,3},{3,2},{4,5},{5,4},{6,7},{7,6},{8,9},{9,8},{10,11... | collective-permute-start | bytes 1769480 | tf_op jit(solution)/shard_map/ppermute | solution.py:21
  100.1 20.4 %collective-permute-start.18 = (f16[256,1152]{1,0:T(8,128)(2,1)}, f16[256,1152]{1,0:T(8,128)(2,1)S(1)}, u32[]{:S(2)}, u32[]{:S(2)}) collective-permute-start(f16[256,1152]{1,0:T(8,128)(2,1)} %fusion.11), channel_id=1, source_target_pairs={{0,1},{1,0},{2,3},{3,2},{4,5},{5,4},{6,7},{7,6},{8,9},{9,8},{10,11... | collective-permute-start | bytes 1769480 | tf_op jit(solution)/shard_map/ppermute | solution.py:21
  100.6 18.5 %copy-start.5 = (f32[256,1152]{1,0:T(8,128)S(1)}, f32[256,1152]{1,0:T(8,128)}, u32[]{:S(2)}) copy-start(f32[256,1152]{1,0:T(8,128)} %convolution_multiply_fusion.8) | copy-start | bytes 3538948
  100.6 10.3 %collective-permute-start.11 = (f16[128,1152]{1,0:T(8,128)(2,1)S(1)}, f16[128,1152]{1,0:T(8,128)(2,1)S(1)}, u32[]{:S(2)}, u32[]{:S(2)}) collective-permute-start(f16[128,1152]{1,0:T(8,128)(2,1)S(1)} %get-tuple-element.21), channel_id=1, source_target_pairs={{0,24},{8,0},{16,8},{24,16},{1,25},{9,1},{17,9},{25,17},{2,26},{10... | collective-permute-start | bytes 884744 | tf_op jit(solution)/shard_map/ppermute | solution.py:21
  110.9 8.2 %collective-permute-start.13 = (f16[128,1152]{1,0:T(8,128)(2,1)S(1)}, f16[128,1152]{1,0:T(8,128)(2,1)S(1)}, u32[]{:S(2)}, u32[]{:S(2)}) collective-permute-start(f16[128,1152]{1,0:T(8,128)(2,1)S(1)} %get-tuple-element.22), channel_id=1, source_target_pairs={{0,8},{8,16},{16,24},{24,0},{1,9},{9,17},{17,25},{25,1},{2,10},{10... | collective-permute-start | bytes 884744 | tf_op jit(solution)/shard_map/ppermute | solution.py:21
  111.0 8.5 %copy-start.1 = (bf16[1024,2048]{1,0:T(8,128)(2,1)S(1)}, bf16[1024,2048]{1,0:T(8,128)(2,1)}, u32[]{:S(2)}) copy-start(bf16[1024,2048]{1,0:T(8,128)(2,1)} %copy-done) | copy-start | bytes 12582916
  119.1 6.0 %collective-permute-start.21 = (f16[256,1152]{1,0:T(8,128)(2,1)S(1)}, f16[256,1152]{1,0:T(8,128)(2,1)S(1)}, u32[]{:S(2)}, u32[]{:S(2)}) collective-permute-start(f16[256,1152]{1,0:T(8,128)(2,1)S(1)} %fusion.12), channel_id=1, source_target_pairs={{0,1},{1,0},{2,3},{3,2},{4,5},{5,4},{6,7},{7,6},{8,9},{9,8},{10,11... | collective-permute-start | bytes 1769480 | tf_op jit(solution)/shard_map/ppermute | solution.py:21
  119.5 26.9 %collective-permute-start.12 = (f16[256,1152]{1,0:T(8,128)(2,1)S(1)}, f16[256,1152]{1,0:T(8,128)(2,1)S(1)}, u32[]{:S(2)}, u32[]{:S(2)}) collective-permute-start(f16[256,1152]{1,0:T(8,128)(2,1)S(1)} %pad_maximum_fusion.2), channel_id=1, source_target_pairs={{0,24},{8,0},{16,8},{24,16},{1,25},{9,1},{17,9},{25,17},{2,26},{10... | collective-permute-start | bytes 1769480 | tf_op jit(solution)/shard_map/ppermute | solution.py:21
  120.5 26.3 %collective-permute-start.14 = (f16[256,1152]{1,0:T(8,128)(2,1)S(1)}, f16[256,1152]{1,0:T(8,128)(2,1)S(1)}, u32[]{:S(2)}, u32[]{:S(2)}) collective-permute-start(f16[256,1152]{1,0:T(8,128)(2,1)S(1)} %pad_maximum_fusion.3), channel_id=1, source_target_pairs={{0,8},{8,16},{16,24},{24,0},{1,9},{9,17},{17,25},{25,1},{2,10},{10... | collective-permute-start | bytes 1769480 | tf_op jit(solution)/shard_map/ppermute | solution.py:21
  124.0 22.8 %slice-start = ((s8[4718592]{0:T(1024)(128)(4,1)}), s8[4194304]{0:T(1024)(128)(4,1)S(1)}, s32[]{:S(2)}) async-start(s8[4718592]{0:T(1024)(128)(4,1)} %bitcast.17), calls=%async_computation | async-start | bytes 8388608
  125.0 21.8 %slice-start.1 = ((s8[4718592]{0:T(1024)(128)(4,1)}), s8[524288]{0:T(1024)(128)(4,1)S(1)}, s32[]{:S(2)}) async-start(s8[4718592]{0:T(1024)(128)(4,1)} %bitcast.17), calls=%async_computation.1 | async-start | bytes 1048576
  125.1 9.4 %collective-permute-start.19 = (f16[128,1152]{1,0:T(8,128)(2,1)S(1)}, f16[128,1152]{1,0:T(8,128)(2,1)S(1)}, u32[]{:S(2)}, u32[]{:S(2)}) collective-permute-start(f16[128,1152]{1,0:T(8,128)(2,1)S(1)} %get-tuple-element.19), channel_id=1, source_target_pairs={{0,96},{32,0},{64,32},{96,64},{1,97},{33,1},{65,33},{97,65},{2,98}... | collective-permute-start | bytes 884744 | tf_op jit(solution)/shard_map/ppermute | solution.py:21
  134.5 9.9 %collective-permute-start.22 = (f16[128,1152]{1,0:T(8,128)(2,1)S(1)}, f16[128,1152]{1,0:T(8,128)(2,1)S(1)}, u32[]{:S(2)}, u32[]{:S(2)}) collective-permute-start(f16[128,1152]{1,0:T(8,128)(2,1)S(1)} %get-tuple-element.20), channel_id=1, source_target_pairs={{0,32},{32,64},{64,96},{96,0},{1,33},{33,65},{65,97},{97,1},{2,34}... | collective-permute-start | bytes 884744 | tf_op jit(solution)/shard_map/ppermute | solution.py:21
  144.4 32.4 %collective-permute-start.20 = (f16[256,1152]{1,0:T(8,128)(2,1)S(1)}, f16[256,1152]{1,0:T(8,128)(2,1)S(1)}, u32[]{:S(2)}, u32[]{:S(2)}) collective-permute-start(f16[256,1152]{1,0:T(8,128)(2,1)S(1)} %pad_maximum_fusion.4), channel_id=1, source_target_pairs={{0,96},{32,0},{64,32},{96,64},{1,97},{33,1},{65,33},{97,65},{2,98}... | collective-permute-start | bytes 1769480 | tf_op jit(solution)/shard_map/ppermute | solution.py:21
  146.4 30.4 %collective-permute-start.23 = (f16[256,1152]{1,0:T(8,128)(2,1)S(1)}, f16[256,1152]{1,0:T(8,128)(2,1)S(1)}, u32[]{:S(2)}, u32[]{:S(2)}) collective-permute-start(f16[256,1152]{1,0:T(8,128)(2,1)S(1)} %pad_maximum_fusion.5), channel_id=1, source_target_pairs={{0,32},{32,64},{64,96},{96,0},{1,33},{33,65},{65,97},{97,1},{2,34}... | collective-permute-start | bytes 1769480 | tf_op jit(solution)/shard_map/ppermute | solution.py:21
  148.5 28.0 %collective-permute-start.15 = (f16[128,1152]{1,0:T(8,128)(2,1)S(1)}, f16[128,1152]{1,0:T(8,128)(2,1)S(1)}, u32[]{:S(2)}, u32[]{:S(2)}) collective-permute-start(f16[128,1152]{1,0:T(8,128)(2,1)S(1)} %slice_convert_fusion.3), channel_id=1, source_target_pairs={{0,2},{2,0},{4,6},{6,4},{1,3},{3,1},{5,7},{7,5},{8,10},{10,8},{12,... | collective-permute-start | bytes 884744 | tf_op jit(solution)/shard_map/ppermute | solution.py:21
  149.4 3.5 %collective-permute-start.26 = (f32[1,3]{1,0:T(1,128)S(1)}, f32[1,3]{1,0:T(1,128)S(1)}, u32[]{:S(2)}, u32[]{:S(2)}) collective-permute-start(f32[1,3]{1,0:T(1,128)S(1)} %bitcast_add_fusion), channel_id=1, source_target_pairs={{0,8},{8,0},{16,24},{24,16},{1,9},{9,1},{17,25},{25,17},{2,10},{10... | collective-permute-start | bytes 44 | tf_op jit(solution)/shard_map/ppermute | solution.py:21
  152.9 5.3 %collective-permute-start.27 = (f32[1,3]{1,0:T(1,128)S(1)}, f32[1,3]{1,0:T(1,128)S(1)}, u32[]{:S(2)}, u32[]{:S(2)}) collective-permute-start(f32[1,3]{1,0:T(1,128)S(1)} %add.96), channel_id=1, source_target_pairs={{0,32},{32,0},{64,96},{96,64},{1,33},{33,1},{65,97},{97,65},{2,34}... | collective-permute-start | bytes 44 | tf_op jit(solution)/shard_map/ppermute | solution.py:21
  158.2 3.5 %collective-permute-start.28 = (f32[1,3]{1,0:T(1,128)S(1)}, f32[1,3]{1,0:T(1,128)S(1)}, u32[]{:S(2)}, u32[]{:S(2)}) collective-permute-start(f32[1,3]{1,0:T(1,128)S(1)} %add.97), channel_id=1, source_target_pairs={{0,2},{2,0},{4,6},{6,4},{1,3},{3,1},{5,7},{7,5},{8,10},{10,8},{12,... | collective-permute-start | bytes 44 | tf_op jit(solution)/shard_map/ppermute | solution.py:21
  161.7 4.8 %collective-permute-start.29 = (f32[1,3]{1,0:T(1,128)S(1)}, f32[1,3]{1,0:T(1,128)S(1)}, u32[]{:S(2)}, u32[]{:S(2)}) collective-permute-start(f32[1,3]{1,0:T(1,128)S(1)} %add.98), channel_id=1, source_target_pairs={{8,16},{16,8},{24,0},{0,24},{9,17},{17,9},{25,1},{1,25},{10,18},{1... | collective-permute-start | bytes 44 | tf_op jit(solution)/shard_map/ppermute | solution.py:21
  166.5 4.8 %collective-permute-start.30 = (f32[1,3]{1,0:T(1,128)S(1)}, f32[1,3]{1,0:T(1,128)S(1)}, u32[]{:S(2)}, u32[]{:S(2)}) collective-permute-start(f32[1,3]{1,0:T(1,128)S(1)} %add.99), channel_id=1, source_target_pairs={{32,64},{64,32},{96,0},{0,96},{33,65},{65,33},{97,1},{1,97},{34,66... | collective-permute-start | bytes 44 | tf_op jit(solution)/shard_map/ppermute | solution.py:21
  171.2 4.8 %collective-permute-start.31 = (f32[1,3]{1,0:T(1,128)S(1)}, f32[1,3]{1,0:T(1,128)S(1)}, u32[]{:S(2)}, u32[]{:S(2)}) collective-permute-start(f32[1,3]{1,0:T(1,128)S(1)} %add.100), channel_id=1, source_target_pairs={{2,4},{4,2},{6,0},{0,6},{3,5},{5,3},{7,1},{1,7},{10,12},{12,10},{1... | collective-permute-start | bytes 44 | tf_op jit(solution)/shard_map/ppermute | solution.py:21
  177.9 8.1 %copy-start.4 = (bf16[128,1152]{1,0:T(8,128)(2,1)S(1)}, bf16[128,1152]{1,0:T(8,128)(2,1)}, u32[]{:S(2)}) copy-start(bf16[128,1152]{1,0:T(8,128)(2,1)} %param.5) | copy-start | bytes 884740
  178.0 8.0 %collective-permute-start.24 = (f16[128,1152]{1,0:T(8,128)(2,1)S(1)}, f16[128,1152]{1,0:T(8,128)(2,1)S(1)}, u32[]{:S(2)}, u32[]{:S(2)}) collective-permute-start(f16[128,1152]{1,0:T(8,128)(2,1)S(1)} %slice_convert_fusion), channel_id=1, source_target_pairs={{2,4},{4,2},{6,0},{0,6},{3,5},{5,3},{7,1},{1,7},{10,12},{12,10},{1... | collective-permute-start | bytes 884744 | tf_op jit(solution)/shard_map/ppermute | solution.py:21

commit v2 on v1

v2 whole, which is shorter than its diff:
```python
import functools

import jax
import jax.numpy as jnp
from jax import lax
from jax.experimental import pallas as pl
from jax.experimental.pallas import tpu as pltpu
from jax.sharding import Mesh, PartitionSpec as P

EPS = 1e-06
AXES = ("y", "x", "zh", "zl", "c")
Z = ("zh", "zl")
EVEN = [(0, 1), (1, 0), (2, 3), (3, 2)]
ODD = [(1, 2), (2, 1), (3, 0), (0, 3)]
UP = [(i, (i + 1) % 4) for i in range(4)]
DOWN = [(i, (i - 1) % 4) for i in range(4)]
SWAP = [(0, 1), (1, 0)]
SCALE = 4.0
TILE = 256
LOG2E = 1.4426950408889634
LN2 = 0.6931471805599453


def send(value, axis, pairs):
    return lax.ppermute(value, axis, pairs)


def fence(*values):
    return lax.optimization_barrier(values)


def normalize(embedding):
    widened = embedding.astype(jnp.float32)
    inverse = lax.rsqrt(jnp.sum(widened * widened, axis=1, keepdims=True) + EPS)
    return (widened * inverse, inverse)


def projection(total, unit_rows, inverse):
    radial = jnp.sum(total * unit_rows, axis=1, keepdims=True)
    return (total - radial * unit_rows) * inverse


def by_eight(value):
    return jnp.sum(value.reshape(value.shape[0] // 8, 8, value.shape[1]), axis=0)


def pair_kernel(n_images, n_texts, tiles, diagonal, scalars, *refs):
    images, texts = refs[:n_images], refs[n_images : n_images + n_texts]
    weights, sums = refs[n_images + n_texts :]
    factor = scalars[0] * LOG2E
    offset = scalars[1] * LOG2E
    totals = [jnp.zeros((8, TILE), jnp.float32) for _ in range(4)]
    for t, (i, j) in enumerate(tiles):
        scores = lax.dot_general(
            images[i][...], texts[j][...], (((1,), (1,)), ((), ())), preferred_element_type=jnp.float32
        )
        logits = scores * factor + offset
        small = jnp.exp2(-jnp.abs(logits))
        denominator = 1.0 + small
        guess = pl.reciprocal(denominator, approx=True)
        inverse = guess * (2.0 - denominator * guess)
        gradient = jnp.where(logits >= 0.0, inverse, small * inverse)
        signed = logits
        if t == diagonal:
            row = lax.broadcasted_iota(jnp.int32, (TILE, TILE), 0)
            column = lax.broadcasted_iota(jnp.int32, (TILE, TILE), 1)
            matched = (row == column) & (row < TILE // 2)
            signed = jnp.where(matched, -logits, logits)
            gradient = jnp.where(matched, gradient - 1.0, gradient)
        product = small
        while product.shape[0] > 8:
            half = product.shape[0] // 2
            left, right = product[:half], product[half:]
            product = left + right + left * right
        totals[0] += jnp.log1p(product)
        totals[1] += by_eight(jnp.maximum(signed, 0.0))
        totals[2] += by_eight(gradient * scores)
        totals[3] += by_eight(gradient)
        weights[t] = gradient.astype(jnp.bfloat16)
    sums[0] = totals[0] + LN2 * totals[1]
    sums[1] = totals[2]
    sums[2] = totals[3]


def pair_weights(scalars, images, texts, tiles, diagonal=None):
    vmem = pl.BlockSpec(memory_space=pltpu.VMEM)
    n = len(tiles)
    return pl.pallas_call(
        functools.partial(pair_kernel, len(images), len(texts), tiles, diagonal),
        in_specs=[pl.BlockSpec(memory_space=pltpu.SMEM)] + [vmem] * (len(images) + len(texts)),
        out_specs=[vmem, vmem],
        out_shape=[
            jax.ShapeDtypeStruct((n, TILE, TILE), jnp.bfloat16),
            jax.ShapeDtypeStruct((3, 8, TILE), jnp.float32),
        ],
        compiler_params=pltpu.CompilerParams(vmem_limit_bytes=24 * 1024 * 1024),
        cost_estimate=pl.CostEstimate(
            flops=2 * n * TILE * TILE * 1152, bytes_accessed=n << 18, transcendentals=2 * n * TILE * TILE
        ),
    )(scalars, *images, *texts)


def direction_kernel(n_images, n_texts, n_weights, image_out, text_out, where, *refs):
    images, texts = refs[:n_images], refs[n_images : n_images + n_texts]
    weights = refs[n_images + n_texts : n_images + n_texts + n_weights]
    outs = refs[n_images + n_texts + n_weights :]
    for o, i in enumerate(image_out):
        total = None
        for j in range(n_texts):
            a, t = where[i, j]
            term = lax.dot_general(
                weights[a][t], texts[j][...], (((1,), (0,)), ((), ())), preferred_element_type=jnp.float32
            )
            total = term if total is None else total + term
        outs[o][...] = SCALE * total
    for o, j in enumerate(text_out):
        total = None
        for i in range(n_images):
            a, t = where[i, j]
            term = lax.dot_general(
                weights[a][t], images[i][...], (((0,), (0,)), ((), ())), preferred_element_type=jnp.float32
            )
            total = term if total is None else total + term
        outs[len(image_out) + o][...] = SCALE * total


def directions(images, texts, weights, where, image_out, text_out):
    vmem = pl.BlockSpec(memory_space=pltpu.VMEM)
    n_out = len(image_out) + len(text_out)
    n_dots = len(image_out) * len(texts) + len(text_out) * len(images)
    return pl.pallas_call(
        functools.partial(
            direction_kernel, len(images), len(texts), len(weights), tuple(image_out), tuple(text_out), where
        ),
        in_specs=[vmem] * (len(images) + len(texts) + len(weights)),
        out_specs=[vmem] * n_out,
        out_shape=[jax.ShapeDtypeStruct((TILE, 1152), jnp.float32)] * n_out,
        compiler_params=pltpu.CompilerParams(vmem_limit_bytes=24 * 1024 * 1024),
        cost_estimate=pl.CostEstimate(
            flops=2 * n_dots * TILE * TILE * 1152, bytes_accessed=n_dots << 18, transcendentals=0
        ),
    )(*images, *texts, *weights)


def narrow(value):
    return value.astype(jnp.float16)


def wide(value):
    return value.astype(jnp.float32)


def per_device(picture_embedding, caption_embedding, logarithmic_scale_factor, offset_shift):
    rows = picture_embedding.shape[0]
    example_number = rows * 128
    image32, image_inverse = normalize(picture_embedding)
    text32, text_inverse = normalize(caption_embedding)
    image = image32.astype(jnp.bfloat16)
    text = text32.astype(jnp.bfloat16)
    temperature = jnp.exp(logarithmic_scale_factor[0])
    scalars = jnp.stack([temperature, offset_shift[0]])

    image, text = fence(image, text)
    image_z, text_z = fence(send(image, Z, EVEN), send(text, Z, ODD))
    i_own = jnp.concatenate([image, image_z], axis=0)
    t_own = jnp.concatenate([text, text_z], axis=0)

    i_low, i_high, t_low, t_high, s_own = fence(
        send(i_own, "x", UP),
        send(i_own, "x", DOWN),
        send(t_own, "y", UP),
        send(t_own, "y", DOWN),
        send(t_own, "c", SWAP),
    )

    far = [
        send(i_low[:rows], "x", UP),
        send(i_high[rows:], "x", DOWN),
        send(t_low[:rows], "y", UP),
        send(t_high[rows:], "y", DOWN),
    ]
    s_near = send(jnp.concatenate([t_low, t_high], axis=0), "c", SWAP)
    near_images = [i_own, i_low, i_high]
    near_texts = [t_own, t_low, t_high, s_own]
    tiles_a = [(i, j) for j in range(4) for i in range(3)]
    weights_a, sums_a = pair_weights(scalars, near_images, near_texts, tiles_a, 0)
    weights_a, s_near = fence(weights_a, s_near)
    s_low, s_high = s_near[: 2 * rows], s_near[2 * rows :]
    tiles_b = [(i, j) for j in range(2) for i in range(3)]
    weights_b, sums_b = pair_weights(scalars, near_images, [s_low, s_high], tiles_b)
    *far, weights_a, weights_b = fence(*far, weights_a, weights_b)
    i_far = jnp.concatenate(far[:2], axis=0)
    t_far = jnp.concatenate(far[2:], axis=0)
    s_far = send(t_far, "c", SWAP)

    images = [i_own, i_low, i_high, i_far]
    texts = [t_own, t_low, t_high, s_own, s_low, s_high, t_far]
    tiles_c = [(3, j) for j in range(7)] + [(i, 6) for i in range(3)]
    weights_c, sums_c = pair_weights(scalars, images, texts, tiles_c)
    weights_c, s_far = fence(weights_c, s_far)
    tiles_d = [(i, 0) for i in range(4)]
    weights_d, sums_d = pair_weights(scalars, images, [s_far], tiles_d)
    texts = texts + [s_far]
    where = {p: (0, t) for t, p in enumerate(tiles_a)}
    where |= {(i, j + 4): (1, t) for t, (i, j) in enumerate(tiles_b)}
    where |= {p: (2, t) for t, p in enumerate(tiles_c)}
    where |= {(i, 7): (3, t) for t, (i, _) in enumerate(tiles_d)}
    weights = [weights_a, weights_b, weights_c, weights_d]

    value = jnp.sum(sums_a + sums_b + sums_c + sums_d, axis=(1, 2)).reshape(1, 3)
    (ps_far,) = directions(images, texts, weights, where, [], [7])
    *weights, ps_far = fence(*weights, ps_far)
    ps_back = send(narrow(ps_far), "c", SWAP)
    (pi_far,) = directions(images, texts, weights, where, [3], [])
    *weights, pi_far = fence(*weights, pi_far)
    back_x = [send(narrow(pi_far[:rows]), "x", DOWN), send(narrow(pi_far[rows:]), "x", UP)]
    (pt_far,) = directions(images, texts, weights, where, [], [6])
    *weights, pt_far, ps_back = fence(*weights, pt_far, ps_back)
    pt_far = pt_far + wide(ps_back)
    back_y = [send(narrow(pt_far[:rows]), "y", DOWN), send(narrow(pt_far[rows:]), "y", UP)]

    ps_low, ps_high = directions(images, texts, weights, where, [], [4, 5])
    *weights, ps_low, ps_high = fence(*weights, ps_low, ps_high)
    ps_near = send(narrow(jnp.concatenate([ps_low, ps_high], axis=0)), "c", SWAP)
    pi_low, pi_high, pt_low, pt_high = directions(images, texts, weights, where, [1, 2], [1, 2])
    *weights, pt_low, pt_high, ps_near, value = fence(*weights, pt_low, pt_high, ps_near, value)
    pt_low = pt_low + wide(ps_near[: 2 * rows])
    pt_high = pt_high + wide(ps_near[2 * rows :])
    value = value + send(value, "c", SWAP)
    (ps_own,) = directions(images, texts, weights, where, [], [3])
    b0, b1, b2, b3, pi_low, pi_high, pt_low, pt_high, ps_own, value, *weights = fence(
        *back_x, *back_y, pi_low, pi_high, pt_low, pt_high, ps_own, value, *weights
    )
    back = [b0, b1, b2, b3]

    pi_low = jnp.concatenate([pi_low[:rows] + wide(back[0]), pi_low[rows:]], axis=0)
    pi_high = jnp.concatenate([pi_high[:rows], pi_high[rows:] + wide(back[1])], axis=0)
    pt_low = jnp.concatenate([pt_low[:rows] + wide(back[2]), pt_low[rows:]], axis=0)
    pt_high = jnp.concatenate([pt_high[:rows], pt_high[rows:] + wide(back[3])], axis=0)
    near = [
        send(narrow(pi_low), "x", DOWN),
        send(narrow(pi_high), "x", UP),
        send(narrow(pt_low), "y", DOWN),
        send(narrow(pt_high), "y", UP),
    ]
    ps_own = send(narrow(ps_own), "c", SWAP)
    pi_own, pt_own = directions(images, texts, weights, where, [0], [0])
    pi_own, pt_own, ps_own, value = fence(pi_own, pt_own, ps_own, value)
    pt_own = pt_own + wide(ps_own)
    for axis, pairs in ((Z, EVEN), (Z, ODD), ("x", EVEN)):
        value = value + send(value, axis, pairs)
    *near, pi_own, pt_own, value = fence(*near, pi_own, pt_own, value)
    pi_own = pi_own + wide(near[0]) + wide(near[1])
    pt_own = pt_own + wide(near[2]) + wide(near[3])

    last = [send(narrow(pi_own[rows:]), Z, EVEN), send(narrow(pt_own[rows:]), Z, ODD)]
    for axis, pairs in (("x", ODD), ("y", EVEN), ("y", ODD)):
        value = value + send(value, axis, pairs)
    objective_results = value[0] * jnp.stack([jnp.float32(1.0), temperature, jnp.float32(1.0)]) / example_number
    scale = temperature / SCALE
    image_gradient = projection(scale * (pi_own[:rows] + wide(last[0])), image32, image_inverse)
    text_grad = projection(scale * (pt_own[:rows] + wide(last[1])), text32, text_inverse)
    return (image_gradient, text_grad, objective_results)


def solution(mesh):
    mesh = Mesh(mesh.devices.reshape(4, 4, 2, 2, 2), AXES)
    return jax.shard_map(
        per_device,
        mesh=mesh,
        in_specs=(P(AXES, None), P(AXES, None), P(), P()),
        out_specs=(P(AXES, None), P(AXES, None), P()),
        check_vma=False,
    )
```

time: 188 us -> 118 us (0.63)
  waiting for transfers between devices: 110 us -> 44.4 us
  matrix products: 19.7 us -> 0 us
  Pallas kernels: 12.4 us -> 24.8 us
  starting transfers between devices: 33.8 us -> 36.1 us
    ppermute x32 -> x33, waiting for transfers between devices: 110 us -> 44.4 us  [send(): return lax.ppermute(value, axis, pairs)]
    dot_general x12 -> x0, matrix products: 19.7 us -> none  [the longest x8 11.4 us: text_part(): lax.dot_general(weights[:, first:first + block], images, (((0,), (0,)), (...]
    pallas_call x1 -> x11, Pallas kernels: 12.4 us -> 24.8 us  [the longest x4 12.6 us: pair_weights(): pl.pallas_call(functools.partial(pair_kernel, len(images), len(texts), ti...]
    ppermute x32 -> x33, starting transfers between devices: 33.8 us -> 36.1 us  [send(): return lax.ppermute(value, axis, pairs)]
  transfers between devices with their start and end apart: 32 -> 33, of which waited for: 18 -> 14; matrix products, arithmetic and copies ran while one was open for 6% -> 4% of each run, Pallas kernels for 0% -> 17%
where the time goes in v2:
time: 118 us
  waiting for transfers between devices  44.4 us (38%)
  starting transfers between devices  36.1 us (31%)
  Pallas kernels  24.8 us (21%)
  other arithmetic  9.68 us (8%)
  between operations  2.43 us (2%)
    ppermute x33, waiting for transfers between devices, send(): return lax.ppermute(value, axis, pairs)  44.4 us
    ppermute x33, starting transfers between devices, send(): return lax.ppermute(value, axis, pairs)  36.1 us
    pallas_call x4, Pallas kernels, pair_weights(): pl.pallas_call(functools.partial(pair_kernel, len(images), len(texts), ti...  12.6 us
    pallas_call x7, Pallas kernels, directions(): pl.pallas_call(functools.partial(direction_kernel, len(images), len(texts...  12.2 us
  transfers between devices with their start and end apart: 33, of which 14 were waited for; matrix products, arithmetic and copies ran while one was open for 4% of the time, Pallas kernels for 17%

profile of v2, /device:TPU:6, one launch (start us, length us, event | category | flops | bytes accessed | tf_op | source)
XLA Modules:
  0.0 118.0 jit_solution(4045543317084638034)
XLA Ops:
  0.6 1.1 fusion.13
  1.7 1.1 fusion.9
  2.9 1.2 %fusion.2 = (bf16[128,1152]{1,0:T(8,128)(2,1)S(1)}, bf16[128,1152]{1,0:T(8,128)(2,1)S(1)}) fusion(bf16[128,1152]{1,0:T(8,128)(2,1)} %param.5, f32[128]{0:T(128)S(1)} %add_rsqrt_fusion, f32[128]{0:T(128)S(1)} %add_rsqrt_fusion.1, bf16[128,1152]{1,0:T(8,128)(2,1)} %param.4), kind=kLoop, calls=%fused_computation.12 | loop fusion | flops 884736 | bytes 1180672 | tf_op jit(solution)/shard_map/convert_element_type | solution.py:159
  4.1 2.0 %collective-permute-start = (bf16[128,1152]{1,0:T(8,128)(2,1)S(1)}, bf16[128,1152]{1,0:T(8,128)(2,1)S(1)}, u32[]{:S(2)}, u32[]{:S(2)}) collective-permute-start(bf16[128,1152]{1,0:T(8,128)(2,1)S(1)} %get-tuple-element.93), channel_id=1, source_target_pairs={{0,2},{2,0},{4,6},{6,4},{1,3},{3,1},{5,7},{7,5},{8,10},{10,8},{12,... | collective-permute-start | bytes 884744 | tf_op jit(solution)/shard_map/ppermute | solution.py:25
  6.1 2.5 %collective-permute-start.1 = (bf16[128,1152]{1,0:T(8,128)(2,1)S(1)}, bf16[128,1152]{1,0:T(8,128)(2,1)S(1)}, u32[]{:S(2)}, u32[]{:S(2)}) collective-permute-start(bf16[128,1152]{1,0:T(8,128)(2,1)S(1)} %get-tuple-element.94), channel_id=1, source_target_pairs={{2,4},{4,2},{6,0},{0,6},{3,5},{5,3},{7,1},{1,7},{10,12},{12,10},{1... | collective-permute-start | bytes 884744 | tf_op jit(solution)/shard_map/ppermute | solution.py:25
  8.7 4.4 %collective-permute-done = bf16[128,1152]{1,0:T(8,128)(2,1)S(1)} collective-permute-done((bf16[128,1152]{1,0:T(8,128)(2,1)S(1)}, bf16[128,1152]{1,0:T(8,128)(2,1)S(1)}, u32[]{:S(2)}, u32[]{:S(2)}) %collective-permute-start) | collective-permute-done | bytes 294944 | tf_op jit(solution)/shard_map/ppermute | solution.py:25
  13.1 2.7 %collective-permute-done.1 = bf16[128,1152]{1,0:T(8,128)(2,1)S(1)} collective-permute-done((bf16[128,1152]{1,0:T(8,128)(2,1)S(1)}, bf16[128,1152]{1,0:T(8,128)(2,1)S(1)}, u32[]{:S(2)}, u32[]{:S(2)}) %collective-permute-start.1) | collective-permute-done | bytes 294944 | tf_op jit(solution)/shard_map/ppermute | solution.py:25
  15.8 0.5 collective-permute-start.2
  16.3 1.5 %collective-permute-start.3 = (bf16[256,1152]{1,0:T(8,128)(2,1)S(1)}, bf16[256,1152]{1,0:T(8,128)(2,1)S(1)}, u32[]{:S(2)}, u32[]{:S(2)}) collective-permute-start(bf16[256,1152]{1,0:T(8,128)(2,1)S(1)} %constant_dynamic-update-slice_fusion.refs_0_), channel_id=1, source_target_pairs={{0,24},{8,0},{16,8},{24,16},{1,25},{9,1},{17,9},{25,17},{2,26},{10... | collective-permute-start | bytes 1769480 | tf_op jit(solution)/shard_map/ppermute | solution.py:25
  17.9 1.6 %collective-permute-start.4 = (bf16[256,1152]{1,0:T(8,128)(2,1)S(1)}, bf16[256,1152]{1,0:T(8,128)(2,1)S(1)}, u32[]{:S(2)}, u32[]{:S(2)}) collective-permute-start(bf16[256,1152]{1,0:T(8,128)(2,1)S(1)} %constant_dynamic-update-slice_fusion.2.refs_3_.refs_4_), channel_id=1, source_target_pairs={{0,32},{32,64},{64,96},{96,0},{1,33},{33,65},{65,97},{97,1},{2,34}... | collective-permute-start | bytes 1769480 | tf_op jit(solution)/shard_map/ppermute | solution.py:25
  19.6 1.7 %collective-permute-start.5 = (bf16[256,1152]{1,0:T(8,128)(2,1)S(1)}, bf16[256,1152]{1,0:T(8,128)(2,1)S(1)}, u32[]{:S(2)}, u32[]{:S(2)}) collective-permute-start(bf16[256,1152]{1,0:T(8,128)(2,1)S(1)} %constant_dynamic-update-slice_fusion.2.refs_3_.refs_4_), channel_id=1, source_target_pairs={{0,96},{32,0},{64,32},{96,64},{1,97},{33,1},{65,33},{97,65},{2,98}... | collective-permute-start | bytes 1769480 | tf_op jit(solution)/shard_map/ppermute | solution.py:25
  21.2 8.5 %collective-permute-done.2.refs_1_ = bf16[256,1152]{1,0:T(8,128)(2,1)S(1)} collective-permute-done((bf16[256,1152]{1,0:T(8,128)(2,1)S(1)}, bf16[256,1152]{1,0:T(8,128)(2,1)S(1)}, u32[]{:S(2)}, u32[]{:S(2)}) %collective-permute-start.2) | collective-permute-done | bytes 589856 | tf_op jit(solution)/shard_map/ppermute | solution.py:25
  29.7 1.4 %collective-permute-done.3.refs_2_ = bf16[256,1152]{1,0:T(8,128)(2,1)S(1)} collective-permute-done((bf16[256,1152]{1,0:T(8,128)(2,1)S(1)}, bf16[256,1152]{1,0:T(8,128)(2,1)S(1)}, u32[]{:S(2)}, u32[]{:S(2)}) %collective-permute-start.3) | collective-permute-done | bytes 589856 | tf_op jit(solution)/shard_map/ppermute | solution.py:25
  31.1 1.4 %collective-permute-done.4.refs_4_.refs_5_ = bf16[256,1152]{1,0:T(8,128)(2,1)S(1)} collective-permute-done((bf16[256,1152]{1,0:T(8,128)(2,1)S(1)}, bf16[256,1152]{1,0:T(8,128)(2,1)S(1)}, u32[]{:S(2)}, u32[]{:S(2)}) %collective-permute-start.4) | collective-permute-done | bytes 589856 | tf_op jit(solution)/shard_map/ppermute | solution.py:25
  34.3 1.8 %collective-permute-start.7 = (bf16[128,1152]{1,0:T(8,128)(2,1)S(1)}, bf16[128,1152]{1,0:T(8,128)(2,1)S(1)}, u32[]{:S(2)}, u32[]{:S(2)}) collective-permute-start(bf16[128,1152]{1,0:T(8,128)(2,1)S(1)} %slice.82), channel_id=1, source_target_pairs={{0,8},{8,16},{16,24},{24,0},{1,9},{9,17},{17,25},{25,1},{2,10},{10... | collective-permute-start | bytes 884744 | tf_op jit(solution)/shard_map/ppermute | solution.py:25
  36.1 0.4 collective-permute-start.8
  36.5 1.6 %collective-permute-start.9 = (bf16[128,1152]{1,0:T(8,128)(2,1)S(1)}, bf16[128,1152]{1,0:T(8,128)(2,1)S(1)}, u32[]{:S(2)}, u32[]{:S(2)}) collective-permute-start(bf16[128,1152]{1,0:T(8,128)(2,1)S(1)} %slice.84), channel_id=1, source_target_pairs={{0,32},{32,64},{64,96},{96,0},{1,33},{33,65},{65,97},{97,1},{2,34}... | collective-permute-start | bytes 884744 | tf_op jit(solution)/shard_map/ppermute | solution.py:25
  38.1 1.7 %collective-permute-start.10 = (bf16[128,1152]{1,0:T(8,128)(2,1)S(1)}, bf16[128,1152]{1,0:T(8,128)(2,1)S(1)}, u32[]{:S(2)}, u32[]{:S(2)}) collective-permute-start(bf16[128,1152]{1,0:T(8,128)(2,1)S(1)} %slice.85), channel_id=1, source_target_pairs={{0,96},{32,0},{64,32},{96,64},{1,97},{33,1},{65,33},{97,65},{2,98}... | collective-permute-start | bytes 884744 | tf_op jit(solution)/shard_map/ppermute | solution.py:25
  39.7 4.3 %shard_map.67 = (bf16[12,256,256]{2,1,0:T(8,128)(2,1)S(1)}, f32[3,8,256]{2,1,0:T(8,128)S(1)}) custom-call(f32[2]{0:T(128)S(1)} %pad_maximum_fusion.6.scalars, bf16[256,1152]{1,0:T(8,128)(2,1)S(1)} %constant_dynamic-update-slice_fusion.refs_0_, bf16[256,1152]{1,0:T(8,128)(2,1)S(1)} %collective-permute-done.2.refs_1_, ...), custom_call_target="tpu_custom_call" | custom-call | flops 1811939328 | bytes 3145728 | tf_op jit(solution)/shard_map/pallas_call | solution.py:88
  44.2 2.6 %shard_map.68 = (bf16[6,256,256]{2,1,0:T(8,128)(2,1)S(1)}, f32[3,8,256]{2,1,0:T(8,128)S(1)}) custom-call(f32[2]{0:T(128)S(1)} %pad_maximum_fusion.6.scalars, bf16[256,1152]{1,0:T(8,128)(2,1)S(1)} %constant_dynamic-update-slice_fusion.refs_0_, bf16[256,1152]{1,0:T(8,128)(2,1)S(1)} %collective-permute-done.2.refs_1_, ...), custom_call_target="tpu_custom_call" | custom-call | flops 905969664 | bytes 1572864 | tf_op jit(solution)/shard_map/pallas_call | solution.py:88
  46.8 0.3 collective-permute-start.12
  47.2 3.7 %shard_map.69 = (bf16[10,256,256]{2,1,0:T(8,128)(2,1)S(1)}, f32[3,8,256]{2,1,0:T(8,128)S(1)}) custom-call(f32[2]{0:T(128)S(1)} %pad_maximum_fusion.6.scalars, bf16[256,1152]{1,0:T(8,128)(2,1)S(1)} %constant_dynamic-update-slice_fusion.refs_0_, bf16[256,1152]{1,0:T(8,128)(2,1)S(1)} %collective-permute-done.2.refs_1_, ...), custom_call_target="tpu_custom_call" | custom-call | flops 1509949440 | bytes 2621440 | tf_op jit(solution)/shard_map/pallas_call | solution.py:88
  50.9 2.0 %shard_map.70 = (bf16[4,256,256]{2,1,0:T(8,128)(2,1)S(1)}, f32[3,8,256]{2,1,0:T(8,128)S(1)}) custom-call(f32[2]{0:T(128)S(1)} %pad_maximum_fusion.6.scalars, bf16[256,1152]{1,0:T(8,128)(2,1)S(1)} %constant_dynamic-update-slice_fusion.refs_0_, bf16[256,1152]{1,0:T(8,128)(2,1)S(1)} %collective-permute-done.2.refs_1_, ...), custom_call_target="tpu_custom_call" | custom-call | flops 603979776 | bytes 1048576 | tf_op jit(solution)/shard_map/pallas_call | solution.py:88
  52.9 0.9 shard_map.71
  53.8 1.5 %shard_map.72 = f32[256,1152]{1,0:T(8,128)S(1)} custom-call(bf16[256,1152]{1,0:T(8,128)(2,1)S(1)} %constant_dynamic-update-slice_fusion.refs_0_, bf16[256,1152]{1,0:T(8,128)(2,1)S(1)} %collective-permute-done.2.refs_1_, bf16[256,1152]{1,0:T(8,128)(2,1)S(1)} %collective-permute-done.3.refs_2_, ...), custom_call_target="tpu_custom_call" | custom-call | flops 1207959552 | bytes 2097152 | tf_op jit(solution)/shard_map/pallas_call | solution.py:131
  55.5 0.6 collective-permute-start.15
  56.2 0.9 collective-permute-start.13
  57.0 2.4 %collective-permute-start.14 = (f16[128,1152]{1,0:T(8,128)(2,1)S(1)}, f16[128,1152]{1,0:T(8,128)(2,1)S(1)}, u32[]{:S(2)}, u32[]{:S(2)}) collective-permute-start(f16[128,1152]{1,0:T(8,128)(2,1)S(1)} %get-tuple-element.197), channel_id=1, source_target_pairs={{0,8},{8,16},{16,24},{24,0},{1,9},{9,17},{17,25},{25,1},{2,10},{10... | collective-permute-start | bytes 884744 | tf_op jit(solution)/shard_map/ppermute | solution.py:25
  59.5 0.9 shard_map.73
  60.5 1.6 %shard_map.74 = (f32[256,1152]{1,0:T(8,128)S(1)}, f32[256,1152]{1,0:T(8,128)S(1)}) custom-call(bf16[256,1152]{1,0:T(8,128)(2,1)S(1)} %constant_dynamic-update-slice_fusion.refs_0_, bf16[256,1152]{1,0:T(8,128)(2,1)S(1)} %collective-permute-done.2.refs_1_, bf16[256,1152]{1,0:T(8,128)(2,1)S(1)} %collective-permute-done.3.refs_2_, ...), custom_call_target="tpu_custom_call" | custom-call | flops 1207959552 | bytes 2097152 | tf_op jit(solution)/shard_map/pallas_call | solution.py:131
  62.2 0.3 pad_maximum_fusion.1
  62.5 0.2 add_convert_fusion
  62.8 3.0 %collective-permute-start.16 = (f16[128,1152]{1,0:T(8,128)(2,1)S(1)}, f16[128,1152]{1,0:T(8,128)(2,1)S(1)}, u32[]{:S(2)}, u32[]{:S(2)}) collective-permute-start(f16[128,1152]{1,0:T(8,128)(2,1)S(1)} %get-tuple-element.196), channel_id=1, source_target_pairs={{0,96},{32,0},{64,32},{96,64},{1,97},{33,1},{65,33},{97,65},{2,98}... | collective-permute-start | bytes 884744 | tf_op jit(solution)/shard_map/ppermute | solution.py:25
  65.8 4.3 %shard_map.75 = (f32[256,1152]{1,0:T(8,128)S(1)}, f32[256,1152]{1,0:T(8,128)S(1)}, f32[256,1152]{1,0:T(8,128)S(1)}, f32[256,1152]{1,0:T(8,128)S(1)}) custom-call(bf16[256,1152]{1,0:T(8,128)(2,1)S(1)} %constant_dynamic-update-slice_fusion.refs_0_, bf16[256,1152]{1,0:T(8,128)(2,1)S(1)} %collective-permute-done.2.refs_1_, ...), custom_call_target="tpu_custom_call" | custom-call | flops 3623878656 | bytes 6291456 | tf_op jit(solution)/shard_map/pallas_call | solution.py:131
  70.1 0.3 collective-permute-start.19
  70.4 0.2 convert_add_fusion.3
  70.6 0.9 shard_map.76
  71.6 1.2 collective-permute-done.16
  72.7 3.4 %collective-permute-done.17 = f16[128,1152]{1,0:T(8,128)(2,1)S(1)} collective-permute-done((f16[128,1152]{1,0:T(8,128)(2,1)S(1)}, f16[128,1152]{1,0:T(8,128)(2,1)S(1)}, u32[]{:S(2)}, u32[]{:S(2)}) %collective-permute-start.17) | collective-permute-done | bytes 294944 | tf_op jit(solution)/shard_map/ppermute | solution.py:25
  76.8 3.3 %collective-permute-start.21 = (f16[256,1152]{1,0:T(8,128)(2,1)S(1)}, f16[256,1152]{1,0:T(8,128)(2,1)S(1)}, u32[]{:S(2)}, u32[]{:S(2)}) collective-permute-start(f16[256,1152]{1,0:T(8,128)(2,1)S(1)} %pad_maximum_fusion.3), channel_id=1, source_target_pairs={{0,8},{8,16},{16,24},{24,0},{1,9},{9,17},{17,25},{25,1},{2,10},{10... | collective-permute-start | bytes 1769480 | tf_op jit(solution)/shard_map/ppermute | solution.py:25
  80.3 0.4 collective-permute-start.22
  81.1 1.8 %collective-permute-start.23 = (f16[256,1152]{1,0:T(8,128)(2,1)S(1)}, f16[256,1152]{1,0:T(8,128)(2,1)S(1)}, u32[]{:S(2)}, u32[]{:S(2)}) collective-permute-start(f16[256,1152]{1,0:T(8,128)(2,1)S(1)} %pad_maximum_fusion.5), channel_id=1, source_target_pairs={{0,32},{32,64},{64,96},{96,0},{1,33},{33,65},{65,97},{97,1},{2,34}... | collective-permute-start | bytes 1769480 | tf_op jit(solution)/shard_map/ppermute | solution.py:25
  82.9 2.2 %shard_map.77 = (f32[256,1152]{1,0:T(8,128)S(1)}, f32[256,1152]{1,0:T(8,128)S(1)}) custom-call(bf16[256,1152]{1,0:T(8,128)(2,1)S(1)} %constant_dynamic-update-slice_fusion.refs_0_, bf16[256,1152]{1,0:T(8,128)(2,1)S(1)} %collective-permute-done.2.refs_1_, bf16[256,1152]{1,0:T(8,128)(2,1)S(1)} %collective-permute-done.3.refs_2_, ...), custom_call_target="tpu_custom_call" | custom-call | flops 1811939328 | bytes 3145728 | tf_op jit(solution)/shard_map/pallas_call | solution.py:131
  85.2 1.0 collective-permute-start.25
  86.2 0.2 convert_add_fusion.2
  86.3 2.5 %collective-permute-done.25 = f32[1,3]{1,0:T(1,128)S(1)} collective-permute-done((f32[1,3]{1,0:T(1,128)S(1)}, f32[1,3]{1,0:T(1,128)S(1)}, u32[]{:S(2)}, u32[]{:S(2)}) %collective-permute-start.25) | collective-permute-done | bytes 44 | tf_op jit(solution)/shard_map/ppermute | solution.py:25
  88.8 2.5 %collective-permute-start.26 = (f32[1,3]{1,0:T(1,128)S(1)}, f32[1,3]{1,0:T(1,128)S(1)}, u32[]{:S(2)}, u32[]{:S(2)}) collective-permute-start(f32[1,3]{1,0:T(1,128)S(1)} %add.102), channel_id=1, source_target_pairs={{2,4},{4,2},{6,0},{0,6},{3,5},{5,3},{7,1},{1,7},{10,12},{12,10},{1... | collective-permute-start | bytes 44 | tf_op jit(solution)/shard_map/ppermute | solution.py:25
  91.3 2.2 %collective-permute-done.26 = f32[1,3]{1,0:T(1,128)S(1)} collective-permute-done((f32[1,3]{1,0:T(1,128)S(1)}, f32[1,3]{1,0:T(1,128)S(1)}, u32[]{:S(2)}, u32[]{:S(2)}) %collective-permute-start.26) | collective-permute-done | bytes 44 | tf_op jit(solution)/shard_map/ppermute | solution.py:25
  93.5 3.5 %collective-permute-done.27 = f32[1,3]{1,0:T(1,128)S(1)} collective-permute-done((f32[1,3]{1,0:T(1,128)S(1)}, f32[1,3]{1,0:T(1,128)S(1)}, u32[]{:S(2)}, u32[]{:S(2)}) %collective-permute-start.27) | collective-permute-done | bytes 44 | tf_op jit(solution)/shard_map/ppermute | solution.py:25
  97.1 1.0 collective-permute-done.23
  98.1 0.2 convert_add_fusion.1
  98.4 1.0 collective-permute-start.28
  99.4 0.2 convert_add_fusion
  99.7 2.1 %collective-permute-start.29 = (f16[128,1152]{1,0:T(8,128)(2,1)S(1)}, f16[128,1152]{1,0:T(8,128)(2,1)S(1)}, u32[]{:S(2)}, u32[]{:S(2)}) collective-permute-start(f16[128,1152]{1,0:T(8,128)(2,1)S(1)} %slice_convert_fusion), channel_id=1, source_target_pairs={{2,4},{4,2},{6,0},{0,6},{3,5},{5,3},{7,1},{1,7},{10,12},{12,10},{1... | collective-permute-start | bytes 884744 | tf_op jit(solution)/shard_map/ppermute | solution.py:25
  101.8 0.4 collective-permute-start.30
  102.2 4.4 %collective-permute-done.30 = f32[1,3]{1,0:T(1,128)S(1)} collective-permute-done((f32[1,3]{1,0:T(1,128)S(1)}, f32[1,3]{1,0:T(1,128)S(1)}, u32[]{:S(2)}, u32[]{:S(2)}) %collective-permute-start.30) | collective-permute-done | bytes 44 | tf_op jit(solution)/shard_map/ppermute | solution.py:25
  106.5 0.5 collective-permute-start.31
  107.1 3.0 %collective-permute-done.31 = f32[1,3]{1,0:T(1,128)S(1)} collective-permute-done((f32[1,3]{1,0:T(1,128)S(1)}, f32[1,3]{1,0:T(1,128)S(1)}, u32[]{:S(2)}, u32[]{:S(2)}) %collective-permute-start.31) | collective-permute-done | bytes 44 | tf_op jit(solution)/shard_map/ppermute | solution.py:25
  110.2 4.7 %collective-permute-done.32 = f32[1,3]{1,0:T(1,128)S(1)} collective-permute-done((f32[1,3]{1,0:T(1,128)S(1)}, f32[1,3]{1,0:T(1,128)S(1)}, u32[]{:S(2)}, u32[]{:S(2)}) %collective-permute-start.32) | collective-permute-done | bytes 44 | tf_op jit(solution)/shard_map/ppermute | solution.py:25
  114.8 0.6 fusion.16
  115.4 0.2 fusion.6
  115.7 1.0 fusion.8
  116.7 0.3 fusion.10
  117.0 1.1 fusion.12
  (72 shorter events, 2.9 us)
Async XLA Ops:
  4.1 9.0 %collective-permute-start = (bf16[128,1152]{1,0:T(8,128)(2,1)S(1)}, bf16[128,1152]{1,0:T(8,128)(2,1)S(1)}, u32[]{:S(2)}, u32[]{:S(2)}) collective-permute-start(bf16[128,1152]{1,0:T(8,128)(2,1)S(1)} %get-tuple-element.93), channel_id=1, source_target_pairs={{0,2},{2,0},{4,6},{6,4},{1,3},{3,1},{5,7},{7,5},{8,10},{10,8},{12,... | collective-permute-start | bytes 884744 | tf_op jit(solution)/shard_map/ppermute | solution.py:25
  6.1 9.7 %collective-permute-start.1 = (bf16[128,1152]{1,0:T(8,128)(2,1)S(1)}, bf16[128,1152]{1,0:T(8,128)(2,1)S(1)}, u32[]{:S(2)}, u32[]{:S(2)}) collective-permute-start(bf16[128,1152]{1,0:T(8,128)(2,1)S(1)} %get-tuple-element.94), channel_id=1, source_target_pairs={{2,4},{4,2},{6,0},{0,6},{3,5},{5,3},{7,1},{1,7},{10,12},{12,10},{1... | collective-permute-start | bytes 884744 | tf_op jit(solution)/shard_map/ppermute | solution.py:25
  15.8 13.9 %collective-permute-start.2 = (bf16[256,1152]{1,0:T(8,128)(2,1)S(1)}, bf16[256,1152]{1,0:T(8,128)(2,1)S(1)}, u32[]{:S(2)}, u32[]{:S(2)}) collective-permute-start(bf16[256,1152]{1,0:T(8,128)(2,1)S(1)} %constant_dynamic-update-slice_fusion.refs_0_), channel_id=1, source_target_pairs={{0,8},{8,16},{16,24},{24,0},{1,9},{9,17},{17,25},{25,1},{2,10},{10... | collective-permute-start | bytes 1769480 | tf_op jit(solution)/shard_map/ppermute | solution.py:25
  16.3 14.8 %collective-permute-start.3 = (bf16[256,1152]{1,0:T(8,128)(2,1)S(1)}, bf16[256,1152]{1,0:T(8,128)(2,1)S(1)}, u32[]{:S(2)}, u32[]{:S(2)}) collective-permute-start(bf16[256,1152]{1,0:T(8,128)(2,1)S(1)} %constant_dynamic-update-slice_fusion.refs_0_), channel_id=1, source_target_pairs={{0,24},{8,0},{16,8},{24,16},{1,25},{9,1},{17,9},{25,17},{2,26},{10... | collective-permute-start | bytes 1769480 | tf_op jit(solution)/shard_map/ppermute | solution.py:25
  17.9 14.7 %collective-permute-start.4 = (bf16[256,1152]{1,0:T(8,128)(2,1)S(1)}, bf16[256,1152]{1,0:T(8,128)(2,1)S(1)}, u32[]{:S(2)}, u32[]{:S(2)}) collective-permute-start(bf16[256,1152]{1,0:T(8,128)(2,1)S(1)} %constant_dynamic-update-slice_fusion.2.refs_3_.refs_4_), channel_id=1, source_target_pairs={{0,32},{32,64},{64,96},{96,0},{1,33},{33,65},{65,97},{97,1},{2,34}... | collective-permute-start | bytes 1769480 | tf_op jit(solution)/shard_map/ppermute | solution.py:25
  19.6 13.0 %collective-permute-start.5 = (bf16[256,1152]{1,0:T(8,128)(2,1)S(1)}, bf16[256,1152]{1,0:T(8,128)(2,1)S(1)}, u32[]{:S(2)}, u32[]{:S(2)}) collective-permute-start(bf16[256,1152]{1,0:T(8,128)(2,1)S(1)} %constant_dynamic-update-slice_fusion.2.refs_3_.refs_4_), channel_id=1, source_target_pairs={{0,96},{32,0},{64,32},{96,64},{1,97},{33,1},{65,33},{97,65},{2,98}... | collective-permute-start | bytes 1769480 | tf_op jit(solution)/shard_map/ppermute | solution.py:25
  21.2 11.4 %collective-permute-start.6 = (bf16[256,1152]{1,0:T(8,128)(2,1)S(1)}, bf16[256,1152]{1,0:T(8,128)(2,1)S(1)}, u32[]{:S(2)}, u32[]{:S(2)}) collective-permute-start(bf16[256,1152]{1,0:T(8,128)(2,1)S(1)} %constant_dynamic-update-slice_fusion.2.refs_3_.refs_4_), channel_id=1, source_target_pairs={{0,1},{1,0},{2,3},{3,2},{4,5},{5,4},{6,7},{7,6},{8,9},{9,8},{10,11... | collective-permute-start | bytes 1769480 | tf_op jit(solution)/shard_map/ppermute | solution.py:25
  32.7 11.3 %collective-permute-start.11 = (bf16[512,1152]{1,0:T(8,128)(2,1)S(1)}, bf16[512,1152]{1,0:T(8,128)(2,1)S(1)}, u32[]{:S(2)}, u32[]{:S(2)}) collective-permute-start(bf16[512,1152]{1,0:T(8,128)(2,1)S(1)} %pad_maximum_fusion), channel_id=1, source_target_pairs={{0,1},{1,0},{2,3},{3,2},{4,5},{5,4},{6,7},{7,6},{8,9},{9,8},{10,11... | collective-permute-start | bytes 3538952 | tf_op jit(solution)/shard_map/ppermute | solution.py:25
  34.3 12.4 %collective-permute-start.7 = (bf16[128,1152]{1,0:T(8,128)(2,1)S(1)}, bf16[128,1152]{1,0:T(8,128)(2,1)S(1)}, u32[]{:S(2)}, u32[]{:S(2)}) collective-permute-start(bf16[128,1152]{1,0:T(8,128)(2,1)S(1)} %slice.82), channel_id=1, source_target_pairs={{0,8},{8,16},{16,24},{24,0},{1,9},{9,17},{17,25},{25,1},{2,10},{10... | collective-permute-start | bytes 884744 | tf_op jit(solution)/shard_map/ppermute | solution.py:25
  36.1 10.7 %collective-permute-start.8 = (bf16[128,1152]{1,0:T(8,128)(2,1)S(1)}, bf16[128,1152]{1,0:T(8,128)(2,1)S(1)}, u32[]{:S(2)}, u32[]{:S(2)}) collective-permute-start(bf16[128,1152]{1,0:T(8,128)(2,1)S(1)} %slice.83), channel_id=1, source_target_pairs={{0,24},{8,0},{16,8},{24,16},{1,25},{9,1},{17,9},{25,17},{2,26},{10... | collective-permute-start | bytes 884744 | tf_op jit(solution)/shard_map/ppermute | solution.py:25
  36.5 10.3 %collective-permute-start.9 = (bf16[128,1152]{1,0:T(8,128)(2,1)S(1)}, bf16[128,1152]{1,0:T(8,128)(2,1)S(1)}, u32[]{:S(2)}, u32[]{:S(2)}) collective-permute-start(bf16[128,1152]{1,0:T(8,128)(2,1)S(1)} %slice.84), channel_id=1, source_target_pairs={{0,32},{32,64},{64,96},{96,0},{1,33},{33,65},{65,97},{97,1},{2,34}... | collective-permute-start | bytes 884744 | tf_op jit(solution)/shard_map/ppermute | solution.py:25
  38.1 8.7 %collective-permute-start.10 = (bf16[128,1152]{1,0:T(8,128)(2,1)S(1)}, bf16[128,1152]{1,0:T(8,128)(2,1)S(1)}, u32[]{:S(2)}, u32[]{:S(2)}) collective-permute-start(bf16[128,1152]{1,0:T(8,128)(2,1)S(1)} %slice.85), channel_id=1, source_target_pairs={{0,96},{32,0},{64,32},{96,64},{1,97},{33,1},{65,33},{97,65},{2,98}... | collective-permute-start | bytes 884744 | tf_op jit(solution)/shard_map/ppermute | solution.py:25
  46.8 4.1 %collective-permute-start.12 = (bf16[256,1152]{1,0:T(8,128)(2,1)S(1)}, bf16[256,1152]{1,0:T(8,128)(2,1)S(1)}, u32[]{:S(2)}, u32[]{:S(2)}) collective-permute-start(bf16[256,1152]{1,0:T(8,128)(2,1)S(1)} %constant_dynamic-update-slice_fusion.6.refs_10_), channel_id=1, source_target_pairs={{0,1},{1,0},{2,3},{3,2},{4,5},{5,4},{6,7},{7,6},{8,9},{9,8},{10,11... | collective-permute-start | bytes 1769480 | tf_op jit(solution)/shard_map/ppermute | solution.py:25
  55.5 5.0 %collective-permute-start.15 = (f16[256,1152]{1,0:T(8,128)(2,1)S(1)}, f16[256,1152]{1,0:T(8,128)(2,1)S(1)}, u32[]{:S(2)}, u32[]{:S(2)}) collective-permute-start(f16[256,1152]{1,0:T(8,128)(2,1)S(1)} %convert_element_type.75), channel_id=1, source_target_pairs={{0,1},{1,0},{2,3},{3,2},{4,5},{5,4},{6,7},{7,6},{8,9},{9,8},{10,11... | collective-permute-start | bytes 1769480 | tf_op jit(solution)/shard_map/ppermute | solution.py:25
  56.2 15.4 %collective-permute-start.13 = (f16[128,1152]{1,0:T(8,128)(2,1)S(1)}, f16[128,1152]{1,0:T(8,128)(2,1)S(1)}, u32[]{:S(2)}, u32[]{:S(2)}) collective-permute-start(f16[128,1152]{1,0:T(8,128)(2,1)S(1)} %get-tuple-element.198), channel_id=1, source_target_pairs={{0,24},{8,0},{16,8},{24,16},{1,25},{9,1},{17,9},{25,17},{2,26},{10... | collective-permute-start | bytes 884744 | tf_op jit(solution)/shard_map/ppermute | solution.py:25
  57.0 14.5 %collective-permute-start.14 = (f16[128,1152]{1,0:T(8,128)(2,1)S(1)}, f16[128,1152]{1,0:T(8,128)(2,1)S(1)}, u32[]{:S(2)}, u32[]{:S(2)}) collective-permute-start(f16[128,1152]{1,0:T(8,128)(2,1)S(1)} %get-tuple-element.197), channel_id=1, source_target_pairs={{0,8},{8,16},{16,24},{24,0},{1,9},{9,17},{17,25},{25,1},{2,10},{10... | collective-permute-start | bytes 884744 | tf_op jit(solution)/shard_map/ppermute | solution.py:25
  62.4 7.7 %collective-permute-start.18 = (f16[512,1152]{1,0:T(8,128)(2,1)S(1)}, f16[512,1152]{1,0:T(8,128)(2,1)S(1)}, u32[]{:S(2)}, u32[]{:S(2)}) collective-permute-start(f16[512,1152]{1,0:T(8,128)(2,1)S(1)} %pad_maximum_fusion.1), channel_id=1, source_target_pairs={{0,1},{1,0},{2,3},{3,2},{4,5},{5,4},{6,7},{7,6},{8,9},{9,8},{10,11... | collective-permute-start | bytes 3538952 | tf_op jit(solution)/shard_map/ppermute | solution.py:25
  62.8 9.9 %collective-permute-start.16 = (f16[128,1152]{1,0:T(8,128)(2,1)S(1)}, f16[128,1152]{1,0:T(8,128)(2,1)S(1)}, u32[]{:S(2)}, u32[]{:S(2)}) collective-permute-start(f16[128,1152]{1,0:T(8,128)(2,1)S(1)} %get-tuple-element.196), channel_id=1, source_target_pairs={{0,96},{32,0},{64,32},{96,64},{1,97},{33,1},{65,33},{97,65},{2,98}... | collective-permute-start | bytes 884744 | tf_op jit(solution)/shard_map/ppermute | solution.py:25
  65.8 10.3 %collective-permute-start.17 = (f16[128,1152]{1,0:T(8,128)(2,1)S(1)}, f16[128,1152]{1,0:T(8,128)(2,1)S(1)}, u32[]{:S(2)}, u32[]{:S(2)}) collective-permute-start(f16[128,1152]{1,0:T(8,128)(2,1)S(1)} %get-tuple-element.195), channel_id=1, source_target_pairs={{0,32},{32,64},{64,96},{96,0},{1,33},{33,65},{65,97},{97,1},{2,34}... | collective-permute-start | bytes 884744 | tf_op jit(solution)/shard_map/ppermute | solution.py:25
  70.1 1.4 %collective-permute-start.19 = (f32[1,3]{1,0:T(1,128)S(1)}, f32[1,3]{1,0:T(1,128)S(1)}, u32[]{:S(2)}, u32[]{:S(2)}) collective-permute-start(f32[1,3]{1,0:T(1,128)S(1)} %bitcast.4), channel_id=1, source_target_pairs={{0,1},{1,0},{2,3},{3,2},{4,5},{5,4},{6,7},{7,6},{8,9},{9,8},{10,11... | collective-permute-start | bytes 44 | tf_op jit(solution)/shard_map/ppermute | solution.py:25
  76.4 20.7 %collective-permute-start.20 = (f16[256,1152]{1,0:T(8,128)(2,1)S(1)}, f16[256,1152]{1,0:T(8,128)(2,1)S(1)}, u32[]{:S(2)}, u32[]{:S(2)}) collective-permute-start(f16[256,1152]{1,0:T(8,128)(2,1)S(1)} %pad_maximum_fusion.2), channel_id=1, source_target_pairs={{0,24},{8,0},{16,8},{24,16},{1,25},{9,1},{17,9},{25,17},{2,26},{10... | collective-permute-start | bytes 1769480 | tf_op jit(solution)/shard_map/ppermute | solution.py:25
  76.8 20.3 %collective-permute-start.21 = (f16[256,1152]{1,0:T(8,128)(2,1)S(1)}, f16[256,1152]{1,0:T(8,128)(2,1)S(1)}, u32[]{:S(2)}, u32[]{:S(2)}) collective-permute-start(f16[256,1152]{1,0:T(8,128)(2,1)S(1)} %pad_maximum_fusion.3), channel_id=1, source_target_pairs={{0,8},{8,16},{16,24},{24,0},{1,9},{9,17},{17,25},{25,1},{2,10},{10... | collective-permute-start | bytes 1769480 | tf_op jit(solution)/shard_map/ppermute | solution.py:25
  80.3 16.8 %collective-permute-start.22 = (f16[256,1152]{1,0:T(8,128)(2,1)S(1)}, f16[256,1152]{1,0:T(8,128)(2,1)S(1)}, u32[]{:S(2)}, u32[]{:S(2)}) collective-permute-start(f16[256,1152]{1,0:T(8,128)(2,1)S(1)} %pad_maximum_fusion.4), channel_id=1, source_target_pairs={{0,96},{32,0},{64,32},{96,64},{1,97},{33,1},{65,33},{97,65},{2,98}... | collective-permute-start | bytes 1769480 | tf_op jit(solution)/shard_map/ppermute | solution.py:25
  80.7 4.4 %collective-permute-start.24 = (f16[256,1152]{1,0:T(8,128)(2,1)S(1)}, f16[256,1152]{1,0:T(8,128)(2,1)S(1)}, u32[]{:S(2)}, u32[]{:S(2)}) collective-permute-start(f16[256,1152]{1,0:T(8,128)(2,1)S(1)} %convert_element_type.83), channel_id=1, source_target_pairs={{0,1},{1,0},{2,3},{3,2},{4,5},{5,4},{6,7},{7,6},{8,9},{9,8},{10,11... | collective-permute-start | bytes 1769480 | tf_op jit(solution)/shard_map/ppermute | solution.py:25
  81.1 17.0 %collective-permute-start.23 = (f16[256,1152]{1,0:T(8,128)(2,1)S(1)}, f16[256,1152]{1,0:T(8,128)(2,1)S(1)}, u32[]{:S(2)}, u32[]{:S(2)}) collective-permute-start(f16[256,1152]{1,0:T(8,128)(2,1)S(1)} %pad_maximum_fusion.5), channel_id=1, source_target_pairs={{0,32},{32,64},{64,96},{96,0},{1,33},{33,65},{65,97},{97,1},{2,34}... | collective-permute-start | bytes 1769480 | tf_op jit(solution)/shard_map/ppermute | solution.py:25
  85.2 3.6 %collective-permute-start.25 = (f32[1,3]{1,0:T(1,128)S(1)}, f32[1,3]{1,0:T(1,128)S(1)}, u32[]{:S(2)}, u32[]{:S(2)}) collective-permute-start(f32[1,3]{1,0:T(1,128)S(1)} %add.96), channel_id=1, source_target_pairs={{0,2},{2,0},{4,6},{6,4},{1,3},{3,1},{5,7},{7,5},{8,10},{10,8},{12,... | collective-permute-start | bytes 44 | tf_op jit(solution)/shard_map/ppermute | solution.py:25
  88.8 4.8 %collective-permute-start.26 = (f32[1,3]{1,0:T(1,128)S(1)}, f32[1,3]{1,0:T(1,128)S(1)}, u32[]{:S(2)}, u32[]{:S(2)}) collective-permute-start(f32[1,3]{1,0:T(1,128)S(1)} %add.102), channel_id=1, source_target_pairs={{2,4},{4,2},{6,0},{0,6},{3,5},{5,3},{7,1},{1,7},{10,12},{12,10},{1... | collective-permute-start | bytes 44 | tf_op jit(solution)/shard_map/ppermute | solution.py:25
  93.5 3.5 %collective-permute-start.27 = (f32[1,3]{1,0:T(1,128)S(1)}, f32[1,3]{1,0:T(1,128)S(1)}, u32[]{:S(2)}, u32[]{:S(2)}) collective-permute-start(f32[1,3]{1,0:T(1,128)S(1)} %add.103), channel_id=1, source_target_pairs={{0,8},{8,0},{16,24},{24,16},{1,9},{9,1},{17,25},{25,17},{2,10},{10... | collective-permute-start | bytes 44 | tf_op jit(solution)/shard_map/ppermute | solution.py:25
  98.4 17.0 %copy-start = (bf16[128,1152]{1,0:T(8,128)(2,1)S(1)}, bf16[128,1152]{1,0:T(8,128)(2,1)}, u32[]{:S(2)}) copy-start(bf16[128,1152]{1,0:T(8,128)(2,1)} %param.4) | copy-start | bytes 884740
  98.4 17.0 %collective-permute-start.28 = (f16[128,1152]{1,0:T(8,128)(2,1)S(1)}, f16[128,1152]{1,0:T(8,128)(2,1)S(1)}, u32[]{:S(2)}, u32[]{:S(2)}) collective-permute-start(f16[128,1152]{1,0:T(8,128)(2,1)S(1)} %slice_convert_fusion.1), channel_id=1, source_target_pairs={{0,2},{2,0},{4,6},{6,4},{1,3},{3,1},{5,7},{7,5},{8,10},{10,8},{12,... | collective-permute-start | bytes 884744 | tf_op jit(solution)/shard_map/ppermute | solution.py:25
  99.7 17.0 %collective-permute-start.29 = (f16[128,1152]{1,0:T(8,128)(2,1)S(1)}, f16[128,1152]{1,0:T(8,128)(2,1)S(1)}, u32[]{:S(2)}, u32[]{:S(2)}) collective-permute-start(f16[128,1152]{1,0:T(8,128)(2,1)S(1)} %slice_convert_fusion), channel_id=1, source_target_pairs={{2,4},{4,2},{6,0},{0,6},{3,5},{5,3},{7,1},{1,7},{10,12},{12,10},{1... | collective-permute-start | bytes 884744 | tf_op jit(solution)/shard_map/ppermute | solution.py:25
  101.8 4.8 %collective-permute-start.30 = (f32[1,3]{1,0:T(1,128)S(1)}, f32[1,3]{1,0:T(1,128)S(1)}, u32[]{:S(2)}, u32[]{:S(2)}) collective-permute-start(f32[1,3]{1,0:T(1,128)S(1)} %add.104), channel_id=1, source_target_pairs={{8,16},{16,8},{24,0},{0,24},{9,17},{17,9},{25,1},{1,25},{10,18},{1... | collective-permute-start | bytes 44 | tf_op jit(solution)/shard_map/ppermute | solution.py:25
  106.5 3.5 %collective-permute-start.31 = (f32[1,3]{1,0:T(1,128)S(1)}, f32[1,3]{1,0:T(1,128)S(1)}, u32[]{:S(2)}, u32[]{:S(2)}) collective-permute-start(f32[1,3]{1,0:T(1,128)S(1)} %add.111), channel_id=1, source_target_pairs={{0,32},{32,0},{64,96},{96,64},{1,33},{33,1},{65,97},{97,65},{2,34}... | collective-permute-start | bytes 44 | tf_op jit(solution)/shard_map/ppermute | solution.py:25
  110.1 4.8 %collective-permute-start.32 = (f32[1,3]{1,0:T(1,128)S(1)}, f32[1,3]{1,0:T(1,128)S(1)}, u32[]{:S(2)}, u32[]{:S(2)}) collective-permute-start(f32[1,3]{1,0:T(1,128)S(1)} %add.112), channel_id=1, source_target_pairs={{32,64},{64,32},{96,0},{0,96},{33,65},{65,33},{97,1},{1,97},{34,66... | collective-permute-start | bytes 44 | tf_op jit(solution)/shard_map/ppermute | solution.py:25
  115.7 1.1 copy-start.1

commit v3 on v2

--- a/solution.py
+++ b/solution.py
@@ -56,10 +56,8 @@
         )
         logits = scores * factor + offset
         small = jnp.exp2(-jnp.abs(logits))
-        denominator = 1.0 + small
-        guess = pl.reciprocal(denominator, approx=True)
-        inverse = guess * (2.0 - denominator * guess)
-        gradient = jnp.where(logits >= 0.0, inverse, small * inverse)
+        inverse = pltpu.reciprocal(1.0 + small, approx=True)
+        gradient = jnp.where(logits >= 0.0, 1.0, small) * inverse
         signed = logits
         if t == diagonal:
             row = lax.broadcasted_iota(jnp.int32, (TILE, TILE), 0)
@@ -94,10 +92,36 @@
             jax.ShapeDtypeStruct((3, 8, TILE), jnp.float32),
         ],
         compiler_params=pltpu.CompilerParams(vmem_limit_bytes=24 * 1024 * 1024),
-        cost_estimate=pl.CostEstimate(
-            flops=2 * n * TILE * TILE * 1152, bytes_accessed=n << 18, transcendentals=2 * n * TILE * TILE
-        ),
+        cost_estimate=pl.CostEstimate(flops=1, bytes_accessed=1, transcendentals=0),
     )(scalars, *images, *texts)
+
+
+def stacked_kernel(n_images, n_weights, text_out, where, *refs):
+    images, weights = refs[:n_images], refs[n_images : n_images + n_weights]
+    before, out = refs[n_images + n_weights : -1], refs[-1]
+    for o, j in enumerate(text_out):
+        rows = pl.ds(o * TILE, TILE)
+        total = before[0][rows, :] if before else None
+        for i in range(n_images):
+            a, t = where[i, j]
+            term = SCALE * lax.dot_general(
+                weights[a][t], images[i][...], (((0,), (0,)), ((), ())), preferred_element_type=jnp.float32
+            )
+            total = term if total is None else total + term
+        out[rows, :] = total
+
+
+def stacked(images, weights, where, text_out, *before):
+    vmem = pl.BlockSpec(memory_space=pltpu.VMEM)
+    n_out = len(text_out)
+    return pl.pallas_call(
+        functools.partial(stacked_kernel, len(images), len(weights), tuple(text_out), where),
+        in_specs=[vmem] * (len(images) + len(weights) + len(before)),
+        out_specs=vmem,
+        out_shape=jax.ShapeDtypeStruct((n_out * TILE, 1152), jnp.float32),
+        compiler_params=pltpu.CompilerParams(vmem_limit_bytes=24 * 1024 * 1024),
+        cost_estimate=pl.CostEstimate(flops=1, bytes_accessed=1, transcendentals=0),
+    )(*images, *weights, *before)
 
 
 def direction_kernel(n_images, n_texts, n_weights, image_out, text_out, where, *refs):
@@ -136,9 +160,7 @@
         out_specs=[vmem] * n_out,
         out_shape=[jax.ShapeDtypeStruct((TILE, 1152), jnp.float32)] * n_out,
         compiler_params=pltpu.CompilerParams(vmem_limit_bytes=24 * 1024 * 1024),
-        cost_estimate=pl.CostEstimate(
-            flops=2 * n_dots * TILE * TILE * 1152, bytes_accessed=n_dots << 18, transcendentals=0
-        ),
+        cost_estimate=pl.CostEstimate(flops=1, bytes_accessed=1, transcendentals=0),
     )(*images, *texts, *weights)
 
 
@@ -153,25 +175,27 @@
 def per_device(picture_embedding, caption_embedding, logarithmic_scale_factor, offset_shift):
     rows = picture_embedding.shape[0]
     example_number = rows * 128
-    image32, image_inverse = normalize(picture_embedding)
-    text32, text_inverse = normalize(caption_embedding)
-    image = image32.astype(jnp.bfloat16)
-    text = text32.astype(jnp.bfloat16)
+    (both,) = fence(jnp.concatenate([picture_embedding, caption_embedding], axis=0))
+    unit32, inverse = normalize(both)
+    unit = unit32.astype(jnp.bfloat16)
+    image, text = unit[:rows], unit[rows:]
     temperature = jnp.exp(logarithmic_scale_factor[0])
     scalars = jnp.stack([temperature, offset_shift[0]])
 
-    image, text = fence(image, text)
     image_z, text_z = fence(send(image, Z, EVEN), send(text, Z, ODD))
     i_own = jnp.concatenate([image, image_z], axis=0)
     t_own = jnp.concatenate([text, text_z], axis=0)
 
-    i_low, i_high, t_low, t_high, s_own = fence(
+    scalars, i_low, i_high, t_low, t_high, text_s, text_zs = fence(
+        scalars,
         send(i_own, "x", UP),
         send(i_own, "x", DOWN),
         send(t_own, "y", UP),
         send(t_own, "y", DOWN),
-        send(t_own, "c", SWAP),
+        send(text, "c", SWAP),
+        send(text_z, "c", SWAP),
     )
+    s_own = jnp.concatenate([text_s, text_zs], axis=0)
 
     far = [
         send(i_low[:rows], "x", UP),
@@ -188,7 +212,10 @@
     s_low, s_high = s_near[: 2 * rows], s_near[2 * rows :]
     tiles_b = [(i, j) for j in range(2) for i in range(3)]
     weights_b, sums_b = pair_weights(scalars, near_images, [s_low, s_high], tiles_b)
-    *far, weights_a, weights_b = fence(*far, weights_a, weights_b)
+    where = {p: (0, t) for t, p in enumerate(tiles_a)}
+    where |= {(i, j + 4): (1, t) for t, (i, j) in enumerate(tiles_b)}
+    ps_near = stacked(near_images, [weights_a, weights_b], where, [4, 5, 3])
+    *far, weights_a, weights_b, ps_near = fence(*far, weights_a, weights_b, ps_near)
     i_far = jnp.concatenate(far[:2], axis=0)
     t_far = jnp.concatenate(far[2:], axis=0)
     s_far = send(t_far, "c", SWAP)
@@ -201,65 +228,62 @@
     tiles_d = [(i, 0) for i in range(4)]
     weights_d, sums_d = pair_weights(scalars, images, [s_far], tiles_d)
     texts = texts + [s_far]
-    where = {p: (0, t) for t, p in enumerate(tiles_a)}
-    where |= {(i, j + 4): (1, t) for t, (i, j) in enumerate(tiles_b)}
     where |= {p: (2, t) for t, p in enumerate(tiles_c)}
     where |= {(i, 7): (3, t) for t, (i, _) in enumerate(tiles_d)}
     weights = [weights_a, weights_b, weights_c, weights_d]
 
+    (ps_far,) = directions(images, texts, weights, where, [], [7])
+    *weights, ps_far = fence(*weights, narrow(ps_far))
+    ps_far = send(ps_far, "c", SWAP)
     value = jnp.sum(sums_a + sums_b + sums_c + sums_d, axis=(1, 2)).reshape(1, 3)
-    (ps_far,) = directions(images, texts, weights, where, [], [7])
-    *weights, ps_far = fence(*weights, ps_far)
-    ps_back = send(narrow(ps_far), "c", SWAP)
-    (pi_far,) = directions(images, texts, weights, where, [3], [])
-    *weights, pi_far = fence(*weights, pi_far)
-    back_x = [send(narrow(pi_far[:rows]), "x", DOWN), send(narrow(pi_far[rows:]), "x", UP)]
-    (pt_far,) = directions(images, texts, weights, where, [], [6])
-    *weights, pt_far, ps_back = fence(*weights, pt_far, ps_back)
-    pt_far = pt_far + wide(ps_back)
-    back_y = [send(narrow(pt_far[:rows]), "y", DOWN), send(narrow(pt_far[rows:]), "y", UP)]
-
-    ps_low, ps_high = directions(images, texts, weights, where, [], [4, 5])
-    *weights, ps_low, ps_high = fence(*weights, ps_low, ps_high)
-    ps_near = send(narrow(jnp.concatenate([ps_low, ps_high], axis=0)), "c", SWAP)
-    pi_low, pi_high, pt_low, pt_high = directions(images, texts, weights, where, [1, 2], [1, 2])
-    *weights, pt_low, pt_high, ps_near, value = fence(*weights, pt_low, pt_high, ps_near, value)
-    pt_low = pt_low + wide(ps_near[: 2 * rows])
-    pt_high = pt_high + wide(ps_near[2 * rows :])
-    value = value + send(value, "c", SWAP)
-    (ps_own,) = directions(images, texts, weights, where, [], [3])
-    b0, b1, b2, b3, pi_low, pi_high, pt_low, pt_high, ps_own, value, *weights = fence(
-        *back_x, *back_y, pi_low, pi_high, pt_low, pt_high, ps_own, value, *weights
+    pi_far, pt_far = directions(images, texts, weights, where, [3], [6])
+    from_far = {(0, j): where[3, j] for j in (4, 5, 3)}
+    ps_near = narrow(stacked([i_far], weights, from_far, [4, 5, 3], ps_near))
+    pi_far = narrow(pi_far)
+    pt_far = narrow(pt_far + wide(ps_far))
+    pi_far, pt_far, ps_near, value, *weights = fence(pi_far, pt_far, ps_near, value, *weights)
+    back = [
+        send(pi_far[:rows], "x", DOWN),
+        send(pi_far[rows:], "x", UP),
+        send(pt_far[:rows], "y", DOWN),
+        send(pt_far[rows:], "y", UP),
+    ]
+    ps_near = send(ps_near, "c", SWAP)
+    pi_low, pi_high, pi_own, pt_low, pt_high, pt_own = directions(images, texts, weights, where, [1, 2, 0], [1, 2, 0])
+    *back, ps_near, pi_low, pi_high, pi_own, pt_low, pt_high, pt_own = fence(
+        *back, ps_near, pi_low, pi_high, pi_own, pt_low, pt_high, pt_own
     )
-    back = [b0, b1, b2, b3]
-
-    pi_low = jnp.concatenate([pi_low[:rows] + wide(back[0]), pi_low[rows:]], axis=0)
-    pi_high = jnp.concatenate([pi_high[:rows], pi_high[rows:] + wide(back[1])], axis=0)
-    pt_low = jnp.concatenate([pt_low[:rows] + wide(back[2]), pt_low[rows:]], axis=0)
-    pt_high = jnp.concatenate([pt_high[:rows], pt_high[rows:] + wide(back[3])], axis=0)
+
+    first, second = ((0, rows), (0, 0)), ((rows, 0), (0, 0))
     near = [
-        send(narrow(pi_low), "x", DOWN),
-        send(narrow(pi_high), "x", UP),
-        send(narrow(pt_low), "y", DOWN),
-        send(narrow(pt_high), "y", UP),
-    ]
-    ps_own = send(narrow(ps_own), "c", SWAP)
-    pi_own, pt_own = directions(images, texts, weights, where, [0], [0])
-    pi_own, pt_own, ps_own, value = fence(pi_own, pt_own, ps_own, value)
-    pt_own = pt_own + wide(ps_own)
-    for axis, pairs in ((Z, EVEN), (Z, ODD), ("x", EVEN)):
+        narrow(pi_low + jnp.pad(wide(back[0]), first)),
+        narrow(pi_high + jnp.pad(wide(back[1]), second)),
+        narrow(pt_low + wide(ps_near[: 2 * rows]) + jnp.pad(wide(back[2]), first)),
+        narrow(pt_high + wide(ps_near[2 * rows : 4 * rows]) + jnp.pad(wide(back[3]), second)),
+    ]
+    *near, value = fence(*near, value)
+    near = [
+        send(near[0], "x", DOWN),
+        send(near[1], "x", UP),
+        send(near[2], "y", DOWN),
+        send(near[3], "y", UP),
+    ]
+    for axis, pairs in (("c", SWAP), (Z, EVEN), (Z, ODD), ("x", EVEN)):
         value = value + send(value, axis, pairs)
+    pt_own = pt_own + wide(ps_near[4 * rows :])
     *near, pi_own, pt_own, value = fence(*near, pi_own, pt_own, value)
     pi_own = pi_own + wide(near[0]) + wide(near[1])
     pt_own = pt_own + wide(near[2]) + wide(near[3])
 
-    last = [send(narrow(pi_own[rows:]), Z, EVEN), send(narrow(pt_own[rows:]), Z, ODD)]
+    last = [narrow(pi_own[rows:]), narrow(pt_own[rows:])]
+    *last, value = fence(*last, value)
+    last = [send(last[0], Z, EVEN), send(last[1], Z, ODD)]
     for axis, pairs in (("x", ODD), ("y", EVEN), ("y", ODD)):
         value = value + send(value, axis, pairs)
     objective_results = value[0] * jnp.stack([jnp.float32(1.0), temperature, jnp.float32(1.0)]) / example_number
     scale = temperature / SCALE
-    image_gradient = projection(scale * (pi_own[:rows] + wide(last[0])), image32, image_inverse)
-    text_grad = projection(scale * (pt_own[:rows] + wide(last[1])), text32, text_inverse)
+    image_gradient = projection(scale * (pi_own[:rows] + wide(last[0])), unit32[:rows], inverse[:rows])
+    text_grad = projection(scale * (pt_own[:rows] + wide(last[1])), unit32[rows:], inverse[rows:])
     return (image_gradient, text_grad, objective_results)
 
 

time: 118 us -> 108 us (0.915)
  other arithmetic: 9.68 us -> 5.75 us
  waiting for transfers between devices: 44.4 us -> 40.8 us
  Pallas kernels: 24.8 us -> 23.3 us
    ppermute x33, waiting for transfers between devices: 44.4 us -> 40.8 us  [send(): return lax.ppermute(value, axis, pairs)]
    pallas_call x7 -> x3, Pallas kernels: 12.2 us -> 9.43 us  [directions(): pl.pallas_call(functools.partial(direction_kernel, len(images), len(texts...]
    pallas_call x0 -> x2, Pallas kernels: none -> 2.46 us  [stacked(): pl.pallas_call(functools.partial(stacked_kernel, len(images), len(weights...]
    reduce_sum x2 -> x1, other arithmetic: 2.21 us -> 0.2 us  [normalize(): inverse = lax.rsqrt(jnp.sum(widened * widened, axis=1, keepdims=True) + EPS)]
  transfers between devices with their start and end apart: 33 -> 33, of which waited for: 14 -> 15; matrix products, arithmetic and copies ran while one was open for 4% -> 2% of each run, Pallas kernels for 17% -> 19%
where the time goes in v3:
time: 108 us
  waiting for transfers between devices  40.8 us (38%)
  starting transfers between devices  35.3 us (33%)
  Pallas kernels  23.3 us (22%)
  other arithmetic  5.75 us (5%)
  between operations  2.34 us (2%)
    ppermute x33, waiting for transfers between devices, send(): return lax.ppermute(value, axis, pairs)  40.8 us
    ppermute x33, starting transfers between devices, send(): return lax.ppermute(value, axis, pairs)  35.3 us
    pallas_call x4, Pallas kernels, pair_weights(): pl.pallas_call(functools.partial(pair_kernel, len(images), len(texts), ti...  11.5 us
    pallas_call x3, Pallas kernels, directions(): pl.pallas_call(functools.partial(direction_kernel, len(images), len(texts...  9.43 us
    pallas_call x2, Pallas kernels, stacked(): pl.pallas_call(functools.partial(stacked_kernel, len(images), len(weights...  2.46 us
  transfers between devices with their start and end apart: 33, of which 15 were waited for; matrix products, arithmetic and copies ran while one was open for 2% of the time, Pallas kernels for 19%

profile of v3, /device:TPU:6, one launch (start us, length us, event | category | flops | bytes accessed | tf_op | source)
XLA Modules:
  0.0 108.1 jit_solution(16115612360110198686)
XLA Ops:
  0.6 1.1 %pad_maximum_fusion.1 = bf16[256,1152]{1,0:T(8,128)(2,1)S(1)} fusion(bf16[128,1152]{1,0:T(8,128)(2,1)} %param.5, bf16[128,1152]{1,0:T(8,128)(2,1)} %param.4), kind=kLoop, calls=%fused_computation.18 | loop fusion | flops 1179648 | bytes 1179648 | tf_op jit(solution)/shard_map/concatenate | solution.py:178
  1.7 0.2 fusion
  1.9 0.2 fusion.4
  2.2 2.0 %collective-permute-start = (bf16[128,1152]{1,0:T(8,128)(2,1)S(1)}, bf16[128,1152]{1,0:T(8,128)(2,1)S(1)}, u32[]{:S(2)}, u32[]{:S(2)}) collective-permute-start(bf16[128,1152]{1,0:T(8,128)(2,1)S(1)} %get-tuple-element.169), channel_id=1, source_target_pairs={{0,2},{2,0},{4,6},{6,4},{1,3},{3,1},{5,7},{7,5},{8,10},{10,8},{12,... | collective-permute-start | bytes 884744 | tf_op jit(solution)/shard_map/ppermute | solution.py:25
  4.2 2.5 %collective-permute-start.1 = (bf16[128,1152]{1,0:T(8,128)(2,1)S(1)}, bf16[128,1152]{1,0:T(8,128)(2,1)S(1)}, u32[]{:S(2)}, u32[]{:S(2)}) collective-permute-start(bf16[128,1152]{1,0:T(8,128)(2,1)S(1)} %get-tuple-element.168), channel_id=1, source_target_pairs={{2,4},{4,2},{6,0},{0,6},{3,5},{5,3},{7,1},{1,7},{10,12},{12,10},{1... | collective-permute-start | bytes 884744 | tf_op jit(solution)/shard_map/ppermute | solution.py:25
  6.7 4.5 %collective-permute-done = bf16[128,1152]{1,0:T(8,128)(2,1)S(1)} collective-permute-done((bf16[128,1152]{1,0:T(8,128)(2,1)S(1)}, bf16[128,1152]{1,0:T(8,128)(2,1)S(1)}, u32[]{:S(2)}, u32[]{:S(2)}) %collective-permute-start) | collective-permute-done | bytes 294944 | tf_op jit(solution)/shard_map/ppermute | solution.py:25
  11.2 2.7 %collective-permute-done.1 = bf16[128,1152]{1,0:T(8,128)(2,1)S(1)} collective-permute-done((bf16[128,1152]{1,0:T(8,128)(2,1)S(1)}, bf16[128,1152]{1,0:T(8,128)(2,1)S(1)}, u32[]{:S(2)}, u32[]{:S(2)}) %collective-permute-start.1) | collective-permute-done | bytes 294944 | tf_op jit(solution)/shard_map/ppermute | solution.py:25
  13.9 0.5 collective-permute-start.2
  14.5 1.5 %collective-permute-start.3 = (bf16[256,1152]{1,0:T(8,128)(2,1)S(1)}, bf16[256,1152]{1,0:T(8,128)(2,1)S(1)}, u32[]{:S(2)}, u32[]{:S(2)}) collective-permute-start(bf16[256,1152]{1,0:T(8,128)(2,1)S(1)} %pad_maximum_fusion.2.refs_0_), channel_id=1, source_target_pairs={{0,24},{8,0},{16,8},{24,16},{1,25},{9,1},{17,9},{25,17},{2,26},{10... | collective-permute-start | bytes 1769480 | tf_op jit(solution)/shard_map/ppermute | solution.py:25
  16.1 1.6 %collective-permute-start.4 = (bf16[256,1152]{1,0:T(8,128)(2,1)S(1)}, bf16[256,1152]{1,0:T(8,128)(2,1)S(1)}, u32[]{:S(2)}, u32[]{:S(2)}) collective-permute-start(bf16[256,1152]{1,0:T(8,128)(2,1)S(1)} %pad_maximum_fusion.3.refs_3_.refs_4_), channel_id=1, source_target_pairs={{0,32},{32,64},{64,96},{96,0},{1,33},{33,65},{65,97},{97,1},{2,34}... | collective-permute-start | bytes 1769480 | tf_op jit(solution)/shard_map/ppermute | solution.py:25
  17.7 1.7 %collective-permute-start.5 = (bf16[256,1152]{1,0:T(8,128)(2,1)S(1)}, bf16[256,1152]{1,0:T(8,128)(2,1)S(1)}, u32[]{:S(2)}, u32[]{:S(2)}) collective-permute-start(bf16[256,1152]{1,0:T(8,128)(2,1)S(1)} %pad_maximum_fusion.3.refs_3_.refs_4_), channel_id=1, source_target_pairs={{0,96},{32,0},{64,32},{96,64},{1,97},{33,1},{65,33},{97,65},{2,98}... | collective-permute-start | bytes 1769480 | tf_op jit(solution)/shard_map/ppermute | solution.py:25
  20.8 0.2 collective-permute-done.7
  21.0 6.9 %collective-permute-done.2.refs_1_ = bf16[256,1152]{1,0:T(8,128)(2,1)S(1)} collective-permute-done((bf16[256,1152]{1,0:T(8,128)(2,1)S(1)}, bf16[256,1152]{1,0:T(8,128)(2,1)S(1)}, u32[]{:S(2)}, u32[]{:S(2)}) %collective-permute-start.2) | collective-permute-done | bytes 589856 | tf_op jit(solution)/shard_map/ppermute | solution.py:25
  27.9 1.4 %collective-permute-done.3.refs_2_ = bf16[256,1152]{1,0:T(8,128)(2,1)S(1)} collective-permute-done((bf16[256,1152]{1,0:T(8,128)(2,1)S(1)}, bf16[256,1152]{1,0:T(8,128)(2,1)S(1)}, u32[]{:S(2)}, u32[]{:S(2)}) %collective-permute-start.3) | collective-permute-done | bytes 589856 | tf_op jit(solution)/shard_map/ppermute | solution.py:25
  29.3 1.4 %collective-permute-done.4.refs_4_.refs_5_ = bf16[256,1152]{1,0:T(8,128)(2,1)S(1)} collective-permute-done((bf16[256,1152]{1,0:T(8,128)(2,1)S(1)}, bf16[256,1152]{1,0:T(8,128)(2,1)S(1)}, u32[]{:S(2)}, u32[]{:S(2)}) %collective-permute-start.4) | collective-permute-done | bytes 589856 | tf_op jit(solution)/shard_map/ppermute | solution.py:25
  31.0 1.8 %collective-permute-start.8 = (bf16[128,1152]{1,0:T(8,128)(2,1)S(1)}, bf16[128,1152]{1,0:T(8,128)(2,1)S(1)}, u32[]{:S(2)}, u32[]{:S(2)}) collective-permute-start(bf16[128,1152]{1,0:T(8,128)(2,1)S(1)} %slice.75), channel_id=1, source_target_pairs={{0,8},{8,16},{16,24},{24,0},{1,9},{9,17},{17,25},{25,1},{2,10},{10... | collective-permute-start | bytes 884744 | tf_op jit(solution)/shard_map/ppermute | solution.py:25
  32.8 0.4 collective-permute-start.9
  33.2 1.6 %collective-permute-start.10 = (bf16[128,1152]{1,0:T(8,128)(2,1)S(1)}, bf16[128,1152]{1,0:T(8,128)(2,1)S(1)}, u32[]{:S(2)}, u32[]{:S(2)}) collective-permute-start(bf16[128,1152]{1,0:T(8,128)(2,1)S(1)} %slice.77), channel_id=1, source_target_pairs={{0,32},{32,64},{64,96},{96,0},{1,33},{33,65},{65,97},{97,1},{2,34}... | collective-permute-start | bytes 884744 | tf_op jit(solution)/shard_map/ppermute | solution.py:25
  34.8 1.7 %collective-permute-start.11 = (bf16[128,1152]{1,0:T(8,128)(2,1)S(1)}, bf16[128,1152]{1,0:T(8,128)(2,1)S(1)}, u32[]{:S(2)}, u32[]{:S(2)}) collective-permute-start(bf16[128,1152]{1,0:T(8,128)(2,1)S(1)} %slice.78), channel_id=1, source_target_pairs={{0,96},{32,0},{64,32},{96,64},{1,97},{33,1},{65,33},{97,65},{2,98}... | collective-permute-start | bytes 884744 | tf_op jit(solution)/shard_map/ppermute | solution.py:25
  36.5 3.9 %shard_map.67 = (bf16[12,256,256]{2,1,0:T(8,128)(2,1)S(1)}, f32[3,8,256]{2,1,0:T(8,128)S(1)}) custom-call(f32[2]{0:T(128)S(1)} %pad_maximum_fusion.4.scalars, bf16[256,1152]{1,0:T(8,128)(2,1)S(1)} %pad_maximum_fusion.2.refs_0_, bf16[256,1152]{1,0:T(8,128)(2,1)S(1)} %collective-permute-done.2.refs_1_, bf16[256,1152]{1,0:T(8,128)(2,1)S(1)} %collective-permute-done.3.refs_2_, ...), custom_call_target="tpu_custom_call" | custom-call | flops 1 | bytes 1 | tf_op jit(solution)/shard_map/pallas_call | solution.py:86
  40.5 2.3 %shard_map.68 = (bf16[6,256,256]{2,1,0:T(8,128)(2,1)S(1)}, f32[3,8,256]{2,1,0:T(8,128)S(1)}) custom-call(f32[2]{0:T(128)S(1)} %pad_maximum_fusion.4.scalars, bf16[256,1152]{1,0:T(8,128)(2,1)S(1)} %pad_maximum_fusion.2.refs_0_, bf16[256,1152]{1,0:T(8,128)(2,1)S(1)} %collective-permute-done.2.refs_1_, bf16[256,1152]{1,0:T(8,128)(2,1)S(1)} %collective-permute-done.3.refs_2_, ...), custom_call_target="tpu_custom_call" | custom-call | flops 1 | bytes 1 | tf_op jit(solution)/shard_map/pallas_call | solution.py:86
  42.9 1.7 %shard_map.69.refs_5_ = f32[768,1152]{1,0:T(8,128)S(1)} custom-call(bf16[256,1152]{1,0:T(8,128)(2,1)S(1)} %pad_maximum_fusion.2.refs_0_, bf16[256,1152]{1,0:T(8,128)(2,1)S(1)} %collective-permute-done.2.refs_1_, bf16[256,1152]{1,0:T(8,128)(2,1)S(1)} %collective-permute-done.3.refs_2_, bf16[12,256,256]{2,1,0:T(8,128)(2,1)S(1)} %get-tuple-element.116.refs_3_.refs_12_.refs_1_, ...), custom_call_target="tpu_custom_call" | custom-call | flops 1 | bytes 1 | tf_op jit(solution)/shard_map/pallas_call | solution.py:117
  44.7 0.3 collective-permute-start.13
  45.1 3.4 %shard_map.70 = (bf16[10,256,256]{2,1,0:T(8,128)(2,1)S(1)}, f32[3,8,256]{2,1,0:T(8,128)S(1)}) custom-call(f32[2]{0:T(128)S(1)} %pad_maximum_fusion.4.scalars, bf16[256,1152]{1,0:T(8,128)(2,1)S(1)} %pad_maximum_fusion.2.refs_0_, bf16[256,1152]{1,0:T(8,128)(2,1)S(1)} %collective-permute-done.2.refs_1_, bf16[256,1152]{1,0:T(8,128)(2,1)S(1)} %collective-permute-done.3.refs_2_, ...), custom_call_target="tpu_custom_call" | custom-call | flops 1 | bytes 1 | tf_op jit(solution)/shard_map/pallas_call | solution.py:86
  48.5 1.8 %shard_map.71 = (bf16[4,256,256]{2,1,0:T(8,128)(2,1)S(1)}, f32[3,8,256]{2,1,0:T(8,128)S(1)}) custom-call(f32[2]{0:T(128)S(1)} %pad_maximum_fusion.4.scalars, bf16[256,1152]{1,0:T(8,128)(2,1)S(1)} %pad_maximum_fusion.2.refs_0_, bf16[256,1152]{1,0:T(8,128)(2,1)S(1)} %collective-permute-done.2.refs_1_, bf16[256,1152]{1,0:T(8,128)(2,1)S(1)} %collective-permute-done.3.refs_2_, ...), custom_call_target="tpu_custom_call" | custom-call | flops 1 | bytes 1 | tf_op jit(solution)/shard_map/pallas_call | solution.py:86
  50.3 0.9 shard_map.72
  51.3 0.6 collective-permute-start.14
  51.8 2.2 %shard_map.73 = (f32[256,1152]{1,0:T(8,128)S(1)}, f32[256,1152]{1,0:T(8,128)S(1)}) custom-call(bf16[256,1152]{1,0:T(8,128)(2,1)S(1)} %pad_maximum_fusion.2.refs_0_, bf16[256,1152]{1,0:T(8,128)(2,1)S(1)} %collective-permute-done.2.refs_1_, bf16[256,1152]{1,0:T(8,128)(2,1)S(1)} %collective-permute-done.3.refs_2_, ...), custom_call_target="tpu_custom_call" | custom-call | flops 1 | bytes 1 | tf_op jit(solution)/shard_map/pallas_call | solution.py:155
  54.1 0.7 shard_map.74
  54.9 0.2 convert_element_type.78
  55.1 0.1 add_reduce_fusion
  55.2 0.1 add_convert_fusion.4
  55.3 0.1 collective-permute-start.19
  55.5 0.1 fusion.7
  55.6 0.9 collective-permute-start.15
  56.5 2.4 %collective-permute-start.16 = (f16[128,1152]{1,0:T(8,128)(2,1)S(1)}, f16[128,1152]{1,0:T(8,128)(2,1)S(1)}, u32[]{:S(2)}, u32[]{:S(2)}) collective-permute-start(f16[128,1152]{1,0:T(8,128)(2,1)S(1)} %get-tuple-element.166), channel_id=1, source_target_pairs={{0,8},{8,16},{16,24},{24,0},{1,9},{9,17},{17,25},{25,1},{2,10},{10... | collective-permute-start | bytes 884744 | tf_op jit(solution)/shard_map/ppermute | solution.py:25
  59.0 1.9 %collective-permute-start.17 = (f16[128,1152]{1,0:T(8,128)(2,1)S(1)}, f16[128,1152]{1,0:T(8,128)(2,1)S(1)}, u32[]{:S(2)}, u32[]{:S(2)}) collective-permute-start(f16[128,1152]{1,0:T(8,128)(2,1)S(1)} %get-tuple-element.165), channel_id=1, source_target_pairs={{0,96},{32,0},{64,32},{96,64},{1,97},{33,1},{65,33},{97,65},{2,98}... | collective-permute-start | bytes 884744 | tf_op jit(solution)/shard_map/ppermute | solution.py:25
  60.8 0.2 collective-permute-start.18
  61.1 6.3 %shard_map.75 = (f32[256,1152]{1,0:T(8,128)S(1)}, f32[256,1152]{1,0:T(8,128)S(1)}, f32[256,1152]{1,0:T(8,128)S(1)}, f32[256,1152]{1,0:T(8,128)S(1)}, f32[256,1152]{1,0:T(8,128)S(1)}, /*index=5*/f32[256,1152]{1,0:T(8,128)S(1)}) custom-call(bf16[256,1152]{1,0:T(8,128)(2,1)S(1)} %pad_maximum_fusion.2.refs_0_, ...), custom_call_target="tpu_custom_call" | custom-call | flops 1 | bytes 1 | tf_op jit(solution)/shard_map/pallas_call | solution.py:155
  67.4 0.5 collective-permute-done.17
  67.9 2.7 %collective-permute-done.18 = f16[128,1152]{1,0:T(8,128)(2,1)S(1)} collective-permute-done((f16[128,1152]{1,0:T(8,128)(2,1)S(1)}, f16[128,1152]{1,0:T(8,128)(2,1)S(1)}, u32[]{:S(2)}, u32[]{:S(2)}) %collective-permute-start.18) | collective-permute-done | bytes 294944 | tf_op jit(solution)/shard_map/ppermute | solution.py:25
  70.6 0.1 add_convert_fusion.3
  70.8 0.6 convert_add_fusion.2
  71.5 3.2 %collective-permute-start.21 = (f16[256,1152]{1,0:T(8,128)(2,1)S(1)}, f16[256,1152]{1,0:T(8,128)(2,1)S(1)}, u32[]{:S(2)}, u32[]{:S(2)}) collective-permute-start(f16[256,1152]{1,0:T(8,128)(2,1)S(1)} %get-tuple-element.137), channel_id=1, source_target_pairs={{0,8},{8,16},{16,24},{24,0},{1,9},{9,17},{17,25},{25,1},{2,10},{10... | collective-permute-start | bytes 1769480 | tf_op jit(solution)/shard_map/ppermute | solution.py:25
  74.7 0.3 collective-permute-start.22
  75.0 1.7 %collective-permute-start.23 = (f16[256,1152]{1,0:T(8,128)(2,1)S(1)}, f16[256,1152]{1,0:T(8,128)(2,1)S(1)}, u32[]{:S(2)}, u32[]{:S(2)}) collective-permute-start(f16[256,1152]{1,0:T(8,128)(2,1)S(1)} %get-tuple-element.139), channel_id=1, source_target_pairs={{0,32},{32,64},{64,96},{96,0},{1,33},{33,65},{65,97},{97,1},{2,34}... | collective-permute-start | bytes 1769480 | tf_op jit(solution)/shard_map/ppermute | solution.py:25
  76.7 1.1 %collective-permute-done.24 = f32[1,3]{1,0:T(1,128)S(1)} collective-permute-done((f32[1,3]{1,0:T(1,128)S(1)}, f32[1,3]{1,0:T(1,128)S(1)}, u32[]{:S(2)}, u32[]{:S(2)}) %collective-permute-start.24) | collective-permute-done | bytes 44 | tf_op jit(solution)/shard_map/ppermute | solution.py:25
  77.9 0.9 collective-permute-start.25
  78.8 2.6 %collective-permute-done.25 = f32[1,3]{1,0:T(1,128)S(1)} collective-permute-done((f32[1,3]{1,0:T(1,128)S(1)}, f32[1,3]{1,0:T(1,128)S(1)}, u32[]{:S(2)}, u32[]{:S(2)}) %collective-permute-start.25) | collective-permute-done | bytes 44 | tf_op jit(solution)/shard_map/ppermute | solution.py:25
  81.4 2.5 %collective-permute-start.26 = (f32[1,3]{1,0:T(1,128)S(1)}, f32[1,3]{1,0:T(1,128)S(1)}, u32[]{:S(2)}, u32[]{:S(2)}) collective-permute-start(f32[1,3]{1,0:T(1,128)S(1)} %add.110), channel_id=1, source_target_pairs={{2,4},{4,2},{6,0},{0,6},{3,5},{5,3},{7,1},{1,7},{10,12},{12,10},{1... | collective-permute-start | bytes 44 | tf_op jit(solution)/shard_map/ppermute | solution.py:25
  83.9 2.2 %collective-permute-done.26 = f32[1,3]{1,0:T(1,128)S(1)} collective-permute-done((f32[1,3]{1,0:T(1,128)S(1)}, f32[1,3]{1,0:T(1,128)S(1)}, u32[]{:S(2)}, u32[]{:S(2)}) %collective-permute-start.26) | collective-permute-done | bytes 44 | tf_op jit(solution)/shard_map/ppermute | solution.py:25
  86.2 3.5 %collective-permute-done.27 = f32[1,3]{1,0:T(1,128)S(1)} collective-permute-done((f32[1,3]{1,0:T(1,128)S(1)}, f32[1,3]{1,0:T(1,128)S(1)}, u32[]{:S(2)}, u32[]{:S(2)}) %collective-permute-start.27) | collective-permute-done | bytes 44 | tf_op jit(solution)/shard_map/ppermute | solution.py:25
  89.7 0.2 convert_add_fusion.1
  89.9 0.2 convert_add_fusion
  90.2 2.6 %collective-permute-start.29 = (f16[128,1152]{1,0:T(8,128)(2,1)S(1)}, f16[128,1152]{1,0:T(8,128)(2,1)S(1)}, u32[]{:S(2)}, u32[]{:S(2)}) collective-permute-start(f16[128,1152]{1,0:T(8,128)(2,1)S(1)} %slice_convert_fusion), channel_id=1, source_target_pairs={{2,4},{4,2},{6,0},{0,6},{3,5},{5,3},{7,1},{1,7},{10,12},{12,10},{1... | collective-permute-start | bytes 884744 | tf_op jit(solution)/shard_map/ppermute | solution.py:25
  92.8 0.5 collective-permute-start.30
  93.3 4.3 %collective-permute-done.30 = f32[1,3]{1,0:T(1,128)S(1)} collective-permute-done((f32[1,3]{1,0:T(1,128)S(1)}, f32[1,3]{1,0:T(1,128)S(1)}, u32[]{:S(2)}, u32[]{:S(2)}) %collective-permute-start.30) | collective-permute-done | bytes 44 | tf_op jit(solution)/shard_map/ppermute | solution.py:25
  97.6 0.2 collective-permute-start.31
  97.7 3.4 %collective-permute-done.31 = f32[1,3]{1,0:T(1,128)S(1)} collective-permute-done((f32[1,3]{1,0:T(1,128)S(1)}, f32[1,3]{1,0:T(1,128)S(1)}, u32[]{:S(2)}, u32[]{:S(2)}) %collective-permute-start.31) | collective-permute-done | bytes 44 | tf_op jit(solution)/shard_map/ppermute | solution.py:25
  101.1 1.5 %collective-permute-start.32 = (f32[1,3]{1,0:T(1,128)S(1)}, f32[1,3]{1,0:T(1,128)S(1)}, u32[]{:S(2)}, u32[]{:S(2)}) collective-permute-start(f32[1,3]{1,0:T(1,128)S(1)} %add.120), channel_id=1, source_target_pairs={{32,64},{64,32},{96,0},{0,96},{33,65},{65,33},{97,1},{1,97},{34,66... | collective-permute-start | bytes 44 | tf_op jit(solution)/shard_map/ppermute | solution.py:25
  102.6 3.3 %collective-permute-done.32 = f32[1,3]{1,0:T(1,128)S(1)} collective-permute-done((f32[1,3]{1,0:T(1,128)S(1)}, f32[1,3]{1,0:T(1,128)S(1)}, u32[]{:S(2)}, u32[]{:S(2)}) %collective-permute-start.32) | collective-permute-done | bytes 44 | tf_op jit(solution)/shard_map/ppermute | solution.py:25
  105.9 0.6 fusion.3
  106.5 0.3 multiply_reduce_fusion
  106.8 1.3 %subtract_multiply_fusion = (f32[128,1152]{1,0:T(8,128)}, f32[128,1152]{1,0:T(8,128)}) fusion(f32[256,1152]{1,0:T(8,128)S(1)} %get-tuple-element.163, f16[128,1152]{1,0:T(8,128)(2,1)S(1)} %collective-permute-done.29, f32[256,1152]{1,0:T(8,128)S(1)} %convert_add_fusion, f32[128]{0:T(128)S(1)} %get-tuple-element.170, f32[128]{0:T(128)S(1)} %get-tuple-element.153, ...), kind=kLoop, calls=%fused_computation.21 | loop fusion | flops 1769472 | bytes 4130820 | tf_op jit(solution)/shard_map/mul | solution.py:40
  (54 shorter events, 1.2 us)
Async XLA Ops:
  2.2 9.0 %collective-permute-start = (bf16[128,1152]{1,0:T(8,128)(2,1)S(1)}, bf16[128,1152]{1,0:T(8,128)(2,1)S(1)}, u32[]{:S(2)}, u32[]{:S(2)}) collective-permute-start(bf16[128,1152]{1,0:T(8,128)(2,1)S(1)} %get-tuple-element.169), channel_id=1, source_target_pairs={{0,2},{2,0},{4,6},{6,4},{1,3},{3,1},{5,7},{7,5},{8,10},{10,8},{12,... | collective-permute-start | bytes 884744 | tf_op jit(solution)/shard_map/ppermute | solution.py:25
  4.2 9.7 %collective-permute-start.1 = (bf16[128,1152]{1,0:T(8,128)(2,1)S(1)}, bf16[128,1152]{1,0:T(8,128)(2,1)S(1)}, u32[]{:S(2)}, u32[]{:S(2)}) collective-permute-start(bf16[128,1152]{1,0:T(8,128)(2,1)S(1)} %get-tuple-element.168), channel_id=1, source_target_pairs={{2,4},{4,2},{6,0},{0,6},{3,5},{5,3},{7,1},{1,7},{10,12},{12,10},{1... | collective-permute-start | bytes 884744 | tf_op jit(solution)/shard_map/ppermute | solution.py:25
  6.7 12.7 %collective-permute-start.6 = (bf16[128,1152]{1,0:T(8,128)(2,1)S(1)}, bf16[128,1152]{1,0:T(8,128)(2,1)S(1)}, u32[]{:S(2)}, u32[]{:S(2)}) collective-permute-start(bf16[128,1152]{1,0:T(8,128)(2,1)S(1)} %get-tuple-element.168), channel_id=1, source_target_pairs={{0,1},{1,0},{2,3},{3,2},{4,5},{5,4},{6,7},{7,6},{8,9},{9,8},{10,11... | collective-permute-start | bytes 884744 | tf_op jit(solution)/shard_map/ppermute | solution.py:25
  13.9 13.9 %collective-permute-start.2 = (bf16[256,1152]{1,0:T(8,128)(2,1)S(1)}, bf16[256,1152]{1,0:T(8,128)(2,1)S(1)}, u32[]{:S(2)}, u32[]{:S(2)}) collective-permute-start(bf16[256,1152]{1,0:T(8,128)(2,1)S(1)} %pad_maximum_fusion.2.refs_0_), channel_id=1, source_target_pairs={{0,8},{8,16},{16,24},{24,0},{1,9},{9,17},{17,25},{25,1},{2,10},{10... | collective-permute-start | bytes 1769480 | tf_op jit(solution)/shard_map/ppermute | solution.py:25
  14.5 14.8 %collective-permute-start.3 = (bf16[256,1152]{1,0:T(8,128)(2,1)S(1)}, bf16[256,1152]{1,0:T(8,128)(2,1)S(1)}, u32[]{:S(2)}, u32[]{:S(2)}) collective-permute-start(bf16[256,1152]{1,0:T(8,128)(2,1)S(1)} %pad_maximum_fusion.2.refs_0_), channel_id=1, source_target_pairs={{0,24},{8,0},{16,8},{24,16},{1,25},{9,1},{17,9},{25,17},{2,26},{10... | collective-permute-start | bytes 1769480 | tf_op jit(solution)/shard_map/ppermute | solution.py:25
  16.1 14.7 %collective-permute-start.4 = (bf16[256,1152]{1,0:T(8,128)(2,1)S(1)}, bf16[256,1152]{1,0:T(8,128)(2,1)S(1)}, u32[]{:S(2)}, u32[]{:S(2)}) collective-permute-start(bf16[256,1152]{1,0:T(8,128)(2,1)S(1)} %pad_maximum_fusion.3.refs_3_.refs_4_), channel_id=1, source_target_pairs={{0,32},{32,64},{64,96},{96,0},{1,33},{33,65},{65,97},{97,1},{2,34}... | collective-permute-start | bytes 1769480 | tf_op jit(solution)/shard_map/ppermute | solution.py:25
  17.7 13.0 %collective-permute-start.5 = (bf16[256,1152]{1,0:T(8,128)(2,1)S(1)}, bf16[256,1152]{1,0:T(8,128)(2,1)S(1)}, u32[]{:S(2)}, u32[]{:S(2)}) collective-permute-start(bf16[256,1152]{1,0:T(8,128)(2,1)S(1)} %pad_maximum_fusion.3.refs_3_.refs_4_), channel_id=1, source_target_pairs={{0,96},{32,0},{64,32},{96,64},{1,97},{33,1},{65,33},{97,65},{2,98}... | collective-permute-start | bytes 1769480 | tf_op jit(solution)/shard_map/ppermute | solution.py:25
  19.4 1.6 %collective-permute-start.7 = (bf16[128,1152]{1,0:T(8,128)(2,1)S(1)}, bf16[128,1152]{1,0:T(8,128)(2,1)S(1)}, u32[]{:S(2)}, u32[]{:S(2)}) collective-permute-start(bf16[128,1152]{1,0:T(8,128)(2,1)S(1)} %collective-permute-done.1), channel_id=1, source_target_pairs={{0,1},{1,0},{2,3},{3,2},{4,5},{5,4},{6,7},{7,6},{8,9},{9,8},{10,11... | collective-permute-start | bytes 884744 | tf_op jit(solution)/shard_map/ppermute | solution.py:25
  30.8 9.6 %collective-permute-start.12 = (bf16[512,1152]{1,0:T(8,128)(2,1)S(1)}, bf16[512,1152]{1,0:T(8,128)(2,1)S(1)}, u32[]{:S(2)}, u32[]{:S(2)}) collective-permute-start(bf16[512,1152]{1,0:T(8,128)(2,1)S(1)} %pad_maximum_fusion), channel_id=1, source_target_pairs={{0,1},{1,0},{2,3},{3,2},{4,5},{5,4},{6,7},{7,6},{8,9},{9,8},{10,11... | collective-permute-start | bytes 3538952 | tf_op jit(solution)/shard_map/ppermute | solution.py:25
  31.0 13.6 %collective-permute-start.8 = (bf16[128,1152]{1,0:T(8,128)(2,1)S(1)}, bf16[128,1152]{1,0:T(8,128)(2,1)S(1)}, u32[]{:S(2)}, u32[]{:S(2)}) collective-permute-start(bf16[128,1152]{1,0:T(8,128)(2,1)S(1)} %slice.75), channel_id=1, source_target_pairs={{0,8},{8,16},{16,24},{24,0},{1,9},{9,17},{17,25},{25,1},{2,10},{10... | collective-permute-start | bytes 884744 | tf_op jit(solution)/shard_map/ppermute | solution.py:25
  32.8 11.8 %collective-permute-start.9 = (bf16[128,1152]{1,0:T(8,128)(2,1)S(1)}, bf16[128,1152]{1,0:T(8,128)(2,1)S(1)}, u32[]{:S(2)}, u32[]{:S(2)}) collective-permute-start(bf16[128,1152]{1,0:T(8,128)(2,1)S(1)} %slice.76), channel_id=1, source_target_pairs={{0,24},{8,0},{16,8},{24,16},{1,25},{9,1},{17,9},{25,17},{2,26},{10... | collective-permute-start | bytes 884744 | tf_op jit(solution)/shard_map/ppermute | solution.py:25
  33.2 11.4 %collective-permute-start.10 = (bf16[128,1152]{1,0:T(8,128)(2,1)S(1)}, bf16[128,1152]{1,0:T(8,128)(2,1)S(1)}, u32[]{:S(2)}, u32[]{:S(2)}) collective-permute-start(bf16[128,1152]{1,0:T(8,128)(2,1)S(1)} %slice.77), channel_id=1, source_target_pairs={{0,32},{32,64},{64,96},{96,0},{1,33},{33,65},{65,97},{97,1},{2,34}... | collective-permute-start | bytes 884744 | tf_op jit(solution)/shard_map/ppermute | solution.py:25
  34.8 9.8 %collective-permute-start.11 = (bf16[128,1152]{1,0:T(8,128)(2,1)S(1)}, bf16[128,1152]{1,0:T(8,128)(2,1)S(1)}, u32[]{:S(2)}, u32[]{:S(2)}) collective-permute-start(bf16[128,1152]{1,0:T(8,128)(2,1)S(1)} %slice.78), channel_id=1, source_target_pairs={{0,96},{32,0},{64,32},{96,64},{1,97},{33,1},{65,33},{97,65},{2,98}... | collective-permute-start | bytes 884744 | tf_op jit(solution)/shard_map/ppermute | solution.py:25
  44.7 3.8 %collective-permute-start.13 = (bf16[256,1152]{1,0:T(8,128)(2,1)S(1)}, bf16[256,1152]{1,0:T(8,128)(2,1)S(1)}, u32[]{:S(2)}, u32[]{:S(2)}) collective-permute-start(bf16[256,1152]{1,0:T(8,128)(2,1)S(1)} %constant_dynamic-update-slice_fusion.4.refs_10_), channel_id=1, source_target_pairs={{0,1},{1,0},{2,3},{3,2},{4,5},{5,4},{6,7},{7,6},{8,9},{9,8},{10,11... | collective-permute-start | bytes 1769480 | tf_op jit(solution)/shard_map/ppermute | solution.py:25
  51.3 3.9 %collective-permute-start.14 = (f16[256,1152]{1,0:T(8,128)(2,1)S(1)}, f16[256,1152]{1,0:T(8,128)(2,1)S(1)}, u32[]{:S(2)}, u32[]{:S(2)}) collective-permute-start(f16[256,1152]{1,0:T(8,128)(2,1)S(1)} %convert_element_type.74), channel_id=1, source_target_pairs={{0,1},{1,0},{2,3},{3,2},{4,5},{5,4},{6,7},{7,6},{8,9},{9,8},{10,11... | collective-permute-start | bytes 1769480 | tf_op jit(solution)/shard_map/ppermute | solution.py:25
  55.3 15.3 %collective-permute-start.19 = (f16[768,1152]{1,0:T(8,128)(2,1)S(1)}, f16[768,1152]{1,0:T(8,128)(2,1)S(1)}, u32[]{:S(2)}, u32[]{:S(2)}) collective-permute-start(f16[768,1152]{1,0:T(8,128)(2,1)S(1)} %convert_element_type.78), channel_id=1, source_target_pairs={{0,1},{1,0},{2,3},{3,2},{4,5},{5,4},{6,7},{7,6},{8,9},{9,8},{10,11... | collective-permute-start | bytes 5308424 | tf_op jit(solution)/shard_map/ppermute | solution.py:25
  55.6 11.8 %collective-permute-start.15 = (f16[128,1152]{1,0:T(8,128)(2,1)S(1)}, f16[128,1152]{1,0:T(8,128)(2,1)S(1)}, u32[]{:S(2)}, u32[]{:S(2)}) collective-permute-start(f16[128,1152]{1,0:T(8,128)(2,1)S(1)} %get-tuple-element.167), channel_id=1, source_target_pairs={{0,24},{8,0},{16,8},{24,16},{1,25},{9,1},{17,9},{25,17},{2,26},{10... | collective-permute-start | bytes 884744 | tf_op jit(solution)/shard_map/ppermute | solution.py:25
  56.5 11.0 %collective-permute-start.16 = (f16[128,1152]{1,0:T(8,128)(2,1)S(1)}, f16[128,1152]{1,0:T(8,128)(2,1)S(1)}, u32[]{:S(2)}, u32[]{:S(2)}) collective-permute-start(f16[128,1152]{1,0:T(8,128)(2,1)S(1)} %get-tuple-element.166), channel_id=1, source_target_pairs={{0,8},{8,16},{16,24},{24,0},{1,9},{9,17},{17,25},{25,1},{2,10},{10... | collective-permute-start | bytes 884744 | tf_op jit(solution)/shard_map/ppermute | solution.py:25
  59.0 8.9 %collective-permute-start.17 = (f16[128,1152]{1,0:T(8,128)(2,1)S(1)}, f16[128,1152]{1,0:T(8,128)(2,1)S(1)}, u32[]{:S(2)}, u32[]{:S(2)}) collective-permute-start(f16[128,1152]{1,0:T(8,128)(2,1)S(1)} %get-tuple-element.165), channel_id=1, source_target_pairs={{0,96},{32,0},{64,32},{96,64},{1,97},{33,1},{65,33},{97,65},{2,98}... | collective-permute-start | bytes 884744 | tf_op jit(solution)/shard_map/ppermute | solution.py:25
  60.8 9.8 %collective-permute-start.18 = (f16[128,1152]{1,0:T(8,128)(2,1)S(1)}, f16[128,1152]{1,0:T(8,128)(2,1)S(1)}, u32[]{:S(2)}, u32[]{:S(2)}) collective-permute-start(f16[128,1152]{1,0:T(8,128)(2,1)S(1)} %get-tuple-element.164), channel_id=1, source_target_pairs={{0,32},{32,64},{64,96},{96,0},{1,33},{33,65},{65,97},{97,1},{2,34}... | collective-permute-start | bytes 884744 | tf_op jit(solution)/shard_map/ppermute | solution.py:25
  71.4 18.3 %collective-permute-start.20 = (f16[256,1152]{1,0:T(8,128)(2,1)S(1)}, f16[256,1152]{1,0:T(8,128)(2,1)S(1)}, u32[]{:S(2)}, u32[]{:S(2)}) collective-permute-start(f16[256,1152]{1,0:T(8,128)(2,1)S(1)} %add_convert_fusion.3), channel_id=1, source_target_pairs={{0,24},{8,0},{16,8},{24,16},{1,25},{9,1},{17,9},{25,17},{2,26},{10... | collective-permute-start | bytes 1769480 | tf_op jit(solution)/shard_map/ppermute | solution.py:25
  71.5 18.2 %collective-permute-start.21 = (f16[256,1152]{1,0:T(8,128)(2,1)S(1)}, f16[256,1152]{1,0:T(8,128)(2,1)S(1)}, u32[]{:S(2)}, u32[]{:S(2)}) collective-permute-start(f16[256,1152]{1,0:T(8,128)(2,1)S(1)} %get-tuple-element.137), channel_id=1, source_target_pairs={{0,8},{8,16},{16,24},{24,0},{1,9},{9,17},{17,25},{25,1},{2,10},{10... | collective-permute-start | bytes 1769480 | tf_op jit(solution)/shard_map/ppermute | solution.py:25
  74.7 15.0 %collective-permute-start.22 = (f16[256,1152]{1,0:T(8,128)(2,1)S(1)}, f16[256,1152]{1,0:T(8,128)(2,1)S(1)}, u32[]{:S(2)}, u32[]{:S(2)}) collective-permute-start(f16[256,1152]{1,0:T(8,128)(2,1)S(1)} %get-tuple-element.138), channel_id=1, source_target_pairs={{0,96},{32,0},{64,32},{96,64},{1,97},{33,1},{65,33},{97,65},{2,98}... | collective-permute-start | bytes 1769480 | tf_op jit(solution)/shard_map/ppermute | solution.py:25
  75.0 14.7 %collective-permute-start.23 = (f16[256,1152]{1,0:T(8,128)(2,1)S(1)}, f16[256,1152]{1,0:T(8,128)(2,1)S(1)}, u32[]{:S(2)}, u32[]{:S(2)}) collective-permute-start(f16[256,1152]{1,0:T(8,128)(2,1)S(1)} %get-tuple-element.139), channel_id=1, source_target_pairs={{0,32},{32,64},{64,96},{96,0},{1,33},{33,65},{65,97},{97,1},{2,34}... | collective-permute-start | bytes 1769480 | tf_op jit(solution)/shard_map/ppermute | solution.py:25
  76.7 1.1 %collective-permute-start.24 = (f32[1,3]{1,0:T(1,128)S(1)}, f32[1,3]{1,0:T(1,128)S(1)}, u32[]{:S(2)}, u32[]{:S(2)}) collective-permute-start(f32[1,3]{1,0:T(1,128)S(1)} %bitcast.4), channel_id=1, source_target_pairs={{0,1},{1,0},{2,3},{3,2},{4,5},{5,4},{6,7},{7,6},{8,9},{9,8},{10,11... | collective-permute-start | bytes 44 | tf_op jit(solution)/shard_map/ppermute | solution.py:25
  77.9 3.5 %collective-permute-start.25 = (f32[1,3]{1,0:T(1,128)S(1)}, f32[1,3]{1,0:T(1,128)S(1)}, u32[]{:S(2)}, u32[]{:S(2)}) collective-permute-start(f32[1,3]{1,0:T(1,128)S(1)} %add.109), channel_id=1, source_target_pairs={{0,2},{2,0},{4,6},{6,4},{1,3},{3,1},{5,7},{7,5},{8,10},{10,8},{12,... | collective-permute-start | bytes 44 | tf_op jit(solution)/shard_map/ppermute | solution.py:25
  81.4 4.8 %collective-permute-start.26 = (f32[1,3]{1,0:T(1,128)S(1)}, f32[1,3]{1,0:T(1,128)S(1)}, u32[]{:S(2)}, u32[]{:S(2)}) collective-permute-start(f32[1,3]{1,0:T(1,128)S(1)} %add.110), channel_id=1, source_target_pairs={{2,4},{4,2},{6,0},{0,6},{3,5},{5,3},{7,1},{1,7},{10,12},{12,10},{1... | collective-permute-start | bytes 44 | tf_op jit(solution)/shard_map/ppermute | solution.py:25
  86.2 3.5 %collective-permute-start.27 = (f32[1,3]{1,0:T(1,128)S(1)}, f32[1,3]{1,0:T(1,128)S(1)}, u32[]{:S(2)}, u32[]{:S(2)}) collective-permute-start(f32[1,3]{1,0:T(1,128)S(1)} %add.111), channel_id=1, source_target_pairs={{0,8},{8,0},{16,24},{24,16},{1,9},{9,1},{17,25},{25,17},{2,10},{10... | collective-permute-start | bytes 44 | tf_op jit(solution)/shard_map/ppermute | solution.py:25
  90.2 16.3 %collective-permute-start.29 = (f16[128,1152]{1,0:T(8,128)(2,1)S(1)}, f16[128,1152]{1,0:T(8,128)(2,1)S(1)}, u32[]{:S(2)}, u32[]{:S(2)}) collective-permute-start(f16[128,1152]{1,0:T(8,128)(2,1)S(1)} %slice_convert_fusion), channel_id=1, source_target_pairs={{2,4},{4,2},{6,0},{0,6},{3,5},{5,3},{7,1},{1,7},{10,12},{12,10},{1... | collective-permute-start | bytes 884744 | tf_op jit(solution)/shard_map/ppermute | solution.py:25
  92.8 13.7 %collective-permute-start.28 = (f16[128,1152]{1,0:T(8,128)(2,1)S(1)}, f16[128,1152]{1,0:T(8,128)(2,1)S(1)}, u32[]{:S(2)}, u32[]{:S(2)}) collective-permute-start(f16[128,1152]{1,0:T(8,128)(2,1)S(1)} %slice_convert_fusion.1), channel_id=1, source_target_pairs={{0,2},{2,0},{4,6},{6,4},{1,3},{3,1},{5,7},{7,5},{8,10},{10,8},{12,... | collective-permute-start | bytes 884744 | tf_op jit(solution)/shard_map/ppermute | solution.py:25
  92.8 4.8 %collective-permute-start.30 = (f32[1,3]{1,0:T(1,128)S(1)}, f32[1,3]{1,0:T(1,128)S(1)}, u32[]{:S(2)}, u32[]{:S(2)}) collective-permute-start(f32[1,3]{1,0:T(1,128)S(1)} %add.112), channel_id=1, source_target_pairs={{8,16},{16,8},{24,0},{0,24},{9,17},{17,9},{25,1},{1,25},{10,18},{1... | collective-permute-start | bytes 44 | tf_op jit(solution)/shard_map/ppermute | solution.py:25
  97.6 3.5 %collective-permute-start.31 = (f32[1,3]{1,0:T(1,128)S(1)}, f32[1,3]{1,0:T(1,128)S(1)}, u32[]{:S(2)}, u32[]{:S(2)}) collective-permute-start(f32[1,3]{1,0:T(1,128)S(1)} %add.119), channel_id=1, source_target_pairs={{0,32},{32,0},{64,96},{96,64},{1,33},{33,1},{65,97},{97,65},{2,34}... | collective-permute-start | bytes 44 | tf_op jit(solution)/shard_map/ppermute | solution.py:25
  101.1 4.8 %collective-permute-start.32 = (f32[1,3]{1,0:T(1,128)S(1)}, f32[1,3]{1,0:T(1,128)S(1)}, u32[]{:S(2)}, u32[]{:S(2)}) collective-permute-start(f32[1,3]{1,0:T(1,128)S(1)} %add.120), channel_id=1, source_target_pairs={{32,64},{64,32},{96,0},{0,96},{33,65},{65,33},{97,1},{1,97},{34,66... | collective-permute-start | bytes 44 | tf_op jit(solution)/shard_map/ppermute | solution.py:25

commit v4 on v3

v4 whole, which is shorter than its diff:
```python
import functools

import jax
import jax.numpy as jnp
from jax import lax
from jax.experimental import pallas as pl
from jax.experimental.pallas import tpu as pltpu
from jax.sharding import Mesh, PartitionSpec as P

EPS = 1e-06
AXES = ("y", "x", "zh", "zl", "c")
Z = ("zh", "zl")
EVEN = [(0, 1), (1, 0), (2, 3), (3, 2)]
ODD = [(1, 2), (2, 1), (3, 0), (0, 3)]
UP = [(i, (i + 1) % 4) for i in range(4)]
DOWN = [(i, (i - 1) % 4) for i in range(4)]
SWAP = [(0, 1), (1, 0)]
SCALE = 4.0
TILE = 256
LOG2E = 1.4426950408889634
LN2 = 0.6931471805599453


def send(value, axis, pairs):
    return lax.ppermute(value, axis, pairs)


def fence(*values):
    return lax.optimization_barrier(values)


def normalize(embedding):
    widened = embedding.astype(jnp.float32)
    inverse = lax.rsqrt(jnp.sum(widened * widened, axis=1, keepdims=True) + EPS)
    return (widened * inverse, inverse)


def projection(total, unit_rows, inverse):
    radial = jnp.sum(total * unit_rows, axis=1, keepdims=True)
    return (total - radial * unit_rows) * inverse


def by_eight(value):
    return jnp.sum(value.reshape(value.shape[0] // 8, 8, value.shape[1]), axis=0)


def pair_tile(scores, factor, offset, diagonal, totals):
    logits = scores * factor + offset
    small = jnp.exp2(-jnp.abs(logits))
    inverse = pltpu.reciprocal(1.0 + small, approx=True)
    gradient = jnp.where(logits >= 0.0, 1.0, small) * inverse
    signed = logits
    if diagonal:
        row = lax.broadcasted_iota(jnp.int32, (TILE, TILE), 0)
        column = lax.broadcasted_iota(jnp.int32, (TILE, TILE), 1)
        matched = (row == column) & (row < TILE // 2)
        signed = jnp.where(matched, -logits, logits)
        gradient = jnp.where(matched, gradient - 1.0, gradient)
    product = small
    while product.shape[0] > 8:
        half = product.shape[0] // 2
        left, right = product[:half], product[half:]
        product = left + right + left * right
    totals[0] += jnp.log1p(product)
    totals[1] += by_eight(jnp.maximum(signed, 0.0))
    totals[2] += by_eight(gradient * scores)
    totals[3] += by_eight(gradient)
    return gradient.astype(jnp.bfloat16)


def block_kernel(n_images, n_texts, n_old, n_before, tiles, diagonal, where, jobs, *refs):
    refs = list(refs)
    take = lambda n: [refs.pop(0) for _ in range(n)]
    scalars = take(1)[0] if tiles else None
    images, texts, old, before = take(n_images), take(n_texts), take(n_old), take(n_before)
    if tiles:
        new, sums = take(2)
        factor = scalars[0] * LOG2E
        offset = scalars[1] * LOG2E
        totals = [jnp.zeros((8, TILE), jnp.float32) for _ in range(4)]
        for t, (i, j) in enumerate(tiles):
            scores = lax.dot_general(
                images[i][...], texts[j][...], (((1,), (1,)), ((), ())), preferred_element_type=jnp.float32
            )
            new[t] = pair_tile(scores, factor, offset, t == diagonal, totals)
        sums[0] = totals[0] + LN2 * totals[1]
        sums[1] = totals[2]
        sums[2] = totals[3]
        old = old + [new]
    for out, row, kind, index, over, base in jobs:
        total = None
        for k in over:
            a, t = where[(index, k) if kind == "image" else (k, index)]
            rows, contract = (texts[k], 1) if kind == "image" else (images[k], 0)
            term = lax.dot_general(
                old[a][t], rows[...], (((contract,), (0,)), ((), ())), preferred_element_type=jnp.float32
            )
            total = term if total is None else total + term
        total = SCALE * total
        place = pl.ds(row * TILE, TILE)
        refs[out][place, :] = total if base is None else total + before[base][place, :]


def block(scalars, images, texts, old, where, tiles=(), diagonal=None, jobs=(), outs=(), before=()):
    vmem = pl.BlockSpec(memory_space=pltpu.VMEM)
    head = [scalars] if tiles else []
    out_shape = [jax.ShapeDtypeStruct((n * TILE, 1152), jnp.float32) for n in outs]
    if tiles:
        out_shape = [
            jax.ShapeDtypeStruct((len(tiles), TILE, TILE), jnp.bfloat16),
            jax.ShapeDtypeStruct((3, 8, TILE), jnp.float32),
        ] + out_shape
    return pl.pallas_call(
        functools.partial(
            block_kernel,
            len(images),
            len(texts),
            len(old),
            len(before),
            tuple(tiles),
            diagonal,
            dict(where),
            tuple(jobs),
        ),
        in_specs=[pl.BlockSpec(memory_space=pltpu.SMEM)] * len(head)
        + [vmem] * (len(images) + len(texts) + len(old) + len(before)),
        out_specs=[vmem] * len(out_shape),
        out_shape=out_shape,
        compiler_params=pltpu.CompilerParams(vmem_limit_bytes=24 * 1024 * 1024),
        cost_estimate=pl.CostEstimate(flops=1, bytes_accessed=1, transcendentals=0),
    )(*head, *images, *texts, *old, *before)


def narrow(value):
    return value.astype(jnp.float16)


def wide(value):
    return value.astype(jnp.float32)


def per_device(picture_embedding, caption_embedding, logarithmic_scale_factor, offset_shift):
    rows = picture_embedding.shape[0]
    example_number = rows * 128
    (both,) = fence(jnp.concatenate([picture_embedding, caption_embedding], axis=0))
    unit32, inverse = normalize(both)
    unit = unit32.astype(jnp.bfloat16)
    image, text = unit[:rows], unit[rows:]
    temperature = jnp.exp(logarithmic_scale_factor[0])
    scalars = jnp.stack([temperature, offset_shift[0]])

    image_z, text_z = fence(send(image, Z, EVEN), send(text, Z, ODD))
    i_own = jnp.concatenate([image, image_z], axis=0)
    t_own = jnp.concatenate([text, text_z], axis=0)

    scalars, i_low, i_high, t_low, t_high, text_s, text_zs = fence(
        scalars,
        send(i_own, "x", UP),
        send(i_own, "x", DOWN),
        send(t_own, "y", UP),
        send(t_own, "y", DOWN),
        send(text, "c", SWAP),
        send(text_z, "c", SWAP),
    )
    s_own = jnp.concatenate([text_s, text_zs], axis=0)

    far = [
        send(i_low[:rows], "x", UP),
        send(i_high[rows:], "x", DOWN),
        send(t_low[:rows], "y", UP),
        send(t_high[rows:], "y", DOWN),
    ]
    s_near = send(jnp.concatenate([t_low, t_high], axis=0), "c", SWAP)
    near_images = [i_own, i_low, i_high]
    near_texts = [t_own, t_low, t_high, s_own]
    where = {}

    def place(number, tiles):
        where.update({p: (number, t) for t, p in enumerate(tiles)})
        return tiles

    tiles_a = place(0, [(i, j) for j in range(4) for i in range(3)])
    weights_a, sums_a = block(scalars, near_images, near_texts, [], where, tiles_a, 0)
    weights_a, s_near = fence(weights_a, s_near)
    s_low, s_high = s_near[: 2 * rows], s_near[2 * rows :]
    near_texts = [t_own, t_low, t_high, s_own, s_low, s_high]
    tiles_b = place(1, [(i, j) for j in (4, 5) for i in range(3)])
    shared = [(0, n, "text", j, (0, 1, 2), None) for n, j in enumerate((4, 5, 3))]
    weights_b, sums_b, ps_near = block(
        scalars, near_images, near_texts, [weights_a], where, tiles_b, None, shared, [3]
    )
    *far, weights_a, weights_b, ps_near = fence(*far, weights_a, weights_b, ps_near)
    i_far = jnp.concatenate(far[:2], axis=0)
    t_far = jnp.concatenate(far[2:], axis=0)
    s_far = send(t_far, "c", SWAP)

    images = [i_own, i_low, i_high, i_far]
    texts = [t_own, t_low, t_high, s_own, s_low, s_high, t_far]
    weights = [weights_a, weights_b]
    tiles_c = place(2, [(3, j) for j in range(7)] + [(i, 6) for i in range(3)])
    weights_c, sums_c, pi_far, pt_far = block(
        scalars,
        images,
        texts,
        weights,
        where,
        tiles_c,
        None,
        [(0, 0, "image", 3, tuple(range(7)), None), (1, 0, "text", 6, (0, 1, 2, 3), None)],
        [1, 1],
    )
    weights_c, s_far = fence(weights_c, s_far)
    texts = texts + [s_far]
    tiles_d = place(3, [(i, 7) for i in range(4)])
    weights_d, sums_d, ps_far = block(
        scalars, images, texts, weights + [weights_c], where, tiles_d, None, [(0, 0, "text", 7, (0, 1, 2, 3), None)], [1]
    )
    weights = [weights_a, weights_b, weights_c, weights_d]

    *weights, ps_far = fence(*weights, narrow(ps_far))
    ps_far = send(ps_far, "c", SWAP)
    value = jnp.sum(sums_a + sums_b + sums_c + sums_d, axis=(1, 2)).reshape(1, 3)
    pi_far, ps_near = block(
        None,
        images,
        texts,
        weights,
        where,
        jobs=[(0, 0, "image", 3, (7,), 0)] + [(1, n, "text", j, (3,), 1) for n, j in enumerate((4, 5, 3))],
        outs=[1, 3],
        before=[pi_far, ps_near],
    )
    ps_near = narrow(ps_near)
    pi_far = narrow(pi_far)
    pt_far = narrow(pt_far + wide(ps_far))
    pi_far, pt_far, ps_near, value, *weights = fence(pi_far, pt_far, ps_near, value, *weights)
    back = [
        send(pi_far[:rows], "x", DOWN),
        send(pi_far[rows:], "x", UP),
        send(pt_far[:rows], "y", DOWN),
        send(pt_far[rows:], "y", UP),
    ]
    ps_near = send(ps_near, "c", SWAP)
    pi_low, pi_high, pi_own, pt_low, pt_high, pt_own = block(
        None,
        images,
        texts,
        weights,
        where,
        jobs=[(n, 0, "image", i, tuple(range(8)), None) for n, i in enumerate((1, 2, 0))]
        + [(n + 3, 0, "text", j, (0, 1, 2, 3), None) for n, j in enumerate((1, 2, 0))],
        outs=[1] * 6,
    )
    *back, ps_near, pi_low, pi_high, pi_own, pt_low, pt_high, pt_own = fence(
        *back, ps_near, pi_low, pi_high, pi_own, pt_low, pt_high, pt_own
    )

    first, second = ((0, rows), (0, 0)), ((rows, 0), (0, 0))
    near = [
        narrow(pi_low + jnp.pad(wide(back[0]), first)),
        narrow(pi_high + jnp.pad(wide(back[1]), second)),
        narrow(pt_low + wide(ps_near[: 2 * rows]) + jnp.pad(wide(back[2]), first)),
        narrow(pt_high + wide(ps_near[2 * rows : 4 * rows]) + jnp.pad(wide(back[3]), second)),
    ]
    *near, value = fence(*near, value)
    near = [
        send(near[0], "x", DOWN),
        send(near[1], "x", UP),
        send(near[2], "y", DOWN),
        send(near[3], "y", UP),
    ]
    for axis, pairs in (("c", SWAP), (Z, EVEN), (Z, ODD), ("x", EVEN)):
        value = value + send(value, axis, pairs)
    pt_own = pt_own + wide(ps_near[4 * rows :])
    *near, pi_own, pt_own, value = fence(*near, pi_own, pt_own, value)
    pi_own = pi_own + wide(near[0]) + wide(near[1])
    pt_own = pt_own + wide(near[2]) + wide(near[3])

    last = [narrow(pi_own[rows:]), narrow(pt_own[rows:])]
    *last, value = fence(*last, value)
    last = [send(last[0], Z, EVEN), send(last[1], Z, ODD)]
    for axis, pairs in (("x", ODD), ("y", EVEN)):
        value = value + send(value, axis, pairs)
    *last, value = fence(*last, value)
    value = value + send(value, "y", ODD)
    objective_results = value[0] * jnp.stack([jnp.float32(1.0), temperature, jnp.float32(1.0)]) / example_number
    scale = temperature / SCALE
    image_gradient = projection(scale * (pi_own[:rows] + wide(last[0])), unit32[:rows], inverse[:rows])
    text_grad = projection(scale * (pt_own[:rows] + wide(last[1])), unit32[rows:], inverse[rows:])
    return (image_gradient, text_grad, objective_results)


def solution(mesh):
    mesh = Mesh(mesh.devices.reshape(4, 4, 2, 2, 2), AXES)
    return jax.shard_map(
        per_device,
        mesh=mesh,
        in_specs=(P(AXES, None), P(AXES, None), P(), P()),
        out_specs=(P(AXES, None), P(AXES, None), P()),
        check_vma=False,
    )
```

time: 108 us -> 107 us (level)
  starting transfers between devices: 35.3 us -> 33.2 us
  waiting for transfers between devices: 40.8 us -> 42.5 us
  Pallas kernels: 23.3 us -> 22 us
    ppermute x33, starting transfers between devices: 35.3 us -> 33.2 us  [send(): return lax.ppermute(value, axis, pairs)]
    ppermute x33, waiting for transfers between devices: 40.8 us -> 42.5 us  [send(): return lax.ppermute(value, axis, pairs)]
    pallas_call x9 -> x6, Pallas kernels: 23.3 us -> 22 us  [block(): pl.pallas_call(functools.partial(block_kernel, len(images), len(texts), l...]
  transfers between devices with their start and end apart: 33 -> 33, of which waited for: 15 -> 17; matrix products, arithmetic and copies ran while one was open for 2% -> 2% of each run, Pallas kernels for 19% -> 18%
where the time goes in v4:
time: 107 us
  waiting for transfers between devices  42.5 us (40%)
  starting transfers between devices  33.2 us (31%)
  Pallas kernels  22 us (21%)
  other arithmetic  5.91 us (6%)
  between operations  2.3 us (2%)
    ppermute x33, waiting for transfers between devices, send(): return lax.ppermute(value, axis, pairs)  42.5 us
    ppermute x33, starting transfers between devices, send(): return lax.ppermute(value, axis, pairs)  33.2 us
    pallas_call x6, Pallas kernels, block(): pl.pallas_call(functools.partial(block_kernel, len(images), len(texts), l...  22 us
  transfers between devices with their start and end apart: 33, of which 17 were waited for; matrix products, arithmetic and copies ran while one was open for 2% of the time, Pallas kernels for 18%

profile of v4, /device:TPU:6, one launch (start us, length us, event | category | flops | bytes accessed | tf_op | source)
XLA Modules:
  0.0 106.6 jit_solution(4727897208280708401)
XLA Ops:
  0.6 1.1 %pad_maximum_fusion.1 = bf16[256,1152]{1,0:T(8,128)(2,1)S(1)} fusion(bf16[128,1152]{1,0:T(8,128)(2,1)} %param.5, bf16[128,1152]{1,0:T(8,128)(2,1)} %param.4), kind=kLoop, calls=%fused_computation.18 | loop fusion | flops 1179648 | bytes 1179648 | tf_op jit(solution)/shard_map/concatenate | solution.py:145
  1.7 0.2 fusion
  1.9 0.2 fusion.4
  2.2 4.1 %collective-permute-start.1 = (bf16[128,1152]{1,0:T(8,128)(2,1)S(1)}, bf16[128,1152]{1,0:T(8,128)(2,1)S(1)}, u32[]{:S(2)}, u32[]{:S(2)}) collective-permute-start(bf16[128,1152]{1,0:T(8,128)(2,1)S(1)} %get-tuple-element.182), channel_id=1, source_target_pairs={{2,4},{4,2},{6,0},{0,6},{3,5},{5,3},{7,1},{1,7},{10,12},{12,10},{1... | collective-permute-start | bytes 884744 | tf_op jit(solution)/shard_map/ppermute | solution.py:25
  6.3 7.0 %collective-permute-done.1 = bf16[128,1152]{1,0:T(8,128)(2,1)S(1)} collective-permute-done((bf16[128,1152]{1,0:T(8,128)(2,1)S(1)}, bf16[128,1152]{1,0:T(8,128)(2,1)S(1)}, u32[]{:S(2)}, u32[]{:S(2)}) %collective-permute-start.1) | collective-permute-done | bytes 294944 | tf_op jit(solution)/shard_map/ppermute | solution.py:25
  13.3 1.5 %collective-permute-done = bf16[128,1152]{1,0:T(8,128)(2,1)S(1)} collective-permute-done((bf16[128,1152]{1,0:T(8,128)(2,1)S(1)}, bf16[128,1152]{1,0:T(8,128)(2,1)S(1)}, u32[]{:S(2)}, u32[]{:S(2)}) %collective-permute-start) | collective-permute-done | bytes 294944 | tf_op jit(solution)/shard_map/ppermute | solution.py:25
  14.8 1.6 %collective-permute-start.4 = (bf16[256,1152]{1,0:T(8,128)(2,1)S(1)}, bf16[256,1152]{1,0:T(8,128)(2,1)S(1)}, u32[]{:S(2)}, u32[]{:S(2)}) collective-permute-start(bf16[256,1152]{1,0:T(8,128)(2,1)S(1)} %pad_maximum_fusion.3.refs_4_.refs_5_), channel_id=1, source_target_pairs={{0,32},{32,64},{64,96},{96,0},{1,33},{33,65},{65,97},{97,1},{2,34}... | collective-permute-start | bytes 1769480 | tf_op jit(solution)/shard_map/ppermute | solution.py:25
  16.5 1.7 %collective-permute-start.5 = (bf16[256,1152]{1,0:T(8,128)(2,1)S(1)}, bf16[256,1152]{1,0:T(8,128)(2,1)S(1)}, u32[]{:S(2)}, u32[]{:S(2)}) collective-permute-start(bf16[256,1152]{1,0:T(8,128)(2,1)S(1)} %pad_maximum_fusion.3.refs_4_.refs_5_), channel_id=1, source_target_pairs={{0,96},{32,0},{64,32},{96,64},{1,97},{33,1},{65,33},{97,65},{2,98}... | collective-permute-start | bytes 1769480 | tf_op jit(solution)/shard_map/ppermute | solution.py:25
  18.2 0.5 collective-permute-start.2
  18.7 1.5 %collective-permute-start.3 = (bf16[256,1152]{1,0:T(8,128)(2,1)S(1)}, bf16[256,1152]{1,0:T(8,128)(2,1)S(1)}, u32[]{:S(2)}, u32[]{:S(2)}) collective-permute-start(bf16[256,1152]{1,0:T(8,128)(2,1)S(1)} %pad_maximum_fusion.2.refs_1_.refs_0_), channel_id=1, source_target_pairs={{0,24},{8,0},{16,8},{24,16},{1,25},{9,1},{17,9},{25,17},{2,26},{10... | collective-permute-start | bytes 1769480 | tf_op jit(solution)/shard_map/ppermute | solution.py:25
  21.7 0.2 collective-permute-done.7
  21.9 8.2 %collective-permute-done.4.refs_5_.refs_6_ = bf16[256,1152]{1,0:T(8,128)(2,1)S(1)} collective-permute-done((bf16[256,1152]{1,0:T(8,128)(2,1)S(1)}, bf16[256,1152]{1,0:T(8,128)(2,1)S(1)}, u32[]{:S(2)}, u32[]{:S(2)}) %collective-permute-start.4) | collective-permute-done | bytes 589856 | tf_op jit(solution)/shard_map/ppermute | solution.py:25
  30.1 1.6 %collective-permute-done.2.refs_2_.refs_1_ = bf16[256,1152]{1,0:T(8,128)(2,1)S(1)} collective-permute-done((bf16[256,1152]{1,0:T(8,128)(2,1)S(1)}, bf16[256,1152]{1,0:T(8,128)(2,1)S(1)}, u32[]{:S(2)}, u32[]{:S(2)}) %collective-permute-start.2) | collective-permute-done | bytes 589856 | tf_op jit(solution)/shard_map/ppermute | solution.py:25
  31.7 1.4 %collective-permute-done.3.refs_3_.refs_2_ = bf16[256,1152]{1,0:T(8,128)(2,1)S(1)} collective-permute-done((bf16[256,1152]{1,0:T(8,128)(2,1)S(1)}, bf16[256,1152]{1,0:T(8,128)(2,1)S(1)}, u32[]{:S(2)}, u32[]{:S(2)}) %collective-permute-start.3) | collective-permute-done | bytes 589856 | tf_op jit(solution)/shard_map/ppermute | solution.py:25
  33.4 0.3 collective-permute-start.10
  33.7 3.0 %collective-permute-start.11 = (bf16[128,1152]{1,0:T(8,128)(2,1)S(1)}, bf16[128,1152]{1,0:T(8,128)(2,1)S(1)}, u32[]{:S(2)}, u32[]{:S(2)}) collective-permute-start(bf16[128,1152]{1,0:T(8,128)(2,1)S(1)} %slice.78), channel_id=1, source_target_pairs={{0,96},{32,0},{64,32},{96,64},{1,97},{33,1},{65,33},{97,65},{2,98}... | collective-permute-start | bytes 884744 | tf_op jit(solution)/shard_map/ppermute | solution.py:25
  36.7 0.4 collective-permute-start.8
  37.1 1.8 %collective-permute-start.9 = (bf16[128,1152]{1,0:T(8,128)(2,1)S(1)}, bf16[128,1152]{1,0:T(8,128)(2,1)S(1)}, u32[]{:S(2)}, u32[]{:S(2)}) collective-permute-start(bf16[128,1152]{1,0:T(8,128)(2,1)S(1)} %slice.76), channel_id=1, source_target_pairs={{0,24},{8,0},{16,8},{24,16},{1,25},{9,1},{17,9},{25,17},{2,26},{10... | collective-permute-start | bytes 884744 | tf_op jit(solution)/shard_map/ppermute | solution.py:25
  39.0 3.9 %shard_map.67 = (bf16[12,256,256]{2,1,0:T(8,128)(2,1)S(1)}, f32[3,8,256]{2,1,0:T(8,128)S(1)}) custom-call(f32[2]{0:T(128)S(1)} %pad_maximum_fusion.4.refs_0_, bf16[256,1152]{1,0:T(8,128)(2,1)S(1)} %pad_maximum_fusion.2.refs_1_.refs_0_, bf16[256,1152]{1,0:T(8,128)(2,1)S(1)} %collective-permute-done.2.refs_2_.refs_1_, ...), custom_call_target="tpu_custom_call" | custom-call | flops 1 | bytes 1 | tf_op jit(solution)/shard_map/pallas_call | solution.py:113
  42.9 0.1 fusion.5
  43.0 3.7 %shard_map.68 = (bf16[6,256,256]{2,1,0:T(8,128)(2,1)S(1)}, f32[3,8,256]{2,1,0:T(8,128)S(1)}, f32[768,1152]{1,0:T(8,128)S(1)}) custom-call(f32[2]{0:T(128)S(1)} %pad_maximum_fusion.4.refs_0_, bf16[256,1152]{1,0:T(8,128)(2,1)S(1)} %pad_maximum_fusion.2.refs_1_.refs_0_, bf16[256,1152]{1,0:T(8,128)(2,1)S(1)} %collective-permute-done.2.refs_2_.refs_1_, ...), custom_call_target="tpu_custom_call" | custom-call | flops 1 | bytes 1 | tf_op jit(solution)/shard_map/pallas_call | solution.py:113
  46.7 0.2 collective-permute-done.9
  47.0 0.3 collective-permute-start.13
  47.4 4.7 %shard_map.69 = (bf16[10,256,256]{2,1,0:T(8,128)(2,1)S(1)}, f32[3,8,256]{2,1,0:T(8,128)S(1)}, f32[256,1152]{1,0:T(8,128)S(1)}, f32[256,1152]{1,0:T(8,128)S(1)}) custom-call(f32[2]{0:T(128)S(1)} %pad_maximum_fusion.4.refs_0_, bf16[256,1152]{1,0:T(8,128)(2,1)S(1)} %pad_maximum_fusion.2.refs_1_.refs_0_, ...), custom_call_target="tpu_custom_call" | custom-call | flops 1 | bytes 1 | tf_op jit(solution)/shard_map/pallas_call | solution.py:113
  52.1 2.5 %shard_map.70 = (bf16[4,256,256]{2,1,0:T(8,128)(2,1)S(1)}, f32[3,8,256]{2,1,0:T(8,128)S(1)}, f32[256,1152]{1,0:T(8,128)S(1)}) custom-call(f32[2]{0:T(128)S(1)} %pad_maximum_fusion.4.refs_0_, bf16[256,1152]{1,0:T(8,128)(2,1)S(1)} %pad_maximum_fusion.2.refs_1_.refs_0_, bf16[256,1152]{1,0:T(8,128)(2,1)S(1)} %collective-permute-done.2.refs_2_.refs_1_, ...), custom_call_target="tpu_custom_call" | custom-call | flops 1 | bytes 1 | tf_op jit(solution)/shard_map/pallas_call | solution.py:113
  54.7 0.6 collective-permute-start.14
  55.2 0.9 shard_map.71
  56.2 0.2 convert_element_type.78
  56.4 0.1 add_reduce_fusion
  56.6 0.3 collective-permute-done.14
  56.9 0.2 add_convert_fusion.4
  57.1 0.5 collective-permute-start.19
  57.5 0.1 fusion.7
  57.6 0.6 collective-permute-start.15
  58.2 2.7 %collective-permute-start.16 = (f16[128,1152]{1,0:T(8,128)(2,1)S(1)}, f16[128,1152]{1,0:T(8,128)(2,1)S(1)}, u32[]{:S(2)}, u32[]{:S(2)}) collective-permute-start(f16[128,1152]{1,0:T(8,128)(2,1)S(1)} %get-tuple-element.180), channel_id=1, source_target_pairs={{0,8},{8,16},{16,24},{24,0},{1,9},{9,17},{17,25},{25,1},{2,10},{10... | collective-permute-start | bytes 884744 | tf_op jit(solution)/shard_map/ppermute | solution.py:25
  60.9 0.1 fusion.6
  61.0 0.5 collective-permute-start.17
  61.5 1.6 %collective-permute-start.18 = (f16[128,1152]{1,0:T(8,128)(2,1)S(1)}, f16[128,1152]{1,0:T(8,128)(2,1)S(1)}, u32[]{:S(2)}, u32[]{:S(2)}) collective-permute-start(f16[128,1152]{1,0:T(8,128)(2,1)S(1)} %get-tuple-element.178), channel_id=1, source_target_pairs={{0,32},{32,64},{64,96},{96,0},{1,33},{33,65},{65,97},{97,1},{2,34}... | collective-permute-start | bytes 884744 | tf_op jit(solution)/shard_map/ppermute | solution.py:25
  63.1 6.3 %shard_map.72 = (f32[256,1152]{1,0:T(8,128)S(1)}, f32[256,1152]{1,0:T(8,128)S(1)}, f32[256,1152]{1,0:T(8,128)S(1)}, f32[256,1152]{1,0:T(8,128)S(1)}, f32[256,1152]{1,0:T(8,128)S(1)}, /*index=5*/f32[256,1152]{1,0:T(8,128)S(1)}) custom-call(bf16[256,1152]{1,0:T(8,128)(2,1)S(1)} %pad_maximum_fusion.2.refs_1_.refs_0_, ...), custom_call_target="tpu_custom_call" | custom-call | flops 1 | bytes 1 | tf_op jit(solution)/shard_map/pallas_call | solution.py:113
  69.5 0.1 collective-permute-done.17
  69.6 1.5 %collective-permute-done.18 = f16[128,1152]{1,0:T(8,128)(2,1)S(1)} collective-permute-done((f16[128,1152]{1,0:T(8,128)(2,1)S(1)}, f16[128,1152]{1,0:T(8,128)(2,1)S(1)}, u32[]{:S(2)}, u32[]{:S(2)}) %collective-permute-start.18) | collective-permute-done | bytes 294944 | tf_op jit(solution)/shard_map/ppermute | solution.py:25
  71.1 0.1 add_convert_fusion.3
  71.2 0.7 convert_add_fusion.2
  72.1 3.2 %collective-permute-start.21 = (f16[256,1152]{1,0:T(8,128)(2,1)S(1)}, f16[256,1152]{1,0:T(8,128)(2,1)S(1)}, u32[]{:S(2)}, u32[]{:S(2)}) collective-permute-start(f16[256,1152]{1,0:T(8,128)(2,1)S(1)} %get-tuple-element.148), channel_id=1, source_target_pairs={{0,8},{8,16},{16,24},{24,0},{1,9},{9,17},{17,25},{25,1},{2,10},{10... | collective-permute-start | bytes 1769480 | tf_op jit(solution)/shard_map/ppermute | solution.py:25
  75.3 0.1 collective-permute-start.22
  75.4 1.9 %collective-permute-start.23 = (f16[256,1152]{1,0:T(8,128)(2,1)S(1)}, f16[256,1152]{1,0:T(8,128)(2,1)S(1)}, u32[]{:S(2)}, u32[]{:S(2)}) collective-permute-start(f16[256,1152]{1,0:T(8,128)(2,1)S(1)} %get-tuple-element.150), channel_id=1, source_target_pairs={{0,32},{32,64},{64,96},{96,0},{1,33},{33,65},{65,97},{97,1},{2,34}... | collective-permute-start | bytes 1769480 | tf_op jit(solution)/shard_map/ppermute | solution.py:25
  77.3 1.1 %collective-permute-done.24 = f32[1,3]{1,0:T(1,128)S(1)} collective-permute-done((f32[1,3]{1,0:T(1,128)S(1)}, f32[1,3]{1,0:T(1,128)S(1)}, u32[]{:S(2)}, u32[]{:S(2)}) %collective-permute-start.24) | collective-permute-done | bytes 44 | tf_op jit(solution)/shard_map/ppermute | solution.py:25
  78.4 0.6 collective-permute-start.25
  79.0 3.0 %collective-permute-done.25 = f32[1,3]{1,0:T(1,128)S(1)} collective-permute-done((f32[1,3]{1,0:T(1,128)S(1)}, f32[1,3]{1,0:T(1,128)S(1)}, u32[]{:S(2)}, u32[]{:S(2)}) %collective-permute-start.25) | collective-permute-done | bytes 44 | tf_op jit(solution)/shard_map/ppermute | solution.py:25
  82.0 1.8 %collective-permute-start.26 = (f32[1,3]{1,0:T(1,128)S(1)}, f32[1,3]{1,0:T(1,128)S(1)}, u32[]{:S(2)}, u32[]{:S(2)}) collective-permute-start(f32[1,3]{1,0:T(1,128)S(1)} %add.110), channel_id=1, source_target_pairs={{2,4},{4,2},{6,0},{0,6},{3,5},{5,3},{7,1},{1,7},{10,12},{12,10},{1... | collective-permute-start | bytes 44 | tf_op jit(solution)/shard_map/ppermute | solution.py:25
  83.8 3.0 %collective-permute-done.26 = f32[1,3]{1,0:T(1,128)S(1)} collective-permute-done((f32[1,3]{1,0:T(1,128)S(1)}, f32[1,3]{1,0:T(1,128)S(1)}, u32[]{:S(2)}, u32[]{:S(2)}) %collective-permute-start.26) | collective-permute-done | bytes 44 | tf_op jit(solution)/shard_map/ppermute | solution.py:25
  86.7 3.5 %collective-permute-done.27 = f32[1,3]{1,0:T(1,128)S(1)} collective-permute-done((f32[1,3]{1,0:T(1,128)S(1)}, f32[1,3]{1,0:T(1,128)S(1)}, u32[]{:S(2)}, u32[]{:S(2)}) %collective-permute-start.27) | collective-permute-done | bytes 44 | tf_op jit(solution)/shard_map/ppermute | solution.py:25
  90.3 0.2 convert_add_fusion
  90.6 0.2 convert_add_fusion.1
  90.8 0.5 collective-permute-start.28
  91.3 1.5 %collective-permute-start.29 = (f16[128,1152]{1,0:T(8,128)(2,1)S(1)}, f16[128,1152]{1,0:T(8,128)(2,1)S(1)}, u32[]{:S(2)}, u32[]{:S(2)}) collective-permute-start(f16[128,1152]{1,0:T(8,128)(2,1)S(1)} %slice_convert_fusion), channel_id=1, source_target_pairs={{2,4},{4,2},{6,0},{0,6},{3,5},{5,3},{7,1},{1,7},{10,12},{12,10},{1... | collective-permute-start | bytes 884744 | tf_op jit(solution)/shard_map/ppermute | solution.py:25
  92.9 4.7 %collective-permute-done.30 = f32[1,3]{1,0:T(1,128)S(1)} collective-permute-done((f32[1,3]{1,0:T(1,128)S(1)}, f32[1,3]{1,0:T(1,128)S(1)}, u32[]{:S(2)}, u32[]{:S(2)}) %collective-permute-start.30) | collective-permute-done | bytes 44 | tf_op jit(solution)/shard_map/ppermute | solution.py:25
  97.6 0.2 collective-permute-start.31
  97.8 3.3 %collective-permute-done.31 = f32[1,3]{1,0:T(1,128)S(1)} collective-permute-done((f32[1,3]{1,0:T(1,128)S(1)}, f32[1,3]{1,0:T(1,128)S(1)}, u32[]{:S(2)}, u32[]{:S(2)}) %collective-permute-start.31) | collective-permute-done | bytes 44 | tf_op jit(solution)/shard_map/ppermute | solution.py:25
  101.1 1.4 %collective-permute-start.32 = (f32[1,3]{1,0:T(1,128)S(1)}, f32[1,3]{1,0:T(1,128)S(1)}, u32[]{:S(2)}, u32[]{:S(2)}) collective-permute-start(f32[1,3]{1,0:T(1,128)S(1)} %add.118), channel_id=1, source_target_pairs={{32,64},{64,32},{96,0},{0,96},{33,65},{65,33},{97,1},{1,97},{34,66... | collective-permute-start | bytes 44 | tf_op jit(solution)/shard_map/ppermute | solution.py:25
  102.6 0.3 multiply_reduce_fusion
  102.9 1.3 %subtract_multiply_fusion = (f32[128,1152]{1,0:T(8,128)}, f32[128,1152]{1,0:T(8,128)}) fusion(f32[256,1152]{1,0:T(8,128)S(1)} %get-tuple-element.177, f16[128,1152]{1,0:T(8,128)(2,1)S(1)} %collective-permute-done.29, f32[256,1152]{1,0:T(8,128)S(1)} %convert_add_fusion, f32[128]{0:T(128)S(1)} %get-tuple-element.184, f32[128]{0:T(128)S(1)} %get-tuple-element.167, ...), kind=kLoop, calls=%fused_computation.21 | loop fusion | flops 1769472 | bytes 4130820 | tf_op jit(solution)/shard_map/mul | solution.py:40
  104.1 1.8 %collective-permute-done.32 = f32[1,3]{1,0:T(1,128)S(1)} collective-permute-done((f32[1,3]{1,0:T(1,128)S(1)}, f32[1,3]{1,0:T(1,128)S(1)}, u32[]{:S(2)}, u32[]{:S(2)}) %collective-permute-start.32) | collective-permute-done | bytes 44 | tf_op jit(solution)/shard_map/ppermute | solution.py:25
  106.0 0.6 fusion.3
  (51 shorter events, 1.1 us)
Async XLA Ops:
  2.2 11.1 %collective-permute-start.1 = (bf16[128,1152]{1,0:T(8,128)(2,1)S(1)}, bf16[128,1152]{1,0:T(8,128)(2,1)S(1)}, u32[]{:S(2)}, u32[]{:S(2)}) collective-permute-start(bf16[128,1152]{1,0:T(8,128)(2,1)S(1)} %get-tuple-element.182), channel_id=1, source_target_pairs={{2,4},{4,2},{6,0},{0,6},{3,5},{5,3},{7,1},{1,7},{10,12},{12,10},{1... | collective-permute-start | bytes 884744 | tf_op jit(solution)/shard_map/ppermute | solution.py:25
  6.3 8.5 %collective-permute-start = (bf16[128,1152]{1,0:T(8,128)(2,1)S(1)}, bf16[128,1152]{1,0:T(8,128)(2,1)S(1)}, u32[]{:S(2)}, u32[]{:S(2)}) collective-permute-start(bf16[128,1152]{1,0:T(8,128)(2,1)S(1)} %get-tuple-element.183), channel_id=1, source_target_pairs={{0,2},{2,0},{4,6},{6,4},{1,3},{3,1},{5,7},{7,5},{8,10},{10,8},{12,... | collective-permute-start | bytes 884744 | tf_op jit(solution)/shard_map/ppermute | solution.py:25
  6.3 14.0 %collective-permute-start.6 = (bf16[128,1152]{1,0:T(8,128)(2,1)S(1)}, bf16[128,1152]{1,0:T(8,128)(2,1)S(1)}, u32[]{:S(2)}, u32[]{:S(2)}) collective-permute-start(bf16[128,1152]{1,0:T(8,128)(2,1)S(1)} %get-tuple-element.182), channel_id=1, source_target_pairs={{0,1},{1,0},{2,3},{3,2},{4,5},{5,4},{6,7},{7,6},{8,9},{9,8},{10,11... | collective-permute-start | bytes 884744 | tf_op jit(solution)/shard_map/ppermute | solution.py:25
  14.8 15.2 %collective-permute-start.4 = (bf16[256,1152]{1,0:T(8,128)(2,1)S(1)}, bf16[256,1152]{1,0:T(8,128)(2,1)S(1)}, u32[]{:S(2)}, u32[]{:S(2)}) collective-permute-start(bf16[256,1152]{1,0:T(8,128)(2,1)S(1)} %pad_maximum_fusion.3.refs_4_.refs_5_), channel_id=1, source_target_pairs={{0,32},{32,64},{64,96},{96,0},{1,33},{33,65},{65,97},{97,1},{2,34}... | collective-permute-start | bytes 1769480 | tf_op jit(solution)/shard_map/ppermute | solution.py:25
  16.5 13.6 %collective-permute-start.5 = (bf16[256,1152]{1,0:T(8,128)(2,1)S(1)}, bf16[256,1152]{1,0:T(8,128)(2,1)S(1)}, u32[]{:S(2)}, u32[]{:S(2)}) collective-permute-start(bf16[256,1152]{1,0:T(8,128)(2,1)S(1)} %pad_maximum_fusion.3.refs_4_.refs_5_), channel_id=1, source_target_pairs={{0,96},{32,0},{64,32},{96,64},{1,97},{33,1},{65,33},{97,65},{2,98}... | collective-permute-start | bytes 1769480 | tf_op jit(solution)/shard_map/ppermute | solution.py:25
  18.2 13.5 %collective-permute-start.2 = (bf16[256,1152]{1,0:T(8,128)(2,1)S(1)}, bf16[256,1152]{1,0:T(8,128)(2,1)S(1)}, u32[]{:S(2)}, u32[]{:S(2)}) collective-permute-start(bf16[256,1152]{1,0:T(8,128)(2,1)S(1)} %pad_maximum_fusion.2.refs_1_.refs_0_), channel_id=1, source_target_pairs={{0,8},{8,16},{16,24},{24,0},{1,9},{9,17},{17,25},{25,1},{2,10},{10... | collective-permute-start | bytes 1769480 | tf_op jit(solution)/shard_map/ppermute | solution.py:25
  18.7 14.4 %collective-permute-start.3 = (bf16[256,1152]{1,0:T(8,128)(2,1)S(1)}, bf16[256,1152]{1,0:T(8,128)(2,1)S(1)}, u32[]{:S(2)}, u32[]{:S(2)}) collective-permute-start(bf16[256,1152]{1,0:T(8,128)(2,1)S(1)} %pad_maximum_fusion.2.refs_1_.refs_0_), channel_id=1, source_target_pairs={{0,24},{8,0},{16,8},{24,16},{1,25},{9,1},{17,9},{25,17},{2,26},{10... | collective-permute-start | bytes 1769480 | tf_op jit(solution)/shard_map/ppermute | solution.py:25
  20.3 1.6 %collective-permute-start.7 = (bf16[128,1152]{1,0:T(8,128)(2,1)S(1)}, bf16[128,1152]{1,0:T(8,128)(2,1)S(1)}, u32[]{:S(2)}, u32[]{:S(2)}) collective-permute-start(bf16[128,1152]{1,0:T(8,128)(2,1)S(1)} %collective-permute-done.1), channel_id=1, source_target_pairs={{0,1},{1,0},{2,3},{3,2},{4,5},{5,4},{6,7},{7,6},{8,9},{9,8},{10,11... | collective-permute-start | bytes 884744 | tf_op jit(solution)/shard_map/ppermute | solution.py:25
  33.2 9.6 %collective-permute-start.12 = (bf16[512,1152]{1,0:T(8,128)(2,1)S(1)}, bf16[512,1152]{1,0:T(8,128)(2,1)S(1)}, u32[]{:S(2)}, u32[]{:S(2)}) collective-permute-start(bf16[512,1152]{1,0:T(8,128)(2,1)S(1)} %pad_maximum_fusion), channel_id=1, source_target_pairs={{0,1},{1,0},{2,3},{3,2},{4,5},{5,4},{6,7},{7,6},{8,9},{9,8},{10,11... | collective-permute-start | bytes 3538952 | tf_op jit(solution)/shard_map/ppermute | solution.py:25
  33.4 13.3 %collective-permute-start.10 = (bf16[128,1152]{1,0:T(8,128)(2,1)S(1)}, bf16[128,1152]{1,0:T(8,128)(2,1)S(1)}, u32[]{:S(2)}, u32[]{:S(2)}) collective-permute-start(bf16[128,1152]{1,0:T(8,128)(2,1)S(1)} %slice.77), channel_id=1, source_target_pairs={{0,32},{32,64},{64,96},{96,0},{1,33},{33,65},{65,97},{97,1},{2,34}... | collective-permute-start | bytes 884744 | tf_op jit(solution)/shard_map/ppermute | solution.py:25
  33.7 13.0 %collective-permute-start.11 = (bf16[128,1152]{1,0:T(8,128)(2,1)S(1)}, bf16[128,1152]{1,0:T(8,128)(2,1)S(1)}, u32[]{:S(2)}, u32[]{:S(2)}) collective-permute-start(bf16[128,1152]{1,0:T(8,128)(2,1)S(1)} %slice.78), channel_id=1, source_target_pairs={{0,96},{32,0},{64,32},{96,64},{1,97},{33,1},{65,33},{97,65},{2,98}... | collective-permute-start | bytes 884744 | tf_op jit(solution)/shard_map/ppermute | solution.py:25
  36.7 10.0 %collective-permute-start.8 = (bf16[128,1152]{1,0:T(8,128)(2,1)S(1)}, bf16[128,1152]{1,0:T(8,128)(2,1)S(1)}, u32[]{:S(2)}, u32[]{:S(2)}) collective-permute-start(bf16[128,1152]{1,0:T(8,128)(2,1)S(1)} %slice.75), channel_id=1, source_target_pairs={{0,8},{8,16},{16,24},{24,0},{1,9},{9,17},{17,25},{25,1},{2,10},{10... | collective-permute-start | bytes 884744 | tf_op jit(solution)/shard_map/ppermute | solution.py:25
  37.1 9.9 %collective-permute-start.9 = (bf16[128,1152]{1,0:T(8,128)(2,1)S(1)}, bf16[128,1152]{1,0:T(8,128)(2,1)S(1)}, u32[]{:S(2)}, u32[]{:S(2)}) collective-permute-start(bf16[128,1152]{1,0:T(8,128)(2,1)S(1)} %slice.76), channel_id=1, source_target_pairs={{0,24},{8,0},{16,8},{24,16},{1,25},{9,1},{17,9},{25,17},{2,26},{10... | collective-permute-start | bytes 884744 | tf_op jit(solution)/shard_map/ppermute | solution.py:25
  47.0 5.1 %collective-permute-start.13 = (bf16[256,1152]{1,0:T(8,128)(2,1)S(1)}, bf16[256,1152]{1,0:T(8,128)(2,1)S(1)}, u32[]{:S(2)}, u32[]{:S(2)}) collective-permute-start(bf16[256,1152]{1,0:T(8,128)(2,1)S(1)} %constant_dynamic-update-slice_fusion.4.refs_11_.refs_10_), channel_id=1, source_target_pairs={{0,1},{1,0},{2,3},{3,2},{4,5},{5,4},{6,7},{7,6},{8,9},{9,8},{10,11... | collective-permute-start | bytes 1769480 | tf_op jit(solution)/shard_map/ppermute | solution.py:25
  54.7 2.2 %collective-permute-start.14 = (f16[256,1152]{1,0:T(8,128)(2,1)S(1)}, f16[256,1152]{1,0:T(8,128)(2,1)S(1)}, u32[]{:S(2)}, u32[]{:S(2)}) collective-permute-start(f16[256,1152]{1,0:T(8,128)(2,1)S(1)} %convert_element_type.74), channel_id=1, source_target_pairs={{0,1},{1,0},{2,3},{3,2},{4,5},{5,4},{6,7},{7,6},{8,9},{9,8},{10,11... | collective-permute-start | bytes 1769480 | tf_op jit(solution)/shard_map/ppermute | solution.py:25
  57.1 14.0 %collective-permute-start.19 = (f16[768,1152]{1,0:T(8,128)(2,1)S(1)}, f16[768,1152]{1,0:T(8,128)(2,1)S(1)}, u32[]{:S(2)}, u32[]{:S(2)}) collective-permute-start(f16[768,1152]{1,0:T(8,128)(2,1)S(1)} %convert_element_type.78), channel_id=1, source_target_pairs={{0,1},{1,0},{2,3},{3,2},{4,5},{5,4},{6,7},{7,6},{8,9},{9,8},{10,11... | collective-permute-start | bytes 5308424 | tf_op jit(solution)/shard_map/ppermute | solution.py:25
  57.6 11.8 %collective-permute-start.15 = (f16[128,1152]{1,0:T(8,128)(2,1)S(1)}, f16[128,1152]{1,0:T(8,128)(2,1)S(1)}, u32[]{:S(2)}, u32[]{:S(2)}) collective-permute-start(f16[128,1152]{1,0:T(8,128)(2,1)S(1)} %get-tuple-element.181), channel_id=1, source_target_pairs={{0,24},{8,0},{16,8},{24,16},{1,25},{9,1},{17,9},{25,17},{2,26},{10... | collective-permute-start | bytes 884744 | tf_op jit(solution)/shard_map/ppermute | solution.py:25
  58.2 11.3 %collective-permute-start.16 = (f16[128,1152]{1,0:T(8,128)(2,1)S(1)}, f16[128,1152]{1,0:T(8,128)(2,1)S(1)}, u32[]{:S(2)}, u32[]{:S(2)}) collective-permute-start(f16[128,1152]{1,0:T(8,128)(2,1)S(1)} %get-tuple-element.180), channel_id=1, source_target_pairs={{0,8},{8,16},{16,24},{24,0},{1,9},{9,17},{17,25},{25,1},{2,10},{10... | collective-permute-start | bytes 884744 | tf_op jit(solution)/shard_map/ppermute | solution.py:25
  61.0 8.6 %collective-permute-start.17 = (f16[128,1152]{1,0:T(8,128)(2,1)S(1)}, f16[128,1152]{1,0:T(8,128)(2,1)S(1)}, u32[]{:S(2)}, u32[]{:S(2)}) collective-permute-start(f16[128,1152]{1,0:T(8,128)(2,1)S(1)} %get-tuple-element.179), channel_id=1, source_target_pairs={{0,96},{32,0},{64,32},{96,64},{1,97},{33,1},{65,33},{97,65},{2,98}... | collective-permute-start | bytes 884744 | tf_op jit(solution)/shard_map/ppermute | solution.py:25
  61.5 9.6 %collective-permute-start.18 = (f16[128,1152]{1,0:T(8,128)(2,1)S(1)}, f16[128,1152]{1,0:T(8,128)(2,1)S(1)}, u32[]{:S(2)}, u32[]{:S(2)}) collective-permute-start(f16[128,1152]{1,0:T(8,128)(2,1)S(1)} %get-tuple-element.178), channel_id=1, source_target_pairs={{0,32},{32,64},{64,96},{96,0},{1,33},{33,65},{65,97},{97,1},{2,34}... | collective-permute-start | bytes 884744 | tf_op jit(solution)/shard_map/ppermute | solution.py:25
  72.0 18.3 %collective-permute-start.20 = (f16[256,1152]{1,0:T(8,128)(2,1)S(1)}, f16[256,1152]{1,0:T(8,128)(2,1)S(1)}, u32[]{:S(2)}, u32[]{:S(2)}) collective-permute-start(f16[256,1152]{1,0:T(8,128)(2,1)S(1)} %add_convert_fusion.3), channel_id=1, source_target_pairs={{0,24},{8,0},{16,8},{24,16},{1,25},{9,1},{17,9},{25,17},{2,26},{10... | collective-permute-start | bytes 1769480 | tf_op jit(solution)/shard_map/ppermute | solution.py:25
  72.1 18.2 %collective-permute-start.21 = (f16[256,1152]{1,0:T(8,128)(2,1)S(1)}, f16[256,1152]{1,0:T(8,128)(2,1)S(1)}, u32[]{:S(2)}, u32[]{:S(2)}) collective-permute-start(f16[256,1152]{1,0:T(8,128)(2,1)S(1)} %get-tuple-element.148), channel_id=1, source_target_pairs={{0,8},{8,16},{16,24},{24,0},{1,9},{9,17},{17,25},{25,1},{2,10},{10... | collective-permute-start | bytes 1769480 | tf_op jit(solution)/shard_map/ppermute | solution.py:25
  75.3 15.0 %collective-permute-start.22 = (f16[256,1152]{1,0:T(8,128)(2,1)S(1)}, f16[256,1152]{1,0:T(8,128)(2,1)S(1)}, u32[]{:S(2)}, u32[]{:S(2)}) collective-permute-start(f16[256,1152]{1,0:T(8,128)(2,1)S(1)} %get-tuple-element.149), channel_id=1, source_target_pairs={{0,96},{32,0},{64,32},{96,64},{1,97},{33,1},{65,33},{97,65},{2,98}... | collective-permute-start | bytes 1769480 | tf_op jit(solution)/shard_map/ppermute | solution.py:25
  75.4 14.9 %collective-permute-start.23 = (f16[256,1152]{1,0:T(8,128)(2,1)S(1)}, f16[256,1152]{1,0:T(8,128)(2,1)S(1)}, u32[]{:S(2)}, u32[]{:S(2)}) collective-permute-start(f16[256,1152]{1,0:T(8,128)(2,1)S(1)} %get-tuple-element.150), channel_id=1, source_target_pairs={{0,32},{32,64},{64,96},{96,0},{1,33},{33,65},{65,97},{97,1},{2,34}... | collective-permute-start | bytes 1769480 | tf_op jit(solution)/shard_map/ppermute | solution.py:25
  77.3 1.1 %collective-permute-start.24 = (f32[1,3]{1,0:T(1,128)S(1)}, f32[1,3]{1,0:T(1,128)S(1)}, u32[]{:S(2)}, u32[]{:S(2)}) collective-permute-start(f32[1,3]{1,0:T(1,128)S(1)} %bitcast.4), channel_id=1, source_target_pairs={{0,1},{1,0},{2,3},{3,2},{4,5},{5,4},{6,7},{7,6},{8,9},{9,8},{10,11... | collective-permute-start | bytes 44 | tf_op jit(solution)/shard_map/ppermute | solution.py:25
  78.4 3.5 %collective-permute-start.25 = (f32[1,3]{1,0:T(1,128)S(1)}, f32[1,3]{1,0:T(1,128)S(1)}, u32[]{:S(2)}, u32[]{:S(2)}) collective-permute-start(f32[1,3]{1,0:T(1,128)S(1)} %add.109), channel_id=1, source_target_pairs={{0,2},{2,0},{4,6},{6,4},{1,3},{3,1},{5,7},{7,5},{8,10},{10,8},{12,... | collective-permute-start | bytes 44 | tf_op jit(solution)/shard_map/ppermute | solution.py:25
  82.0 4.8 %collective-permute-start.26 = (f32[1,3]{1,0:T(1,128)S(1)}, f32[1,3]{1,0:T(1,128)S(1)}, u32[]{:S(2)}, u32[]{:S(2)}) collective-permute-start(f32[1,3]{1,0:T(1,128)S(1)} %add.110), channel_id=1, source_target_pairs={{2,4},{4,2},{6,0},{0,6},{3,5},{5,3},{7,1},{1,7},{10,12},{12,10},{1... | collective-permute-start | bytes 44 | tf_op jit(solution)/shard_map/ppermute | solution.py:25
  86.7 3.5 %collective-permute-start.27 = (f32[1,3]{1,0:T(1,128)S(1)}, f32[1,3]{1,0:T(1,128)S(1)}, u32[]{:S(2)}, u32[]{:S(2)}) collective-permute-start(f32[1,3]{1,0:T(1,128)S(1)} %add.111), channel_id=1, source_target_pairs={{0,8},{8,0},{16,24},{24,16},{1,9},{9,1},{17,25},{25,17},{2,10},{10... | collective-permute-start | bytes 44 | tf_op jit(solution)/shard_map/ppermute | solution.py:25
  90.8 10.3 %collective-permute-start.28 = (f16[128,1152]{1,0:T(8,128)(2,1)S(1)}, f16[128,1152]{1,0:T(8,128)(2,1)S(1)}, u32[]{:S(2)}, u32[]{:S(2)}) collective-permute-start(f16[128,1152]{1,0:T(8,128)(2,1)S(1)} %slice_convert_fusion.1), channel_id=1, source_target_pairs={{0,2},{2,0},{4,6},{6,4},{1,3},{3,1},{5,7},{7,5},{8,10},{10,8},{12,... | collective-permute-start | bytes 884744 | tf_op jit(solution)/shard_map/ppermute | solution.py:25
  91.3 9.8 %collective-permute-start.29 = (f16[128,1152]{1,0:T(8,128)(2,1)S(1)}, f16[128,1152]{1,0:T(8,128)(2,1)S(1)}, u32[]{:S(2)}, u32[]{:S(2)}) collective-permute-start(f16[128,1152]{1,0:T(8,128)(2,1)S(1)} %slice_convert_fusion), channel_id=1, source_target_pairs={{2,4},{4,2},{6,0},{0,6},{3,5},{5,3},{7,1},{1,7},{10,12},{12,10},{1... | collective-permute-start | bytes 884744 | tf_op jit(solution)/shard_map/ppermute | solution.py:25
  92.8 4.8 %collective-permute-start.30 = (f32[1,3]{1,0:T(1,128)S(1)}, f32[1,3]{1,0:T(1,128)S(1)}, u32[]{:S(2)}, u32[]{:S(2)}) collective-permute-start(f32[1,3]{1,0:T(1,128)S(1)} %add.112), channel_id=1, source_target_pairs={{8,16},{16,8},{24,0},{0,24},{9,17},{17,9},{25,1},{1,25},{10,18},{1... | collective-permute-start | bytes 44 | tf_op jit(solution)/shard_map/ppermute | solution.py:25
  97.6 3.5 %collective-permute-start.31 = (f32[1,3]{1,0:T(1,128)S(1)}, f32[1,3]{1,0:T(1,128)S(1)}, u32[]{:S(2)}, u32[]{:S(2)}) collective-permute-start(f32[1,3]{1,0:T(1,128)S(1)} %add.117), channel_id=1, source_target_pairs={{0,32},{32,0},{64,96},{96,64},{1,33},{33,1},{65,97},{97,65},{2,34}... | collective-permute-start | bytes 44 | tf_op jit(solution)/shard_map/ppermute | solution.py:25
  101.1 4.8 %collective-permute-start.32 = (f32[1,3]{1,0:T(1,128)S(1)}, f32[1,3]{1,0:T(1,128)S(1)}, u32[]{:S(2)}, u32[]{:S(2)}) collective-permute-start(f32[1,3]{1,0:T(1,128)S(1)} %add.118), channel_id=1, source_target_pairs={{32,64},{64,32},{96,0},{0,96},{33,65},{65,33},{97,1},{1,97},{34,66... | collective-permute-start | bytes 44 | tf_op jit(solution)/shard_map/ppermute | solution.py:25

commit v5 on v4

--- a/solution.py
+++ b/solution.py
@@ -217,9 +217,10 @@
     )
     weights = [weights_a, weights_b, weights_c, weights_d]
 
-    *weights, ps_far = fence(*weights, narrow(ps_far))
+    value = jnp.sum(sums_a + sums_b + sums_c + sums_d, axis=(1, 2)).reshape(1, 3)
+    *weights, ps_far, value = fence(*weights, narrow(ps_far), value)
     ps_far = send(ps_far, "c", SWAP)
-    value = jnp.sum(sums_a + sums_b + sums_c + sums_d, axis=(1, 2)).reshape(1, 3)
+    value = value + send(value, "c", SWAP)
     pi_far, ps_near = block(
         None,
         images,
@@ -269,7 +270,7 @@
         send(near[2], "y", DOWN),
         send(near[3], "y", UP),
     ]
-    for axis, pairs in (("c", SWAP), (Z, EVEN), (Z, ODD), ("x", EVEN)):
+    for axis, pairs in ((Z, EVEN), (Z, ODD), ("x", EVEN)):
         value = value + send(value, axis, pairs)
     pt_own = pt_own + wide(ps_near[4 * rows :])
     *near, pi_own, pt_own, value = fence(*near, pi_own, pt_own, value)
@@ -279,14 +280,14 @@
     last = [narrow(pi_own[rows:]), narrow(pt_own[rows:])]
     *last, value = fence(*last, value)
     last = [send(last[0], Z, EVEN), send(last[1], Z, ODD)]
-    for axis, pairs in (("x", ODD), ("y", EVEN)):
-        value = value + send(value, axis, pairs)
-    *last, value = fence(*last, value)
-    value = value + send(value, "y", ODD)
-    objective_results = value[0] * jnp.stack([jnp.float32(1.0), temperature, jnp.float32(1.0)]) / example_number
+    value = value + send(value, "x", ODD)
+    low, far, high = (send(value, "y", [(i, (i + step) % 4) for i in range(4)]) for step in (1, 2, 3))
     scale = temperature / SCALE
     image_gradient = projection(scale * (pi_own[:rows] + wide(last[0])), unit32[:rows], inverse[:rows])
     text_grad = projection(scale * (pt_own[:rows] + wide(last[1])), unit32[rows:], inverse[rows:])
+    image_gradient, text_grad, value, low, far, high = fence(image_gradient, text_grad, value, low, far, high)
+    value = (value + far) + (low + high)
+    objective_results = value[0] * jnp.stack([jnp.float32(1.0), temperature, jnp.float32(1.0)]) / example_number
     return (image_gradient, text_grad, objective_results)
 
 

time: 107 us -> 104 us (0.972)
  waiting for transfers between devices: 42.5 us -> 37.8 us
  starting transfers between devices: 33.2 us -> 35 us
    ppermute x33 -> x34, waiting for transfers between devices: 42.5 us -> 37.8 us  [send(): return lax.ppermute(value, axis, pairs)]
    ppermute x33 -> x34, starting transfers between devices: 33.2 us -> 35 us  [send(): return lax.ppermute(value, axis, pairs)]
  transfers between devices with their start and end apart: 33 -> 34, of which waited for: 17 -> 17; matrix products, arithmetic and copies ran while one was open for 2% -> 2% of each run, Pallas kernels for 18% -> 19%
where the time goes in v5:
time: 104 us
  waiting for transfers between devices  37.8 us (36%)
  starting transfers between devices  35 us (34%)
  Pallas kernels  22 us (21%)
  other arithmetic  5.91 us (6%)
  between operations  2.29 us (2%)
    ppermute x34, waiting for transfers between devices, send(): return lax.ppermute(value, axis, pairs)  37.8 us
    ppermute x34, starting transfers between devices, send(): return lax.ppermute(value, axis, pairs)  35 us
    pallas_call x6, Pallas kernels, block(): pl.pallas_call(functools.partial(block_kernel, len(images), len(texts), l...  22 us
  transfers between devices with their start and end apart: 34, of which 17 were waited for; matrix products, arithmetic and copies ran while one was open for 2% of the time, Pallas kernels for 19%

profile of v5, /device:TPU:6, one launch (start us, length us, event | category | flops | bytes accessed | tf_op | source)
XLA Modules:
  0.0 103.6 jit_solution(12526872363785983741)
XLA Ops:
  0.6 1.1 %pad_maximum_fusion.1 = bf16[256,1152]{1,0:T(8,128)(2,1)S(1)} fusion(bf16[128,1152]{1,0:T(8,128)(2,1)} %param.5, bf16[128,1152]{1,0:T(8,128)(2,1)} %param.4), kind=kLoop, calls=%fused_computation.18 | loop fusion | flops 1179648 | bytes 1179648 | tf_op jit(solution)/shard_map/concatenate | solution.py:145
  1.7 0.2 fusion
  1.9 0.2 fusion.4
  2.2 4.1 %collective-permute-start.1 = (bf16[128,1152]{1,0:T(8,128)(2,1)S(1)}, bf16[128,1152]{1,0:T(8,128)(2,1)S(1)}, u32[]{:S(2)}, u32[]{:S(2)}) collective-permute-start(bf16[128,1152]{1,0:T(8,128)(2,1)S(1)} %get-tuple-element.190), channel_id=1, source_target_pairs={{2,4},{4,2},{6,0},{0,6},{3,5},{5,3},{7,1},{1,7},{10,12},{12,10},{1... | collective-permute-start | bytes 884744 | tf_op jit(solution)/shard_map/ppermute | solution.py:25
  6.3 7.0 %collective-permute-done.1 = bf16[128,1152]{1,0:T(8,128)(2,1)S(1)} collective-permute-done((bf16[128,1152]{1,0:T(8,128)(2,1)S(1)}, bf16[128,1152]{1,0:T(8,128)(2,1)S(1)}, u32[]{:S(2)}, u32[]{:S(2)}) %collective-permute-start.1) | collective-permute-done | bytes 294944 | tf_op jit(solution)/shard_map/ppermute | solution.py:25
  13.3 1.5 %collective-permute-done = bf16[128,1152]{1,0:T(8,128)(2,1)S(1)} collective-permute-done((bf16[128,1152]{1,0:T(8,128)(2,1)S(1)}, bf16[128,1152]{1,0:T(8,128)(2,1)S(1)}, u32[]{:S(2)}, u32[]{:S(2)}) %collective-permute-start) | collective-permute-done | bytes 294944 | tf_op jit(solution)/shard_map/ppermute | solution.py:25
  14.8 1.6 %collective-permute-start.4 = (bf16[256,1152]{1,0:T(8,128)(2,1)S(1)}, bf16[256,1152]{1,0:T(8,128)(2,1)S(1)}, u32[]{:S(2)}, u32[]{:S(2)}) collective-permute-start(bf16[256,1152]{1,0:T(8,128)(2,1)S(1)} %pad_maximum_fusion.3.refs_4_.refs_5_), channel_id=1, source_target_pairs={{0,32},{32,64},{64,96},{96,0},{1,33},{33,65},{65,97},{97,1},{2,34}... | collective-permute-start | bytes 1769480 | tf_op jit(solution)/shard_map/ppermute | solution.py:25
  16.5 1.7 %collective-permute-start.5 = (bf16[256,1152]{1,0:T(8,128)(2,1)S(1)}, bf16[256,1152]{1,0:T(8,128)(2,1)S(1)}, u32[]{:S(2)}, u32[]{:S(2)}) collective-permute-start(bf16[256,1152]{1,0:T(8,128)(2,1)S(1)} %pad_maximum_fusion.3.refs_4_.refs_5_), channel_id=1, source_target_pairs={{0,96},{32,0},{64,32},{96,64},{1,97},{33,1},{65,33},{97,65},{2,98}... | collective-permute-start | bytes 1769480 | tf_op jit(solution)/shard_map/ppermute | solution.py:25
  18.2 0.5 collective-permute-start.2
  18.7 1.5 %collective-permute-start.3 = (bf16[256,1152]{1,0:T(8,128)(2,1)S(1)}, bf16[256,1152]{1,0:T(8,128)(2,1)S(1)}, u32[]{:S(2)}, u32[]{:S(2)}) collective-permute-start(bf16[256,1152]{1,0:T(8,128)(2,1)S(1)} %pad_maximum_fusion.2.refs_1_.refs_0_), channel_id=1, source_target_pairs={{0,24},{8,0},{16,8},{24,16},{1,25},{9,1},{17,9},{25,17},{2,26},{10... | collective-permute-start | bytes 1769480 | tf_op jit(solution)/shard_map/ppermute | solution.py:25
  21.7 0.2 collective-permute-done.7
  21.9 8.2 %collective-permute-done.4.refs_5_.refs_6_ = bf16[256,1152]{1,0:T(8,128)(2,1)S(1)} collective-permute-done((bf16[256,1152]{1,0:T(8,128)(2,1)S(1)}, bf16[256,1152]{1,0:T(8,128)(2,1)S(1)}, u32[]{:S(2)}, u32[]{:S(2)}) %collective-permute-start.4) | collective-permute-done | bytes 589856 | tf_op jit(solution)/shard_map/ppermute | solution.py:25
  30.1 1.6 %collective-permute-done.2.refs_2_.refs_1_ = bf16[256,1152]{1,0:T(8,128)(2,1)S(1)} collective-permute-done((bf16[256,1152]{1,0:T(8,128)(2,1)S(1)}, bf16[256,1152]{1,0:T(8,128)(2,1)S(1)}, u32[]{:S(2)}, u32[]{:S(2)}) %collective-permute-start.2) | collective-permute-done | bytes 589856 | tf_op jit(solution)/shard_map/ppermute | solution.py:25
  31.7 1.4 %collective-permute-done.3.refs_3_.refs_2_ = bf16[256,1152]{1,0:T(8,128)(2,1)S(1)} collective-permute-done((bf16[256,1152]{1,0:T(8,128)(2,1)S(1)}, bf16[256,1152]{1,0:T(8,128)(2,1)S(1)}, u32[]{:S(2)}, u32[]{:S(2)}) %collective-permute-start.3) | collective-permute-done | bytes 589856 | tf_op jit(solution)/shard_map/ppermute | solution.py:25
  33.4 0.3 collective-permute-start.10
  33.7 3.0 %collective-permute-start.11 = (bf16[128,1152]{1,0:T(8,128)(2,1)S(1)}, bf16[128,1152]{1,0:T(8,128)(2,1)S(1)}, u32[]{:S(2)}, u32[]{:S(2)}) collective-permute-start(bf16[128,1152]{1,0:T(8,128)(2,1)S(1)} %slice.78), channel_id=1, source_target_pairs={{0,96},{32,0},{64,32},{96,64},{1,97},{33,1},{65,33},{97,65},{2,98}... | collective-permute-start | bytes 884744 | tf_op jit(solution)/shard_map/ppermute | solution.py:25
  36.7 0.4 collective-permute-start.8
  37.1 1.8 %collective-permute-start.9 = (bf16[128,1152]{1,0:T(8,128)(2,1)S(1)}, bf16[128,1152]{1,0:T(8,128)(2,1)S(1)}, u32[]{:S(2)}, u32[]{:S(2)}) collective-permute-start(bf16[128,1152]{1,0:T(8,128)(2,1)S(1)} %slice.76), channel_id=1, source_target_pairs={{0,24},{8,0},{16,8},{24,16},{1,25},{9,1},{17,9},{25,17},{2,26},{10... | collective-permute-start | bytes 884744 | tf_op jit(solution)/shard_map/ppermute | solution.py:25
  39.0 3.9 %shard_map.67 = (bf16[12,256,256]{2,1,0:T(8,128)(2,1)S(1)}, f32[3,8,256]{2,1,0:T(8,128)S(1)}) custom-call(f32[2]{0:T(128)S(1)} %pad_maximum_fusion.4.refs_0_, bf16[256,1152]{1,0:T(8,128)(2,1)S(1)} %pad_maximum_fusion.2.refs_1_.refs_0_, bf16[256,1152]{1,0:T(8,128)(2,1)S(1)} %collective-permute-done.2.refs_2_.refs_1_, ...), custom_call_target="tpu_custom_call" | custom-call | flops 1 | bytes 1 | tf_op jit(solution)/shard_map/pallas_call | solution.py:113
  43.0 3.7 %shard_map.68 = (bf16[6,256,256]{2,1,0:T(8,128)(2,1)S(1)}, f32[3,8,256]{2,1,0:T(8,128)S(1)}, f32[768,1152]{1,0:T(8,128)S(1)}) custom-call(f32[2]{0:T(128)S(1)} %pad_maximum_fusion.4.refs_0_, bf16[256,1152]{1,0:T(8,128)(2,1)S(1)} %pad_maximum_fusion.2.refs_1_.refs_0_, bf16[256,1152]{1,0:T(8,128)(2,1)S(1)} %collective-permute-done.2.refs_2_.refs_1_, ...), custom_call_target="tpu_custom_call" | custom-call | flops 1 | bytes 1 | tf_op jit(solution)/shard_map/pallas_call | solution.py:113
  46.7 0.2 collective-permute-done.9
  47.0 0.3 collective-permute-start.13
  47.4 4.7 %shard_map.69 = (bf16[10,256,256]{2,1,0:T(8,128)(2,1)S(1)}, f32[3,8,256]{2,1,0:T(8,128)S(1)}, f32[256,1152]{1,0:T(8,128)S(1)}, f32[256,1152]{1,0:T(8,128)S(1)}) custom-call(f32[2]{0:T(128)S(1)} %pad_maximum_fusion.4.refs_0_, bf16[256,1152]{1,0:T(8,128)(2,1)S(1)} %pad_maximum_fusion.2.refs_1_.refs_0_, ...), custom_call_target="tpu_custom_call" | custom-call | flops 1 | bytes 1 | tf_op jit(solution)/shard_map/pallas_call | solution.py:113
  52.1 2.5 %shard_map.70 = (bf16[4,256,256]{2,1,0:T(8,128)(2,1)S(1)}, f32[3,8,256]{2,1,0:T(8,128)S(1)}, f32[256,1152]{1,0:T(8,128)S(1)}) custom-call(f32[2]{0:T(128)S(1)} %pad_maximum_fusion.4.refs_0_, bf16[256,1152]{1,0:T(8,128)(2,1)S(1)} %pad_maximum_fusion.2.refs_1_.refs_0_, bf16[256,1152]{1,0:T(8,128)(2,1)S(1)} %collective-permute-done.2.refs_2_.refs_1_, ...), custom_call_target="tpu_custom_call" | custom-call | flops 1 | bytes 1 | tf_op jit(solution)/shard_map/pallas_call | solution.py:113
  54.7 0.1 add_reduce_fusion
  54.8 0.5 collective-permute-start.14
  55.4 0.9 shard_map.71
  56.3 0.2 convert_element_type.78
  56.6 0.3 collective-permute-done.15
  56.9 0.2 add_convert_fusion.4
  57.1 0.5 collective-permute-start.20
  57.6 0.1 fusion.7
  57.7 0.6 collective-permute-start.16
  58.2 2.7 %collective-permute-start.17 = (f16[128,1152]{1,0:T(8,128)(2,1)S(1)}, f16[128,1152]{1,0:T(8,128)(2,1)S(1)}, u32[]{:S(2)}, u32[]{:S(2)}) collective-permute-start(f16[128,1152]{1,0:T(8,128)(2,1)S(1)} %get-tuple-element.188), channel_id=1, source_target_pairs={{0,8},{8,16},{16,24},{24,0},{1,9},{9,17},{17,25},{25,1},{2,10},{10... | collective-permute-start | bytes 884744 | tf_op jit(solution)/shard_map/ppermute | solution.py:25
  61.0 0.1 fusion.6
  61.1 0.5 collective-permute-start.18
  61.6 1.6 %collective-permute-start.19 = (f16[128,1152]{1,0:T(8,128)(2,1)S(1)}, f16[128,1152]{1,0:T(8,128)(2,1)S(1)}, u32[]{:S(2)}, u32[]{:S(2)}) collective-permute-start(f16[128,1152]{1,0:T(8,128)(2,1)S(1)} %get-tuple-element.186), channel_id=1, source_target_pairs={{0,32},{32,64},{64,96},{96,0},{1,33},{33,65},{65,97},{97,1},{2,34}... | collective-permute-start | bytes 884744 | tf_op jit(solution)/shard_map/ppermute | solution.py:25
  63.2 6.3 %shard_map.72 = (f32[256,1152]{1,0:T(8,128)S(1)}, f32[256,1152]{1,0:T(8,128)S(1)}, f32[256,1152]{1,0:T(8,128)S(1)}, f32[256,1152]{1,0:T(8,128)S(1)}, f32[256,1152]{1,0:T(8,128)S(1)}, /*index=5*/f32[256,1152]{1,0:T(8,128)S(1)}) custom-call(bf16[256,1152]{1,0:T(8,128)(2,1)S(1)} %pad_maximum_fusion.2.refs_1_.refs_0_, ...), custom_call_target="tpu_custom_call" | custom-call | flops 1 | bytes 1 | tf_op jit(solution)/shard_map/pallas_call | solution.py:113
  69.5 0.1 collective-permute-done.18
  69.6 1.5 %collective-permute-done.19 = f16[128,1152]{1,0:T(8,128)(2,1)S(1)} collective-permute-done((f16[128,1152]{1,0:T(8,128)(2,1)S(1)}, f16[128,1152]{1,0:T(8,128)(2,1)S(1)}, u32[]{:S(2)}, u32[]{:S(2)}) %collective-permute-start.19) | collective-permute-done | bytes 294944 | tf_op jit(solution)/shard_map/ppermute | solution.py:25
  71.2 0.1 add_convert_fusion.3
  71.3 0.7 convert_add_fusion.2
  72.1 3.2 %collective-permute-start.22 = (f16[256,1152]{1,0:T(8,128)(2,1)S(1)}, f16[256,1152]{1,0:T(8,128)(2,1)S(1)}, u32[]{:S(2)}, u32[]{:S(2)}) collective-permute-start(f16[256,1152]{1,0:T(8,128)(2,1)S(1)} %get-tuple-element.153), channel_id=1, source_target_pairs={{0,8},{8,16},{16,24},{24,0},{1,9},{9,17},{17,25},{25,1},{2,10},{10... | collective-permute-start | bytes 1769480 | tf_op jit(solution)/shard_map/ppermute | solution.py:25
  75.3 0.1 collective-permute-start.23
  75.5 1.9 %collective-permute-start.24 = (f16[256,1152]{1,0:T(8,128)(2,1)S(1)}, f16[256,1152]{1,0:T(8,128)(2,1)S(1)}, u32[]{:S(2)}, u32[]{:S(2)}) collective-permute-start(f16[256,1152]{1,0:T(8,128)(2,1)S(1)} %get-tuple-element.155), channel_id=1, source_target_pairs={{0,32},{32,64},{64,96},{96,0},{1,33},{33,65},{65,97},{97,1},{2,34}... | collective-permute-start | bytes 1769480 | tf_op jit(solution)/shard_map/ppermute | solution.py:25
  77.4 0.6 collective-permute-start.25
  78.0 3.0 %collective-permute-done.25 = f32[1,3]{1,0:T(1,128)S(1)} collective-permute-done((f32[1,3]{1,0:T(1,128)S(1)}, f32[1,3]{1,0:T(1,128)S(1)}, u32[]{:S(2)}, u32[]{:S(2)}) %collective-permute-start.25) | collective-permute-done | bytes 44 | tf_op jit(solution)/shard_map/ppermute | solution.py:25
  80.9 1.8 %collective-permute-start.26 = (f32[1,3]{1,0:T(1,128)S(1)}, f32[1,3]{1,0:T(1,128)S(1)}, u32[]{:S(2)}, u32[]{:S(2)}) collective-permute-start(f32[1,3]{1,0:T(1,128)S(1)} %add.113), channel_id=1, source_target_pairs={{2,4},{4,2},{6,0},{0,6},{3,5},{5,3},{7,1},{1,7},{10,12},{12,10},{1... | collective-permute-start | bytes 44 | tf_op jit(solution)/shard_map/ppermute | solution.py:25
  82.7 3.0 %collective-permute-done.26 = f32[1,3]{1,0:T(1,128)S(1)} collective-permute-done((f32[1,3]{1,0:T(1,128)S(1)}, f32[1,3]{1,0:T(1,128)S(1)}, u32[]{:S(2)}, u32[]{:S(2)}) %collective-permute-start.26) | collective-permute-done | bytes 44 | tf_op jit(solution)/shard_map/ppermute | solution.py:25
  85.7 3.5 %collective-permute-done.27 = f32[1,3]{1,0:T(1,128)S(1)} collective-permute-done((f32[1,3]{1,0:T(1,128)S(1)}, f32[1,3]{1,0:T(1,128)S(1)}, u32[]{:S(2)}, u32[]{:S(2)}) %collective-permute-start.27) | collective-permute-done | bytes 44 | tf_op jit(solution)/shard_map/ppermute | solution.py:25
  89.2 0.9 collective-permute-done.24
  90.2 0.2 convert_add_fusion
  90.4 0.2 convert_add_fusion.1
  90.7 0.7 collective-permute-start.28
  91.4 1.3 %collective-permute-start.29 = (f16[128,1152]{1,0:T(8,128)(2,1)S(1)}, f16[128,1152]{1,0:T(8,128)(2,1)S(1)}, u32[]{:S(2)}, u32[]{:S(2)}) collective-permute-start(f16[128,1152]{1,0:T(8,128)(2,1)S(1)} %slice_convert_fusion), channel_id=1, source_target_pairs={{2,4},{4,2},{6,0},{0,6},{3,5},{5,3},{7,1},{1,7},{10,12},{12,10},{1... | collective-permute-start | bytes 884744 | tf_op jit(solution)/shard_map/ppermute | solution.py:25
  92.7 0.3 collective-permute-start.30
  93.0 4.5 %collective-permute-done.30 = f32[1,3]{1,0:T(1,128)S(1)} collective-permute-done((f32[1,3]{1,0:T(1,128)S(1)}, f32[1,3]{1,0:T(1,128)S(1)}, u32[]{:S(2)}, u32[]{:S(2)}) %collective-permute-start.30) | collective-permute-done | bytes 44 | tf_op jit(solution)/shard_map/ppermute | solution.py:25
  97.5 1.8 %collective-permute-start.32 = (f32[1,3]{1,0:T(1,128)S(1)}, f32[1,3]{1,0:T(1,128)S(1)}, u32[]{:S(2)}, u32[]{:S(2)}) collective-permute-start(f32[1,3]{1,0:T(1,128)S(1)} %add.122), channel_id=1, source_target_pairs={{0,64},{32,96},{64,0},{96,32},{1,65},{33,97},{65,1},{97,33},{2,66}... | collective-permute-start | bytes 44 | tf_op jit(solution)/shard_map/ppermute | solution.py:25
  99.3 1.3 %collective-permute-start.33 = (f32[1,3]{1,0:T(1,128)S(1)}, f32[1,3]{1,0:T(1,128)S(1)}, u32[]{:S(2)}, u32[]{:S(2)}) collective-permute-start(f32[1,3]{1,0:T(1,128)S(1)} %add.122), channel_id=1, source_target_pairs={{0,96},{32,0},{64,32},{96,64},{1,97},{33,1},{65,33},{97,65},{2,98}... | collective-permute-start | bytes 44 | tf_op jit(solution)/shard_map/ppermute | solution.py:25
  100.7 0.3 multiply_reduce_fusion
  100.9 1.3 %subtract_multiply_fusion = (f32[128,1152]{1,0:T(8,128)}, f32[128,1152]{1,0:T(8,128)}) fusion(f32[256,1152]{1,0:T(8,128)S(1)} %get-tuple-element.185, f16[128,1152]{1,0:T(8,128)(2,1)S(1)} %collective-permute-done.29, f32[256,1152]{1,0:T(8,128)S(1)} %convert_add_fusion, f32[128]{0:T(128)S(1)} %get-tuple-element.192, f32[128]{0:T(128)S(1)} %get-tuple-element.175, ...), kind=kLoop, calls=%fused_computation.21 | loop fusion | flops 1769472 | bytes 4130820 | tf_op jit(solution)/shard_map/mul | solution.py:40
  102.2 0.3 collective-permute-done.32
  102.6 0.5 collective-permute-done.33
  103.0 0.6 fusion.3
  (52 shorter events, 1.3 us)
Async XLA Ops:
  2.2 11.1 %collective-permute-start.1 = (bf16[128,1152]{1,0:T(8,128)(2,1)S(1)}, bf16[128,1152]{1,0:T(8,128)(2,1)S(1)}, u32[]{:S(2)}, u32[]{:S(2)}) collective-permute-start(bf16[128,1152]{1,0:T(8,128)(2,1)S(1)} %get-tuple-element.190), channel_id=1, source_target_pairs={{2,4},{4,2},{6,0},{0,6},{3,5},{5,3},{7,1},{1,7},{10,12},{12,10},{1... | collective-permute-start | bytes 884744 | tf_op jit(solution)/shard_map/ppermute | solution.py:25
  6.3 8.5 %collective-permute-start = (bf16[128,1152]{1,0:T(8,128)(2,1)S(1)}, bf16[128,1152]{1,0:T(8,128)(2,1)S(1)}, u32[]{:S(2)}, u32[]{:S(2)}) collective-permute-start(bf16[128,1152]{1,0:T(8,128)(2,1)S(1)} %get-tuple-element.191), channel_id=1, source_target_pairs={{0,2},{2,0},{4,6},{6,4},{1,3},{3,1},{5,7},{7,5},{8,10},{10,8},{12,... | collective-permute-start | bytes 884744 | tf_op jit(solution)/shard_map/ppermute | solution.py:25
  6.3 14.0 %collective-permute-start.6 = (bf16[128,1152]{1,0:T(8,128)(2,1)S(1)}, bf16[128,1152]{1,0:T(8,128)(2,1)S(1)}, u32[]{:S(2)}, u32[]{:S(2)}) collective-permute-start(bf16[128,1152]{1,0:T(8,128)(2,1)S(1)} %get-tuple-element.190), channel_id=1, source_target_pairs={{0,1},{1,0},{2,3},{3,2},{4,5},{5,4},{6,7},{7,6},{8,9},{9,8},{10,11... | collective-permute-start | bytes 884744 | tf_op jit(solution)/shard_map/ppermute | solution.py:25
  14.8 15.2 %collective-permute-start.4 = (bf16[256,1152]{1,0:T(8,128)(2,1)S(1)}, bf16[256,1152]{1,0:T(8,128)(2,1)S(1)}, u32[]{:S(2)}, u32[]{:S(2)}) collective-permute-start(bf16[256,1152]{1,0:T(8,128)(2,1)S(1)} %pad_maximum_fusion.3.refs_4_.refs_5_), channel_id=1, source_target_pairs={{0,32},{32,64},{64,96},{96,0},{1,33},{33,65},{65,97},{97,1},{2,34}... | collective-permute-start | bytes 1769480 | tf_op jit(solution)/shard_map/ppermute | solution.py:25
  16.5 13.6 %collective-permute-start.5 = (bf16[256,1152]{1,0:T(8,128)(2,1)S(1)}, bf16[256,1152]{1,0:T(8,128)(2,1)S(1)}, u32[]{:S(2)}, u32[]{:S(2)}) collective-permute-start(bf16[256,1152]{1,0:T(8,128)(2,1)S(1)} %pad_maximum_fusion.3.refs_4_.refs_5_), channel_id=1, source_target_pairs={{0,96},{32,0},{64,32},{96,64},{1,97},{33,1},{65,33},{97,65},{2,98}... | collective-permute-start | bytes 1769480 | tf_op jit(solution)/shard_map/ppermute | solution.py:25
  18.2 13.5 %collective-permute-start.2 = (bf16[256,1152]{1,0:T(8,128)(2,1)S(1)}, bf16[256,1152]{1,0:T(8,128)(2,1)S(1)}, u32[]{:S(2)}, u32[]{:S(2)}) collective-permute-start(bf16[256,1152]{1,0:T(8,128)(2,1)S(1)} %pad_maximum_fusion.2.refs_1_.refs_0_), channel_id=1, source_target_pairs={{0,8},{8,16},{16,24},{24,0},{1,9},{9,17},{17,25},{25,1},{2,10},{10... | collective-permute-start | bytes 1769480 | tf_op jit(solution)/shard_map/ppermute | solution.py:25
  18.7 14.4 %collective-permute-start.3 = (bf16[256,1152]{1,0:T(8,128)(2,1)S(1)}, bf16[256,1152]{1,0:T(8,128)(2,1)S(1)}, u32[]{:S(2)}, u32[]{:S(2)}) collective-permute-start(bf16[256,1152]{1,0:T(8,128)(2,1)S(1)} %pad_maximum_fusion.2.refs_1_.refs_0_), channel_id=1, source_target_pairs={{0,24},{8,0},{16,8},{24,16},{1,25},{9,1},{17,9},{25,17},{2,26},{10... | collective-permute-start | bytes 1769480 | tf_op jit(solution)/shard_map/ppermute | solution.py:25
  20.3 1.6 %collective-permute-start.7 = (bf16[128,1152]{1,0:T(8,128)(2,1)S(1)}, bf16[128,1152]{1,0:T(8,128)(2,1)S(1)}, u32[]{:S(2)}, u32[]{:S(2)}) collective-permute-start(bf16[128,1152]{1,0:T(8,128)(2,1)S(1)} %collective-permute-done.1), channel_id=1, source_target_pairs={{0,1},{1,0},{2,3},{3,2},{4,5},{5,4},{6,7},{7,6},{8,9},{9,8},{10,11... | collective-permute-start | bytes 884744 | tf_op jit(solution)/shard_map/ppermute | solution.py:25
  33.2 9.6 %collective-permute-start.12 = (bf16[512,1152]{1,0:T(8,128)(2,1)S(1)}, bf16[512,1152]{1,0:T(8,128)(2,1)S(1)}, u32[]{:S(2)}, u32[]{:S(2)}) collective-permute-start(bf16[512,1152]{1,0:T(8,128)(2,1)S(1)} %pad_maximum_fusion), channel_id=1, source_target_pairs={{0,1},{1,0},{2,3},{3,2},{4,5},{5,4},{6,7},{7,6},{8,9},{9,8},{10,11... | collective-permute-start | bytes 3538952 | tf_op jit(solution)/shard_map/ppermute | solution.py:25
  33.4 13.3 %collective-permute-start.10 = (bf16[128,1152]{1,0:T(8,128)(2,1)S(1)}, bf16[128,1152]{1,0:T(8,128)(2,1)S(1)}, u32[]{:S(2)}, u32[]{:S(2)}) collective-permute-start(bf16[128,1152]{1,0:T(8,128)(2,1)S(1)} %slice.77), channel_id=1, source_target_pairs={{0,32},{32,64},{64,96},{96,0},{1,33},{33,65},{65,97},{97,1},{2,34}... | collective-permute-start | bytes 884744 | tf_op jit(solution)/shard_map/ppermute | solution.py:25
  33.7 13.0 %collective-permute-start.11 = (bf16[128,1152]{1,0:T(8,128)(2,1)S(1)}, bf16[128,1152]{1,0:T(8,128)(2,1)S(1)}, u32[]{:S(2)}, u32[]{:S(2)}) collective-permute-start(bf16[128,1152]{1,0:T(8,128)(2,1)S(1)} %slice.78), channel_id=1, source_target_pairs={{0,96},{32,0},{64,32},{96,64},{1,97},{33,1},{65,33},{97,65},{2,98}... | collective-permute-start | bytes 884744 | tf_op jit(solution)/shard_map/ppermute | solution.py:25
  36.7 10.0 %collective-permute-start.8 = (bf16[128,1152]{1,0:T(8,128)(2,1)S(1)}, bf16[128,1152]{1,0:T(8,128)(2,1)S(1)}, u32[]{:S(2)}, u32[]{:S(2)}) collective-permute-start(bf16[128,1152]{1,0:T(8,128)(2,1)S(1)} %slice.75), channel_id=1, source_target_pairs={{0,8},{8,16},{16,24},{24,0},{1,9},{9,17},{17,25},{25,1},{2,10},{10... | collective-permute-start | bytes 884744 | tf_op jit(solution)/shard_map/ppermute | solution.py:25
  37.1 9.9 %collective-permute-start.9 = (bf16[128,1152]{1,0:T(8,128)(2,1)S(1)}, bf16[128,1152]{1,0:T(8,128)(2,1)S(1)}, u32[]{:S(2)}, u32[]{:S(2)}) collective-permute-start(bf16[128,1152]{1,0:T(8,128)(2,1)S(1)} %slice.76), channel_id=1, source_target_pairs={{0,24},{8,0},{16,8},{24,16},{1,25},{9,1},{17,9},{25,17},{2,26},{10... | collective-permute-start | bytes 884744 | tf_op jit(solution)/shard_map/ppermute | solution.py:25
  47.0 5.1 %collective-permute-start.13 = (bf16[256,1152]{1,0:T(8,128)(2,1)S(1)}, bf16[256,1152]{1,0:T(8,128)(2,1)S(1)}, u32[]{:S(2)}, u32[]{:S(2)}) collective-permute-start(bf16[256,1152]{1,0:T(8,128)(2,1)S(1)} %constant_dynamic-update-slice_fusion.4.refs_11_.refs_10_), channel_id=1, source_target_pairs={{0,1},{1,0},{2,3},{3,2},{4,5},{5,4},{6,7},{7,6},{8,9},{9,8},{10,11... | collective-permute-start | bytes 1769480 | tf_op jit(solution)/shard_map/ppermute | solution.py:25
  54.8 2.1 %collective-permute-start.14 = (f16[256,1152]{1,0:T(8,128)(2,1)S(1)}, f16[256,1152]{1,0:T(8,128)(2,1)S(1)}, u32[]{:S(2)}, u32[]{:S(2)}) collective-permute-start(f16[256,1152]{1,0:T(8,128)(2,1)S(1)} %convert_element_type.74), channel_id=1, source_target_pairs={{0,1},{1,0},{2,3},{3,2},{4,5},{5,4},{6,7},{7,6},{8,9},{9,8},{10,11... | collective-permute-start | bytes 1769480 | tf_op jit(solution)/shard_map/ppermute | solution.py:25
  55.3 1.6 %collective-permute-start.15 = (f32[1,3]{1,0:T(1,128)S(1)}, f32[1,3]{1,0:T(1,128)S(1)}, u32[]{:S(2)}, u32[]{:S(2)}) collective-permute-start(f32[1,3]{1,0:T(1,128)S(1)} %bitcast.4), channel_id=1, source_target_pairs={{0,1},{1,0},{2,3},{3,2},{4,5},{5,4},{6,7},{7,6},{8,9},{9,8},{10,11... | collective-permute-start | bytes 44 | tf_op jit(solution)/shard_map/ppermute | solution.py:25
  57.1 14.0 %collective-permute-start.20 = (f16[768,1152]{1,0:T(8,128)(2,1)S(1)}, f16[768,1152]{1,0:T(8,128)(2,1)S(1)}, u32[]{:S(2)}, u32[]{:S(2)}) collective-permute-start(f16[768,1152]{1,0:T(8,128)(2,1)S(1)} %convert_element_type.78), channel_id=1, source_target_pairs={{0,1},{1,0},{2,3},{3,2},{4,5},{5,4},{6,7},{7,6},{8,9},{9,8},{10,11... | collective-permute-start | bytes 5308424 | tf_op jit(solution)/shard_map/ppermute | solution.py:25
  57.7 11.8 %collective-permute-start.16 = (f16[128,1152]{1,0:T(8,128)(2,1)S(1)}, f16[128,1152]{1,0:T(8,128)(2,1)S(1)}, u32[]{:S(2)}, u32[]{:S(2)}) collective-permute-start(f16[128,1152]{1,0:T(8,128)(2,1)S(1)} %get-tuple-element.189), channel_id=1, source_target_pairs={{0,24},{8,0},{16,8},{24,16},{1,25},{9,1},{17,9},{25,17},{2,26},{10... | collective-permute-start | bytes 884744 | tf_op jit(solution)/shard_map/ppermute | solution.py:25
  58.2 11.3 %collective-permute-start.17 = (f16[128,1152]{1,0:T(8,128)(2,1)S(1)}, f16[128,1152]{1,0:T(8,128)(2,1)S(1)}, u32[]{:S(2)}, u32[]{:S(2)}) collective-permute-start(f16[128,1152]{1,0:T(8,128)(2,1)S(1)} %get-tuple-element.188), channel_id=1, source_target_pairs={{0,8},{8,16},{16,24},{24,0},{1,9},{9,17},{17,25},{25,1},{2,10},{10... | collective-permute-start | bytes 884744 | tf_op jit(solution)/shard_map/ppermute | solution.py:25
  61.1 8.6 %collective-permute-start.18 = (f16[128,1152]{1,0:T(8,128)(2,1)S(1)}, f16[128,1152]{1,0:T(8,128)(2,1)S(1)}, u32[]{:S(2)}, u32[]{:S(2)}) collective-permute-start(f16[128,1152]{1,0:T(8,128)(2,1)S(1)} %get-tuple-element.187), channel_id=1, source_target_pairs={{0,96},{32,0},{64,32},{96,64},{1,97},{33,1},{65,33},{97,65},{2,98}... | collective-permute-start | bytes 884744 | tf_op jit(solution)/shard_map/ppermute | solution.py:25
  61.6 9.6 %collective-permute-start.19 = (f16[128,1152]{1,0:T(8,128)(2,1)S(1)}, f16[128,1152]{1,0:T(8,128)(2,1)S(1)}, u32[]{:S(2)}, u32[]{:S(2)}) collective-permute-start(f16[128,1152]{1,0:T(8,128)(2,1)S(1)} %get-tuple-element.186), channel_id=1, source_target_pairs={{0,32},{32,64},{64,96},{96,0},{1,33},{33,65},{65,97},{97,1},{2,34}... | collective-permute-start | bytes 884744 | tf_op jit(solution)/shard_map/ppermute | solution.py:25
  72.0 17.2 %collective-permute-start.21 = (f16[256,1152]{1,0:T(8,128)(2,1)S(1)}, f16[256,1152]{1,0:T(8,128)(2,1)S(1)}, u32[]{:S(2)}, u32[]{:S(2)}) collective-permute-start(f16[256,1152]{1,0:T(8,128)(2,1)S(1)} %add_convert_fusion.3), channel_id=1, source_target_pairs={{0,24},{8,0},{16,8},{24,16},{1,25},{9,1},{17,9},{25,17},{2,26},{10... | collective-permute-start | bytes 1769480 | tf_op jit(solution)/shard_map/ppermute | solution.py:25
  72.1 17.1 %collective-permute-start.22 = (f16[256,1152]{1,0:T(8,128)(2,1)S(1)}, f16[256,1152]{1,0:T(8,128)(2,1)S(1)}, u32[]{:S(2)}, u32[]{:S(2)}) collective-permute-start(f16[256,1152]{1,0:T(8,128)(2,1)S(1)} %get-tuple-element.153), channel_id=1, source_target_pairs={{0,8},{8,16},{16,24},{24,0},{1,9},{9,17},{17,25},{25,1},{2,10},{10... | collective-permute-start | bytes 1769480 | tf_op jit(solution)/shard_map/ppermute | solution.py:25
  75.3 13.9 %collective-permute-start.23 = (f16[256,1152]{1,0:T(8,128)(2,1)S(1)}, f16[256,1152]{1,0:T(8,128)(2,1)S(1)}, u32[]{:S(2)}, u32[]{:S(2)}) collective-permute-start(f16[256,1152]{1,0:T(8,128)(2,1)S(1)} %get-tuple-element.154), channel_id=1, source_target_pairs={{0,96},{32,0},{64,32},{96,64},{1,97},{33,1},{65,33},{97,65},{2,98}... | collective-permute-start | bytes 1769480 | tf_op jit(solution)/shard_map/ppermute | solution.py:25
  75.5 14.7 %collective-permute-start.24 = (f16[256,1152]{1,0:T(8,128)(2,1)S(1)}, f16[256,1152]{1,0:T(8,128)(2,1)S(1)}, u32[]{:S(2)}, u32[]{:S(2)}) collective-permute-start(f16[256,1152]{1,0:T(8,128)(2,1)S(1)} %get-tuple-element.155), channel_id=1, source_target_pairs={{0,32},{32,64},{64,96},{96,0},{1,33},{33,65},{65,97},{97,1},{2,34}... | collective-permute-start | bytes 1769480 | tf_op jit(solution)/shard_map/ppermute | solution.py:25
  77.4 3.5 %collective-permute-start.25 = (f32[1,3]{1,0:T(1,128)S(1)}, f32[1,3]{1,0:T(1,128)S(1)}, u32[]{:S(2)}, u32[]{:S(2)}) collective-permute-start(f32[1,3]{1,0:T(1,128)S(1)} %add.105), channel_id=1, source_target_pairs={{0,2},{2,0},{4,6},{6,4},{1,3},{3,1},{5,7},{7,5},{8,10},{10,8},{12,... | collective-permute-start | bytes 44 | tf_op jit(solution)/shard_map/ppermute | solution.py:25
  80.9 4.8 %collective-permute-start.26 = (f32[1,3]{1,0:T(1,128)S(1)}, f32[1,3]{1,0:T(1,128)S(1)}, u32[]{:S(2)}, u32[]{:S(2)}) collective-permute-start(f32[1,3]{1,0:T(1,128)S(1)} %add.113), channel_id=1, source_target_pairs={{2,4},{4,2},{6,0},{0,6},{3,5},{5,3},{7,1},{1,7},{10,12},{12,10},{1... | collective-permute-start | bytes 44 | tf_op jit(solution)/shard_map/ppermute | solution.py:25
  85.7 3.5 %collective-permute-start.27 = (f32[1,3]{1,0:T(1,128)S(1)}, f32[1,3]{1,0:T(1,128)S(1)}, u32[]{:S(2)}, u32[]{:S(2)}) collective-permute-start(f32[1,3]{1,0:T(1,128)S(1)} %add.114), channel_id=1, source_target_pairs={{0,8},{8,0},{16,24},{24,16},{1,9},{9,1},{17,25},{25,17},{2,10},{10... | collective-permute-start | bytes 44 | tf_op jit(solution)/shard_map/ppermute | solution.py:25
  90.7 10.0 %collective-permute-start.28 = (f16[128,1152]{1,0:T(8,128)(2,1)S(1)}, f16[128,1152]{1,0:T(8,128)(2,1)S(1)}, u32[]{:S(2)}, u32[]{:S(2)}) collective-permute-start(f16[128,1152]{1,0:T(8,128)(2,1)S(1)} %slice_convert_fusion.1), channel_id=1, source_target_pairs={{0,2},{2,0},{4,6},{6,4},{1,3},{3,1},{5,7},{7,5},{8,10},{10,8},{12,... | collective-permute-start | bytes 884744 | tf_op jit(solution)/shard_map/ppermute | solution.py:25
  91.4 9.3 %collective-permute-start.29 = (f16[128,1152]{1,0:T(8,128)(2,1)S(1)}, f16[128,1152]{1,0:T(8,128)(2,1)S(1)}, u32[]{:S(2)}, u32[]{:S(2)}) collective-permute-start(f16[128,1152]{1,0:T(8,128)(2,1)S(1)} %slice_convert_fusion), channel_id=1, source_target_pairs={{2,4},{4,2},{6,0},{0,6},{3,5},{5,3},{7,1},{1,7},{10,12},{12,10},{1... | collective-permute-start | bytes 884744 | tf_op jit(solution)/shard_map/ppermute | solution.py:25
  92.7 4.8 %collective-permute-start.30 = (f32[1,3]{1,0:T(1,128)S(1)}, f32[1,3]{1,0:T(1,128)S(1)}, u32[]{:S(2)}, u32[]{:S(2)}) collective-permute-start(f32[1,3]{1,0:T(1,128)S(1)} %add.115), channel_id=1, source_target_pairs={{8,16},{16,8},{24,0},{0,24},{9,17},{17,9},{25,1},{1,25},{10,18},{1... | collective-permute-start | bytes 44 | tf_op jit(solution)/shard_map/ppermute | solution.py:25
  97.4 4.8 %collective-permute-start.31 = (f32[1,3]{1,0:T(1,128)S(1)}, f32[1,3]{1,0:T(1,128)S(1)}, u32[]{:S(2)}, u32[]{:S(2)}) collective-permute-start(f32[1,3]{1,0:T(1,128)S(1)} %add.122), channel_id=1, source_target_pairs={{0,32},{32,64},{64,96},{96,0},{1,33},{33,65},{65,97},{97,1},{2,34}... | collective-permute-start | bytes 44 | tf_op jit(solution)/shard_map/ppermute | solution.py:25
  97.5 5.0 %collective-permute-start.32 = (f32[1,3]{1,0:T(1,128)S(1)}, f32[1,3]{1,0:T(1,128)S(1)}, u32[]{:S(2)}, u32[]{:S(2)}) collective-permute-start(f32[1,3]{1,0:T(1,128)S(1)} %add.122), channel_id=1, source_target_pairs={{0,64},{32,96},{64,0},{96,32},{1,65},{33,97},{65,1},{97,33},{2,66}... | collective-permute-start | bytes 44 | tf_op jit(solution)/shard_map/ppermute | solution.py:25
  99.3 3.7 %collective-permute-start.33 = (f32[1,3]{1,0:T(1,128)S(1)}, f32[1,3]{1,0:T(1,128)S(1)}, u32[]{:S(2)}, u32[]{:S(2)}) collective-permute-start(f32[1,3]{1,0:T(1,128)S(1)} %add.122), channel_id=1, source_target_pairs={{0,96},{32,0},{64,32},{96,64},{1,97},{33,1},{65,33},{97,65},{2,98}... | collective-permute-start | bytes 44 | tf_op jit(solution)/shard_map/ppermute | solution.py:25

commit v6 on v5

--- a/solution.py
+++ b/solution.py
@@ -149,12 +149,21 @@
     temperature = jnp.exp(logarithmic_scale_factor[0])
     scalars = jnp.stack([temperature, offset_shift[0]])
 
-    image_z, text_z = fence(send(image, Z, EVEN), send(text, Z, ODD))
+    image_z, text_z = send(image, Z, EVEN), send(text, Z, ODD)
     i_own = jnp.concatenate([image, image_z], axis=0)
     t_own = jnp.concatenate([text, text_z], axis=0)
 
-    scalars, i_low, i_high, t_low, t_high, text_s, text_zs = fence(
+    where = {}
+
+    def place(number, tiles):
+        where.update({p: (number, t) for t, p in enumerate(tiles)})
+        return tiles
+
+    weights_z, sums_z = block(scalars, [i_own], [t_own], [], where, place(4, [(0, 0)]), 0)
+    scalars, weights_z, sums_z, i_low, i_high, t_low, t_high, text_s, text_zs = fence(
         scalars,
+        weights_z,
+        sums_z,
         send(i_own, "x", UP),
         send(i_own, "x", DOWN),
         send(t_own, "y", UP),
@@ -173,14 +182,8 @@
     s_near = send(jnp.concatenate([t_low, t_high], axis=0), "c", SWAP)
     near_images = [i_own, i_low, i_high]
     near_texts = [t_own, t_low, t_high, s_own]
-    where = {}
-
-    def place(number, tiles):
-        where.update({p: (number, t) for t, p in enumerate(tiles)})
-        return tiles
-
-    tiles_a = place(0, [(i, j) for j in range(4) for i in range(3)])
-    weights_a, sums_a = block(scalars, near_images, near_texts, [], where, tiles_a, 0)
+    tiles_a = place(0, [(i, j) for j in range(4) for i in range(3) if (i, j) != (0, 0)])
+    weights_a, sums_a = block(scalars, near_images, near_texts, [], where, tiles_a)
     weights_a, s_near = fence(weights_a, s_near)
     s_low, s_high = s_near[: 2 * rows], s_near[2 * rows :]
     near_texts = [t_own, t_low, t_high, s_own, s_low, s_high]
@@ -215,9 +218,9 @@
     weights_d, sums_d, ps_far = block(
         scalars, images, texts, weights + [weights_c], where, tiles_d, None, [(0, 0, "text", 7, (0, 1, 2, 3), None)], [1]
     )
-    weights = [weights_a, weights_b, weights_c, weights_d]
-
-    value = jnp.sum(sums_a + sums_b + sums_c + sums_d, axis=(1, 2)).reshape(1, 3)
+    weights = [weights_a, weights_b, weights_c, weights_d, weights_z]
+
+    value = jnp.sum(sums_z + sums_a + sums_b + sums_c + sums_d, axis=(1, 2)).reshape(1, 3)
     *weights, ps_far, value = fence(*weights, narrow(ps_far), value)
     ps_far = send(ps_far, "c", SWAP)
     value = value + send(value, "c", SWAP)
@@ -252,16 +255,19 @@
         + [(n + 3, 0, "text", j, (0, 1, 2, 3), None) for n, j in enumerate((1, 2, 0))],
         outs=[1] * 6,
     )
-    *back, ps_near, pi_low, pi_high, pi_own, pt_low, pt_high, pt_own = fence(
-        *back, ps_near, pi_low, pi_high, pi_own, pt_low, pt_high, pt_own
+    pt_low = pt_low + wide(ps_near[: 2 * rows])
+    pt_high = pt_high + wide(ps_near[2 * rows : 4 * rows])
+    pt_own = pt_own + wide(ps_near[4 * rows :])
+    *back, pi_low, pi_high, pi_own, pt_low, pt_high, pt_own = fence(
+        *back, pi_low, pi_high, pi_own, pt_low, pt_high, pt_own
     )
 
     first, second = ((0, rows), (0, 0)), ((rows, 0), (0, 0))
     near = [
         narrow(pi_low + jnp.pad(wide(back[0]), first)),
         narrow(pi_high + jnp.pad(wide(back[1]), second)),
-        narrow(pt_low + wide(ps_near[: 2 * rows]) + jnp.pad(wide(back[2]), first)),
-        narrow(pt_high + wide(ps_near[2 * rows : 4 * rows]) + jnp.pad(wide(back[3]), second)),
+        narrow(pt_low + jnp.pad(wide(back[2]), first)),
+        narrow(pt_high + jnp.pad(wide(back[3]), second)),
     ]
     *near, value = fence(*near, value)
     near = [
@@ -272,13 +278,12 @@
     ]
     for axis, pairs in ((Z, EVEN), (Z, ODD), ("x", EVEN)):
         value = value + send(value, axis, pairs)
-    pt_own = pt_own + wide(ps_near[4 * rows :])
     *near, pi_own, pt_own, value = fence(*near, pi_own, pt_own, value)
     pi_own = pi_own + wide(near[0]) + wide(near[1])
     pt_own = pt_own + wide(near[2]) + wide(near[3])
 
     last = [narrow(pi_own[rows:]), narrow(pt_own[rows:])]
-    *last, value = fence(*last, value)
+    last = fence(*last)
     last = [send(last[0], Z, EVEN), send(last[1], Z, ODD)]
     value = value + send(value, "x", ODD)
     low, far, high = (send(value, "y", [(i, (i + step) % 4) for i in range(4)]) for step in (1, 2, 3))

time: 104 us -> 104 us (level)
  waiting for transfers between devices: 37.8 us -> 36.1 us
    ppermute x34, waiting for transfers between devices: 37.8 us -> 36.1 us  [send(): return lax.ppermute(value, axis, pairs)]
    ppermute x34, starting transfers between devices: 35 us -> 36 us  [send(): return lax.ppermute(value, axis, pairs)]
    pallas_call x6 -> x7, Pallas kernels: 22 us -> 22.5 us  [block(): pl.pallas_call(functools.partial(block_kernel, len(images), len(texts), l...]
  transfers between devices with their start and end apart: 34 -> 34, of which waited for: 17 -> 14; matrix products, arithmetic and copies ran while one was open for 2% -> 3% of each run, Pallas kernels for 19% -> 19%
where the time goes in v6:
time: 104 us
  waiting for transfers between devices  36.1 us (35%)
  starting transfers between devices  36 us (35%)
  Pallas kernels  22.5 us (22%)
  other arithmetic  6.03 us (6%)
  between operations  2.33 us (2%)
    ppermute x34, waiting for transfers between devices, send(): return lax.ppermute(value, axis, pairs)  36.1 us
    ppermute x34, starting transfers between devices, send(): return lax.ppermute(value, axis, pairs)  36 us
    pallas_call x7, Pallas kernels, block(): pl.pallas_call(functools.partial(block_kernel, len(images), len(texts), l...  22.5 us
  transfers between devices with their start and end apart: 34, of which 14 were waited for; matrix products, arithmetic and copies ran while one was open for 3% of the time, Pallas kernels for 19%

profile of v6, /device:TPU:6, one launch (start us, length us, event | category | flops | bytes accessed | tf_op | source)
XLA Modules:
  0.0 103.7 jit_solution(14857496909367957587)
XLA Ops:
  0.6 1.1 %pad_maximum_fusion.1 = bf16[256,1152]{1,0:T(8,128)(2,1)S(1)} fusion(bf16[128,1152]{1,0:T(8,128)(2,1)} %param.5, bf16[128,1152]{1,0:T(8,128)(2,1)} %param.4), kind=kLoop, calls=%fused_computation.20 | loop fusion | flops 1179648 | bytes 1179648 | tf_op jit(solution)/shard_map/concatenate | solution.py:145
  1.7 0.2 fusion
  1.9 0.2 fusion.4
  2.2 4.1 %collective-permute-start.1 = (bf16[128,1152]{1,0:T(8,128)(2,1)S(1)}, bf16[128,1152]{1,0:T(8,128)(2,1)S(1)}, u32[]{:S(2)}, u32[]{:S(2)}) collective-permute-start(bf16[128,1152]{1,0:T(8,128)(2,1)S(1)} %get-tuple-element.194), channel_id=1, source_target_pairs={{2,4},{4,2},{6,0},{0,6},{3,5},{5,3},{7,1},{1,7},{10,12},{12,10},{1... | collective-permute-start | bytes 884744 | tf_op jit(solution)/shard_map/ppermute | solution.py:25
  6.3 7.0 %collective-permute-done.1 = bf16[128,1152]{1,0:T(8,128)(2,1)S(1)} collective-permute-done((bf16[128,1152]{1,0:T(8,128)(2,1)S(1)}, bf16[128,1152]{1,0:T(8,128)(2,1)S(1)}, u32[]{:S(2)}, u32[]{:S(2)}) %collective-permute-start.1) | collective-permute-done | bytes 294944 | tf_op jit(solution)/shard_map/ppermute | solution.py:25
  13.4 1.6 %collective-permute-start.4 = (bf16[256,1152]{1,0:T(8,128)(2,1)S(1)}, bf16[256,1152]{1,0:T(8,128)(2,1)S(1)}, u32[]{:S(2)}, u32[]{:S(2)}) collective-permute-start(bf16[256,1152]{1,0:T(8,128)(2,1)S(1)} %pad_maximum_fusion.3.refs_2_.refs_4_.refs_5_), channel_id=1, source_target_pairs={{0,32},{32,64},{64,96},{96,0},{1,33},{33,65},{65,97},{97,1},{2,34}... | collective-permute-start | bytes 1769480 | tf_op jit(solution)/shard_map/ppermute | solution.py:25
  15.0 1.7 %collective-permute-start.5 = (bf16[256,1152]{1,0:T(8,128)(2,1)S(1)}, bf16[256,1152]{1,0:T(8,128)(2,1)S(1)}, u32[]{:S(2)}, u32[]{:S(2)}) collective-permute-start(bf16[256,1152]{1,0:T(8,128)(2,1)S(1)} %pad_maximum_fusion.3.refs_2_.refs_4_.refs_5_), channel_id=1, source_target_pairs={{0,96},{32,0},{64,32},{96,64},{1,97},{33,1},{65,33},{97,65},{2,98}... | collective-permute-start | bytes 1769480 | tf_op jit(solution)/shard_map/ppermute | solution.py:25
  16.7 0.5 collective-permute-start.2
  17.3 1.5 %collective-permute-start.3 = (bf16[256,1152]{1,0:T(8,128)(2,1)S(1)}, bf16[256,1152]{1,0:T(8,128)(2,1)S(1)}, u32[]{:S(2)}, u32[]{:S(2)}) collective-permute-start(bf16[256,1152]{1,0:T(8,128)(2,1)S(1)} %pad_maximum_fusion.2.refs_1_.refs_0_), channel_id=1, source_target_pairs={{0,24},{8,0},{16,8},{24,16},{1,25},{9,1},{17,9},{25,17},{2,26},{10... | collective-permute-start | bytes 1769480 | tf_op jit(solution)/shard_map/ppermute | solution.py:25
  20.2 1.0 shard_map.67
  21.3 7.9 %collective-permute-done.4.refs_5_.refs_6_ = bf16[256,1152]{1,0:T(8,128)(2,1)S(1)} collective-permute-done((bf16[256,1152]{1,0:T(8,128)(2,1)S(1)}, bf16[256,1152]{1,0:T(8,128)(2,1)S(1)}, u32[]{:S(2)}, u32[]{:S(2)}) %collective-permute-start.4) | collective-permute-done | bytes 589856 | tf_op jit(solution)/shard_map/ppermute | solution.py:25
  29.2 1.6 %collective-permute-done.2.refs_2_.refs_1_ = bf16[256,1152]{1,0:T(8,128)(2,1)S(1)} collective-permute-done((bf16[256,1152]{1,0:T(8,128)(2,1)S(1)}, bf16[256,1152]{1,0:T(8,128)(2,1)S(1)}, u32[]{:S(2)}, u32[]{:S(2)}) %collective-permute-start.2) | collective-permute-done | bytes 589856 | tf_op jit(solution)/shard_map/ppermute | solution.py:25
  30.9 1.4 %collective-permute-done.3.refs_3_.refs_2_ = bf16[256,1152]{1,0:T(8,128)(2,1)S(1)} collective-permute-done((bf16[256,1152]{1,0:T(8,128)(2,1)S(1)}, bf16[256,1152]{1,0:T(8,128)(2,1)S(1)}, u32[]{:S(2)}, u32[]{:S(2)}) %collective-permute-start.3) | collective-permute-done | bytes 589856 | tf_op jit(solution)/shard_map/ppermute | solution.py:25
  32.3 0.1 pad_maximum_fusion
  32.6 0.3 collective-permute-start.10
  32.8 3.0 %collective-permute-start.11 = (bf16[128,1152]{1,0:T(8,128)(2,1)S(1)}, bf16[128,1152]{1,0:T(8,128)(2,1)S(1)}, u32[]{:S(2)}, u32[]{:S(2)}) collective-permute-start(bf16[128,1152]{1,0:T(8,128)(2,1)S(1)} %slice.78), channel_id=1, source_target_pairs={{0,96},{32,0},{64,32},{96,64},{1,97},{33,1},{65,33},{97,65},{2,98}... | collective-permute-start | bytes 884744 | tf_op jit(solution)/shard_map/ppermute | solution.py:25
  35.9 0.4 collective-permute-start.8
  36.3 1.8 %collective-permute-start.9 = (bf16[128,1152]{1,0:T(8,128)(2,1)S(1)}, bf16[128,1152]{1,0:T(8,128)(2,1)S(1)}, u32[]{:S(2)}, u32[]{:S(2)}) collective-permute-start(bf16[128,1152]{1,0:T(8,128)(2,1)S(1)} %slice.76), channel_id=1, source_target_pairs={{0,24},{8,0},{16,8},{24,16},{1,25},{9,1},{17,9},{25,17},{2,26},{10... | collective-permute-start | bytes 884744 | tf_op jit(solution)/shard_map/ppermute | solution.py:25
  38.1 3.3 %shard_map.68 = (bf16[11,256,256]{2,1,0:T(8,128)(2,1)S(1)}, f32[3,8,256]{2,1,0:T(8,128)S(1)}) custom-call(f32[2]{0:T(128)S(1)} %pad_maximum_fusion.4.refs_0_, bf16[256,1152]{1,0:T(8,128)(2,1)S(1)} %pad_maximum_fusion.2.refs_1_.refs_0_, bf16[256,1152]{1,0:T(8,128)(2,1)S(1)} %collective-permute-done.2.refs_2_.refs_1_, ...), custom_call_target="tpu_custom_call" | custom-call | flops 1 | bytes 1 | tf_op jit(solution)/shard_map/pallas_call | solution.py:113
  41.5 0.1 fusion.5
  41.6 3.7 %shard_map.69 = (bf16[6,256,256]{2,1,0:T(8,128)(2,1)S(1)}, f32[3,8,256]{2,1,0:T(8,128)S(1)}, f32[768,1152]{1,0:T(8,128)S(1)}) custom-call(f32[2]{0:T(128)S(1)} %pad_maximum_fusion.4.refs_0_, bf16[256,1152]{1,0:T(8,128)(2,1)S(1)} %pad_maximum_fusion.2.refs_1_.refs_0_, bf16[256,1152]{1,0:T(8,128)(2,1)S(1)} %collective-permute-done.2.refs_2_.refs_1_, ...), custom_call_target="tpu_custom_call" | custom-call | flops 1 | bytes 1 | tf_op jit(solution)/shard_map/pallas_call | solution.py:113
  45.3 0.8 collective-permute-done.9
  46.2 0.3 collective-permute-start.13
  46.5 4.7 %shard_map.70 = (bf16[10,256,256]{2,1,0:T(8,128)(2,1)S(1)}, f32[3,8,256]{2,1,0:T(8,128)S(1)}, f32[256,1152]{1,0:T(8,128)S(1)}, f32[256,1152]{1,0:T(8,128)S(1)}) custom-call(f32[2]{0:T(128)S(1)} %pad_maximum_fusion.4.refs_0_, bf16[256,1152]{1,0:T(8,128)(2,1)S(1)} %pad_maximum_fusion.2.refs_1_.refs_0_, ...), custom_call_target="tpu_custom_call" | custom-call | flops 1 | bytes 1 | tf_op jit(solution)/shard_map/pallas_call | solution.py:113
  51.3 2.5 %shard_map.71 = (bf16[4,256,256]{2,1,0:T(8,128)(2,1)S(1)}, f32[3,8,256]{2,1,0:T(8,128)S(1)}, f32[256,1152]{1,0:T(8,128)S(1)}) custom-call(f32[2]{0:T(128)S(1)} %pad_maximum_fusion.4.refs_0_, bf16[256,1152]{1,0:T(8,128)(2,1)S(1)} %pad_maximum_fusion.2.refs_1_.refs_0_, bf16[256,1152]{1,0:T(8,128)(2,1)S(1)} %collective-permute-done.2.refs_2_.refs_1_, ...), custom_call_target="tpu_custom_call" | custom-call | flops 1 | bytes 1 | tf_op jit(solution)/shard_map/pallas_call | solution.py:113
  53.9 0.1 add_reduce_fusion
  54.0 0.5 collective-permute-start.14
  54.5 0.1 collective-permute-start.15
  54.6 0.9 shard_map.72
  55.5 0.2 convert_element_type.78
  55.8 0.3 collective-permute-done.15
  56.1 0.1 add_convert_fusion.4
  56.3 0.5 collective-permute-start.20
  56.7 0.1 fusion.7
  56.8 0.6 collective-permute-start.16
  57.4 2.7 %collective-permute-start.17 = (f16[128,1152]{1,0:T(8,128)(2,1)S(1)}, f16[128,1152]{1,0:T(8,128)(2,1)S(1)}, u32[]{:S(2)}, u32[]{:S(2)}) collective-permute-start(f16[128,1152]{1,0:T(8,128)(2,1)S(1)} %get-tuple-element.192), channel_id=1, source_target_pairs={{0,8},{8,16},{16,24},{24,0},{1,9},{9,17},{17,25},{25,1},{2,10},{10... | collective-permute-start | bytes 884744 | tf_op jit(solution)/shard_map/ppermute | solution.py:25
  60.1 0.1 fusion.6
  60.2 0.5 collective-permute-start.18
  60.8 1.6 %collective-permute-start.19 = (f16[128,1152]{1,0:T(8,128)(2,1)S(1)}, f16[128,1152]{1,0:T(8,128)(2,1)S(1)}, u32[]{:S(2)}, u32[]{:S(2)}) collective-permute-start(f16[128,1152]{1,0:T(8,128)(2,1)S(1)} %get-tuple-element.190), channel_id=1, source_target_pairs={{0,32},{32,64},{64,96},{96,0},{1,33},{33,65},{65,97},{97,1},{2,34}... | collective-permute-start | bytes 884744 | tf_op jit(solution)/shard_map/ppermute | solution.py:25
  62.3 6.3 %shard_map.73 = (f32[256,1152]{1,0:T(8,128)S(1)}, f32[256,1152]{1,0:T(8,128)S(1)}, f32[256,1152]{1,0:T(8,128)S(1)}, f32[256,1152]{1,0:T(8,128)S(1)}, f32[256,1152]{1,0:T(8,128)S(1)}, /*index=5*/f32[256,1152]{1,0:T(8,128)S(1)}) custom-call(bf16[256,1152]{1,0:T(8,128)(2,1)S(1)} %pad_maximum_fusion.2.refs_1_.refs_0_, ...), custom_call_target="tpu_custom_call" | custom-call | flops 1 | bytes 1 | tf_op jit(solution)/shard_map/pallas_call | solution.py:113
  68.7 0.4 convert_add_fusion.2
  69.1 1.2 %collective-permute-done.19 = f16[128,1152]{1,0:T(8,128)(2,1)S(1)} collective-permute-done((f16[128,1152]{1,0:T(8,128)(2,1)S(1)}, f16[128,1152]{1,0:T(8,128)(2,1)S(1)}, u32[]{:S(2)}, u32[]{:S(2)}) %collective-permute-start.19) | collective-permute-done | bytes 294944 | tf_op jit(solution)/shard_map/ppermute | solution.py:25
  70.3 0.3 add_convert_fusion
  70.6 0.2 add_convert_fusion.2
  70.9 3.2 %collective-permute-start.22 = (f16[256,1152]{1,0:T(8,128)(2,1)S(1)}, f16[256,1152]{1,0:T(8,128)(2,1)S(1)}, u32[]{:S(2)}, u32[]{:S(2)}) collective-permute-start(f16[256,1152]{1,0:T(8,128)(2,1)S(1)} %get-tuple-element.158), channel_id=1, source_target_pairs={{0,8},{8,16},{16,24},{24,0},{1,9},{9,17},{17,25},{25,1},{2,10},{10... | collective-permute-start | bytes 1769480 | tf_op jit(solution)/shard_map/ppermute | solution.py:25
  74.2 0.5 collective-permute-start.23
  74.6 1.5 %collective-permute-start.24 = (f16[256,1152]{1,0:T(8,128)(2,1)S(1)}, f16[256,1152]{1,0:T(8,128)(2,1)S(1)}, u32[]{:S(2)}, u32[]{:S(2)}) collective-permute-start(f16[256,1152]{1,0:T(8,128)(2,1)S(1)} %get-tuple-element.160), channel_id=1, source_target_pairs={{0,32},{32,64},{64,96},{96,0},{1,33},{33,65},{65,97},{97,1},{2,34}... | collective-permute-start | bytes 1769480 | tf_op jit(solution)/shard_map/ppermute | solution.py:25
  76.2 3.5 %collective-permute-done.25 = f32[1,3]{1,0:T(1,128)S(1)} collective-permute-done((f32[1,3]{1,0:T(1,128)S(1)}, f32[1,3]{1,0:T(1,128)S(1)}, u32[]{:S(2)}, u32[]{:S(2)}) %collective-permute-start.25) | collective-permute-done | bytes 44 | tf_op jit(solution)/shard_map/ppermute | solution.py:25
  79.7 2.6 %collective-permute-start.26 = (f32[1,3]{1,0:T(1,128)S(1)}, f32[1,3]{1,0:T(1,128)S(1)}, u32[]{:S(2)}, u32[]{:S(2)}) collective-permute-start(f32[1,3]{1,0:T(1,128)S(1)} %add.117), channel_id=1, source_target_pairs={{2,4},{4,2},{6,0},{0,6},{3,5},{5,3},{7,1},{1,7},{10,12},{12,10},{1... | collective-permute-start | bytes 44 | tf_op jit(solution)/shard_map/ppermute | solution.py:25
  82.3 2.1 %collective-permute-done.26 = f32[1,3]{1,0:T(1,128)S(1)} collective-permute-done((f32[1,3]{1,0:T(1,128)S(1)}, f32[1,3]{1,0:T(1,128)S(1)}, u32[]{:S(2)}, u32[]{:S(2)}) %collective-permute-start.26) | collective-permute-done | bytes 44 | tf_op jit(solution)/shard_map/ppermute | solution.py:25
  84.5 3.5 %collective-permute-done.27 = f32[1,3]{1,0:T(1,128)S(1)} collective-permute-done((f32[1,3]{1,0:T(1,128)S(1)}, f32[1,3]{1,0:T(1,128)S(1)}, u32[]{:S(2)}, u32[]{:S(2)}) %collective-permute-start.27) | collective-permute-done | bytes 44 | tf_op jit(solution)/shard_map/ppermute | solution.py:25
  88.0 1.3 %collective-permute-done.24 = f16[256,1152]{1,0:T(8,128)(2,1)S(1)} collective-permute-done((f16[256,1152]{1,0:T(8,128)(2,1)S(1)}, f16[256,1152]{1,0:T(8,128)(2,1)S(1)}, u32[]{:S(2)}, u32[]{:S(2)}) %collective-permute-start.24) | collective-permute-done | bytes 589856 | tf_op jit(solution)/shard_map/ppermute | solution.py:25
  89.4 0.2 convert_add_fusion
  89.6 0.2 convert_add_fusion.1
  90.0 2.7 %collective-permute-start.29 = (f16[128,1152]{1,0:T(8,128)(2,1)S(1)}, f16[128,1152]{1,0:T(8,128)(2,1)S(1)}, u32[]{:S(2)}, u32[]{:S(2)}) collective-permute-start(f16[128,1152]{1,0:T(8,128)(2,1)S(1)} %slice_convert_fusion), channel_id=1, source_target_pairs={{2,4},{4,2},{6,0},{0,6},{3,5},{5,3},{7,1},{1,7},{10,12},{12,10},{1... | collective-permute-start | bytes 884744 | tf_op jit(solution)/shard_map/ppermute | solution.py:25
  92.7 0.3 collective-permute-start.30
  93.0 4.5 %collective-permute-done.30 = f32[1,3]{1,0:T(1,128)S(1)} collective-permute-done((f32[1,3]{1,0:T(1,128)S(1)}, f32[1,3]{1,0:T(1,128)S(1)}, u32[]{:S(2)}, u32[]{:S(2)}) %collective-permute-start.30) | collective-permute-done | bytes 44 | tf_op jit(solution)/shard_map/ppermute | solution.py:25
  97.5 1.8 %collective-permute-start.32 = (f32[1,3]{1,0:T(1,128)S(1)}, f32[1,3]{1,0:T(1,128)S(1)}, u32[]{:S(2)}, u32[]{:S(2)}) collective-permute-start(f32[1,3]{1,0:T(1,128)S(1)} %add.126), channel_id=1, source_target_pairs={{0,64},{32,96},{64,0},{96,32},{1,65},{33,97},{65,1},{97,33},{2,66}... | collective-permute-start | bytes 44 | tf_op jit(solution)/shard_map/ppermute | solution.py:25
  99.3 1.4 %collective-permute-start.33 = (f32[1,3]{1,0:T(1,128)S(1)}, f32[1,3]{1,0:T(1,128)S(1)}, u32[]{:S(2)}, u32[]{:S(2)}) collective-permute-start(f32[1,3]{1,0:T(1,128)S(1)} %add.126), channel_id=1, source_target_pairs={{0,96},{32,0},{64,32},{96,64},{1,97},{33,1},{65,33},{97,65},{2,98}... | collective-permute-start | bytes 44 | tf_op jit(solution)/shard_map/ppermute | solution.py:25
  100.7 0.3 multiply_reduce_fusion
  101.0 1.3 %subtract_multiply_fusion = (f32[128,1152]{1,0:T(8,128)}, f32[128,1152]{1,0:T(8,128)}) fusion(f32[256,1152]{1,0:T(8,128)S(1)} %get-tuple-element.189, f16[128,1152]{1,0:T(8,128)(2,1)S(1)} %collective-permute-done.29, f32[256,1152]{1,0:T(8,128)S(1)} %convert_add_fusion, f32[128]{0:T(128)S(1)} %get-tuple-element.196, f32[128]{0:T(128)S(1)} %get-tuple-element.179, ...), kind=kLoop, calls=%fused_computation.23 | loop fusion | flops 1769472 | bytes 4130820 | tf_op jit(solution)/shard_map/mul | solution.py:40
  102.4 0.1 collective-permute-done.32
  102.5 0.6 collective-permute-done.33
  103.1 0.6 fusion.3
  (54 shorter events, 1.0 us)
Async XLA Ops:
  2.2 11.1 %collective-permute-start.1 = (bf16[128,1152]{1,0:T(8,128)(2,1)S(1)}, bf16[128,1152]{1,0:T(8,128)(2,1)S(1)}, u32[]{:S(2)}, u32[]{:S(2)}) collective-permute-start(bf16[128,1152]{1,0:T(8,128)(2,1)S(1)} %get-tuple-element.194), channel_id=1, source_target_pairs={{2,4},{4,2},{6,0},{0,6},{3,5},{5,3},{7,1},{1,7},{10,12},{12,10},{1... | collective-permute-start | bytes 884744 | tf_op jit(solution)/shard_map/ppermute | solution.py:25
  6.3 10.4 %collective-permute-start = (bf16[128,1152]{1,0:T(8,128)(2,1)S(1)}, bf16[128,1152]{1,0:T(8,128)(2,1)S(1)}, u32[]{:S(2)}, u32[]{:S(2)}) collective-permute-start(bf16[128,1152]{1,0:T(8,128)(2,1)S(1)} %get-tuple-element.195), channel_id=1, source_target_pairs={{0,2},{2,0},{4,6},{6,4},{1,3},{3,1},{5,7},{7,5},{8,10},{10,8},{12,... | collective-permute-start | bytes 884744 | tf_op jit(solution)/shard_map/ppermute | solution.py:25
  6.3 12.5 %collective-permute-start.6 = (bf16[128,1152]{1,0:T(8,128)(2,1)S(1)}, bf16[128,1152]{1,0:T(8,128)(2,1)S(1)}, u32[]{:S(2)}, u32[]{:S(2)}) collective-permute-start(bf16[128,1152]{1,0:T(8,128)(2,1)S(1)} %get-tuple-element.194), channel_id=1, source_target_pairs={{0,1},{1,0},{2,3},{3,2},{4,5},{5,4},{6,7},{7,6},{8,9},{9,8},{10,11... | collective-permute-start | bytes 884744 | tf_op jit(solution)/shard_map/ppermute | solution.py:25
  13.4 15.9 %collective-permute-start.4 = (bf16[256,1152]{1,0:T(8,128)(2,1)S(1)}, bf16[256,1152]{1,0:T(8,128)(2,1)S(1)}, u32[]{:S(2)}, u32[]{:S(2)}) collective-permute-start(bf16[256,1152]{1,0:T(8,128)(2,1)S(1)} %pad_maximum_fusion.3.refs_2_.refs_4_.refs_5_), channel_id=1, source_target_pairs={{0,32},{32,64},{64,96},{96,0},{1,33},{33,65},{65,97},{97,1},{2,34}... | collective-permute-start | bytes 1769480 | tf_op jit(solution)/shard_map/ppermute | solution.py:25
  15.0 14.2 %collective-permute-start.5 = (bf16[256,1152]{1,0:T(8,128)(2,1)S(1)}, bf16[256,1152]{1,0:T(8,128)(2,1)S(1)}, u32[]{:S(2)}, u32[]{:S(2)}) collective-permute-start(bf16[256,1152]{1,0:T(8,128)(2,1)S(1)} %pad_maximum_fusion.3.refs_2_.refs_4_.refs_5_), channel_id=1, source_target_pairs={{0,96},{32,0},{64,32},{96,64},{1,97},{33,1},{65,33},{97,65},{2,98}... | collective-permute-start | bytes 1769480 | tf_op jit(solution)/shard_map/ppermute | solution.py:25
  16.7 14.2 %collective-permute-start.2 = (bf16[256,1152]{1,0:T(8,128)(2,1)S(1)}, bf16[256,1152]{1,0:T(8,128)(2,1)S(1)}, u32[]{:S(2)}, u32[]{:S(2)}) collective-permute-start(bf16[256,1152]{1,0:T(8,128)(2,1)S(1)} %pad_maximum_fusion.2.refs_1_.refs_0_), channel_id=1, source_target_pairs={{0,8},{8,16},{16,24},{24,0},{1,9},{9,17},{17,25},{25,1},{2,10},{10... | collective-permute-start | bytes 1769480 | tf_op jit(solution)/shard_map/ppermute | solution.py:25
  17.3 15.0 %collective-permute-start.3 = (bf16[256,1152]{1,0:T(8,128)(2,1)S(1)}, bf16[256,1152]{1,0:T(8,128)(2,1)S(1)}, u32[]{:S(2)}, u32[]{:S(2)}) collective-permute-start(bf16[256,1152]{1,0:T(8,128)(2,1)S(1)} %pad_maximum_fusion.2.refs_1_.refs_0_), channel_id=1, source_target_pairs={{0,24},{8,0},{16,8},{24,16},{1,25},{9,1},{17,9},{25,17},{2,26},{10... | collective-permute-start | bytes 1769480 | tf_op jit(solution)/shard_map/ppermute | solution.py:25
  18.8 2.5 %collective-permute-start.7 = (bf16[128,1152]{1,0:T(8,128)(2,1)S(1)}, bf16[128,1152]{1,0:T(8,128)(2,1)S(1)}, u32[]{:S(2)}, u32[]{:S(2)}) collective-permute-start(bf16[128,1152]{1,0:T(8,128)(2,1)S(1)} %collective-permute-done.1), channel_id=1, source_target_pairs={{0,1},{1,0},{2,3},{3,2},{4,5},{5,4},{6,7},{7,6},{8,9},{9,8},{10,11... | collective-permute-start | bytes 884744 | tf_op jit(solution)/shard_map/ppermute | solution.py:25
  32.4 9.1 %collective-permute-start.12 = (bf16[512,1152]{1,0:T(8,128)(2,1)S(1)}, bf16[512,1152]{1,0:T(8,128)(2,1)S(1)}, u32[]{:S(2)}, u32[]{:S(2)}) collective-permute-start(bf16[512,1152]{1,0:T(8,128)(2,1)S(1)} %pad_maximum_fusion), channel_id=1, source_target_pairs={{0,1},{1,0},{2,3},{3,2},{4,5},{5,4},{6,7},{7,6},{8,9},{9,8},{10,11... | collective-permute-start | bytes 3538952 | tf_op jit(solution)/shard_map/ppermute | solution.py:25
  32.6 12.7 %collective-permute-start.10 = (bf16[128,1152]{1,0:T(8,128)(2,1)S(1)}, bf16[128,1152]{1,0:T(8,128)(2,1)S(1)}, u32[]{:S(2)}, u32[]{:S(2)}) collective-permute-start(bf16[128,1152]{1,0:T(8,128)(2,1)S(1)} %slice.77), channel_id=1, source_target_pairs={{0,32},{32,64},{64,96},{96,0},{1,33},{33,65},{65,97},{97,1},{2,34}... | collective-permute-start | bytes 884744 | tf_op jit(solution)/shard_map/ppermute | solution.py:25
  32.8 12.4 %collective-permute-start.11 = (bf16[128,1152]{1,0:T(8,128)(2,1)S(1)}, bf16[128,1152]{1,0:T(8,128)(2,1)S(1)}, u32[]{:S(2)}, u32[]{:S(2)}) collective-permute-start(bf16[128,1152]{1,0:T(8,128)(2,1)S(1)} %slice.78), channel_id=1, source_target_pairs={{0,96},{32,0},{64,32},{96,64},{1,97},{33,1},{65,33},{97,65},{2,98}... | collective-permute-start | bytes 884744 | tf_op jit(solution)/shard_map/ppermute | solution.py:25
  35.9 9.4 %collective-permute-start.8 = (bf16[128,1152]{1,0:T(8,128)(2,1)S(1)}, bf16[128,1152]{1,0:T(8,128)(2,1)S(1)}, u32[]{:S(2)}, u32[]{:S(2)}) collective-permute-start(bf16[128,1152]{1,0:T(8,128)(2,1)S(1)} %slice.75), channel_id=1, source_target_pairs={{0,8},{8,16},{16,24},{24,0},{1,9},{9,17},{17,25},{25,1},{2,10},{10... | collective-permute-start | bytes 884744 | tf_op jit(solution)/shard_map/ppermute | solution.py:25
  36.3 9.9 %collective-permute-start.9 = (bf16[128,1152]{1,0:T(8,128)(2,1)S(1)}, bf16[128,1152]{1,0:T(8,128)(2,1)S(1)}, u32[]{:S(2)}, u32[]{:S(2)}) collective-permute-start(bf16[128,1152]{1,0:T(8,128)(2,1)S(1)} %slice.76), channel_id=1, source_target_pairs={{0,24},{8,0},{16,8},{24,16},{1,25},{9,1},{17,9},{25,17},{2,26},{10... | collective-permute-start | bytes 884744 | tf_op jit(solution)/shard_map/ppermute | solution.py:25
  46.2 5.1 %collective-permute-start.13 = (bf16[256,1152]{1,0:T(8,128)(2,1)S(1)}, bf16[256,1152]{1,0:T(8,128)(2,1)S(1)}, u32[]{:S(2)}, u32[]{:S(2)}) collective-permute-start(bf16[256,1152]{1,0:T(8,128)(2,1)S(1)} %constant_dynamic-update-slice_fusion.4.refs_11_.refs_10_), channel_id=1, source_target_pairs={{0,1},{1,0},{2,3},{3,2},{4,5},{5,4},{6,7},{7,6},{8,9},{9,8},{10,11... | collective-permute-start | bytes 1769480 | tf_op jit(solution)/shard_map/ppermute | solution.py:25
  54.0 2.2 %collective-permute-start.14 = (f16[256,1152]{1,0:T(8,128)(2,1)S(1)}, f16[256,1152]{1,0:T(8,128)(2,1)S(1)}, u32[]{:S(2)}, u32[]{:S(2)}) collective-permute-start(f16[256,1152]{1,0:T(8,128)(2,1)S(1)} %convert_element_type.74), channel_id=1, source_target_pairs={{0,1},{1,0},{2,3},{3,2},{4,5},{5,4},{6,7},{7,6},{8,9},{9,8},{10,11... | collective-permute-start | bytes 1769480 | tf_op jit(solution)/shard_map/ppermute | solution.py:25
  54.5 1.6 %collective-permute-start.15 = (f32[1,3]{1,0:T(1,128)S(1)}, f32[1,3]{1,0:T(1,128)S(1)}, u32[]{:S(2)}, u32[]{:S(2)}) collective-permute-start(f32[1,3]{1,0:T(1,128)S(1)} %bitcast.4), channel_id=1, source_target_pairs={{0,1},{1,0},{2,3},{3,2},{4,5},{5,4},{6,7},{7,6},{8,9},{9,8},{10,11... | collective-permute-start | bytes 44 | tf_op jit(solution)/shard_map/ppermute | solution.py:25
  56.3 12.4 %collective-permute-start.20 = (f16[768,1152]{1,0:T(8,128)(2,1)S(1)}, f16[768,1152]{1,0:T(8,128)(2,1)S(1)}, u32[]{:S(2)}, u32[]{:S(2)}) collective-permute-start(f16[768,1152]{1,0:T(8,128)(2,1)S(1)} %convert_element_type.78), channel_id=1, source_target_pairs={{0,1},{1,0},{2,3},{3,2},{4,5},{5,4},{6,7},{7,6},{8,9},{9,8},{10,11... | collective-permute-start | bytes 5308424 | tf_op jit(solution)/shard_map/ppermute | solution.py:25
  56.8 12.3 %collective-permute-start.16 = (f16[128,1152]{1,0:T(8,128)(2,1)S(1)}, f16[128,1152]{1,0:T(8,128)(2,1)S(1)}, u32[]{:S(2)}, u32[]{:S(2)}) collective-permute-start(f16[128,1152]{1,0:T(8,128)(2,1)S(1)} %get-tuple-element.193), channel_id=1, source_target_pairs={{0,24},{8,0},{16,8},{24,16},{1,25},{9,1},{17,9},{25,17},{2,26},{10... | collective-permute-start | bytes 884744 | tf_op jit(solution)/shard_map/ppermute | solution.py:25
  57.4 11.7 %collective-permute-start.17 = (f16[128,1152]{1,0:T(8,128)(2,1)S(1)}, f16[128,1152]{1,0:T(8,128)(2,1)S(1)}, u32[]{:S(2)}, u32[]{:S(2)}) collective-permute-start(f16[128,1152]{1,0:T(8,128)(2,1)S(1)} %get-tuple-element.192), channel_id=1, source_target_pairs={{0,8},{8,16},{16,24},{24,0},{1,9},{9,17},{17,25},{25,1},{2,10},{10... | collective-permute-start | bytes 884744 | tf_op jit(solution)/shard_map/ppermute | solution.py:25
  60.2 8.9 %collective-permute-start.18 = (f16[128,1152]{1,0:T(8,128)(2,1)S(1)}, f16[128,1152]{1,0:T(8,128)(2,1)S(1)}, u32[]{:S(2)}, u32[]{:S(2)}) collective-permute-start(f16[128,1152]{1,0:T(8,128)(2,1)S(1)} %get-tuple-element.191), channel_id=1, source_target_pairs={{0,96},{32,0},{64,32},{96,64},{1,97},{33,1},{65,33},{97,65},{2,98}... | collective-permute-start | bytes 884744 | tf_op jit(solution)/shard_map/ppermute | solution.py:25
  60.8 9.6 %collective-permute-start.19 = (f16[128,1152]{1,0:T(8,128)(2,1)S(1)}, f16[128,1152]{1,0:T(8,128)(2,1)S(1)}, u32[]{:S(2)}, u32[]{:S(2)}) collective-permute-start(f16[128,1152]{1,0:T(8,128)(2,1)S(1)} %get-tuple-element.190), channel_id=1, source_target_pairs={{0,32},{32,64},{64,96},{96,0},{1,33},{33,65},{65,97},{97,1},{2,34}... | collective-permute-start | bytes 884744 | tf_op jit(solution)/shard_map/ppermute | solution.py:25
  70.8 17.2 %collective-permute-start.21 = (f16[256,1152]{1,0:T(8,128)(2,1)S(1)}, f16[256,1152]{1,0:T(8,128)(2,1)S(1)}, u32[]{:S(2)}, u32[]{:S(2)}) collective-permute-start(f16[256,1152]{1,0:T(8,128)(2,1)S(1)} %get-tuple-element.157), channel_id=1, source_target_pairs={{0,24},{8,0},{16,8},{24,16},{1,25},{9,1},{17,9},{25,17},{2,26},{10... | collective-permute-start | bytes 1769480 | tf_op jit(solution)/shard_map/ppermute | solution.py:25
  70.9 17.1 %collective-permute-start.22 = (f16[256,1152]{1,0:T(8,128)(2,1)S(1)}, f16[256,1152]{1,0:T(8,128)(2,1)S(1)}, u32[]{:S(2)}, u32[]{:S(2)}) collective-permute-start(f16[256,1152]{1,0:T(8,128)(2,1)S(1)} %get-tuple-element.158), channel_id=1, source_target_pairs={{0,8},{8,16},{16,24},{24,0},{1,9},{9,17},{17,25},{25,1},{2,10},{10... | collective-permute-start | bytes 1769480 | tf_op jit(solution)/shard_map/ppermute | solution.py:25
  74.2 13.9 %collective-permute-start.23 = (f16[256,1152]{1,0:T(8,128)(2,1)S(1)}, f16[256,1152]{1,0:T(8,128)(2,1)S(1)}, u32[]{:S(2)}, u32[]{:S(2)}) collective-permute-start(f16[256,1152]{1,0:T(8,128)(2,1)S(1)} %get-tuple-element.159), channel_id=1, source_target_pairs={{0,96},{32,0},{64,32},{96,64},{1,97},{33,1},{65,33},{97,65},{2,98}... | collective-permute-start | bytes 1769480 | tf_op jit(solution)/shard_map/ppermute | solution.py:25
  74.6 14.8 %collective-permute-start.24 = (f16[256,1152]{1,0:T(8,128)(2,1)S(1)}, f16[256,1152]{1,0:T(8,128)(2,1)S(1)}, u32[]{:S(2)}, u32[]{:S(2)}) collective-permute-start(f16[256,1152]{1,0:T(8,128)(2,1)S(1)} %get-tuple-element.160), channel_id=1, source_target_pairs={{0,32},{32,64},{64,96},{96,0},{1,33},{33,65},{65,97},{97,1},{2,34}... | collective-permute-start | bytes 1769480 | tf_op jit(solution)/shard_map/ppermute | solution.py:25
  76.2 3.5 %collective-permute-start.25 = (f32[1,3]{1,0:T(1,128)S(1)}, f32[1,3]{1,0:T(1,128)S(1)}, u32[]{:S(2)}, u32[]{:S(2)}) collective-permute-start(f32[1,3]{1,0:T(1,128)S(1)} %add.109), channel_id=1, source_target_pairs={{0,2},{2,0},{4,6},{6,4},{1,3},{3,1},{5,7},{7,5},{8,10},{10,8},{12,... | collective-permute-start | bytes 44 | tf_op jit(solution)/shard_map/ppermute | solution.py:25
  79.7 4.8 %collective-permute-start.26 = (f32[1,3]{1,0:T(1,128)S(1)}, f32[1,3]{1,0:T(1,128)S(1)}, u32[]{:S(2)}, u32[]{:S(2)}) collective-permute-start(f32[1,3]{1,0:T(1,128)S(1)} %add.117), channel_id=1, source_target_pairs={{2,4},{4,2},{6,0},{0,6},{3,5},{5,3},{7,1},{1,7},{10,12},{12,10},{1... | collective-permute-start | bytes 44 | tf_op jit(solution)/shard_map/ppermute | solution.py:25
  84.5 3.5 %collective-permute-start.27 = (f32[1,3]{1,0:T(1,128)S(1)}, f32[1,3]{1,0:T(1,128)S(1)}, u32[]{:S(2)}, u32[]{:S(2)}) collective-permute-start(f32[1,3]{1,0:T(1,128)S(1)} %add.118), channel_id=1, source_target_pairs={{0,8},{8,0},{16,24},{24,16},{1,9},{9,1},{17,25},{25,17},{2,10},{10... | collective-permute-start | bytes 44 | tf_op jit(solution)/shard_map/ppermute | solution.py:25
  89.9 10.8 %collective-permute-start.28 = (f16[128,1152]{1,0:T(8,128)(2,1)S(1)}, f16[128,1152]{1,0:T(8,128)(2,1)S(1)}, u32[]{:S(2)}, u32[]{:S(2)}) collective-permute-start(f16[128,1152]{1,0:T(8,128)(2,1)S(1)} %slice_convert_fusion.1), channel_id=1, source_target_pairs={{0,2},{2,0},{4,6},{6,4},{1,3},{3,1},{5,7},{7,5},{8,10},{10,8},{12,... | collective-permute-start | bytes 884744 | tf_op jit(solution)/shard_map/ppermute | solution.py:25
  90.0 10.7 %collective-permute-start.29 = (f16[128,1152]{1,0:T(8,128)(2,1)S(1)}, f16[128,1152]{1,0:T(8,128)(2,1)S(1)}, u32[]{:S(2)}, u32[]{:S(2)}) collective-permute-start(f16[128,1152]{1,0:T(8,128)(2,1)S(1)} %slice_convert_fusion), channel_id=1, source_target_pairs={{2,4},{4,2},{6,0},{0,6},{3,5},{5,3},{7,1},{1,7},{10,12},{12,10},{1... | collective-permute-start | bytes 884744 | tf_op jit(solution)/shard_map/ppermute | solution.py:25
  92.7 4.8 %collective-permute-start.30 = (f32[1,3]{1,0:T(1,128)S(1)}, f32[1,3]{1,0:T(1,128)S(1)}, u32[]{:S(2)}, u32[]{:S(2)}) collective-permute-start(f32[1,3]{1,0:T(1,128)S(1)} %add.119), channel_id=1, source_target_pairs={{8,16},{16,8},{24,0},{0,24},{9,17},{17,9},{25,1},{1,25},{10,18},{1... | collective-permute-start | bytes 44 | tf_op jit(solution)/shard_map/ppermute | solution.py:25
  97.4 4.9 %collective-permute-start.31 = (f32[1,3]{1,0:T(1,128)S(1)}, f32[1,3]{1,0:T(1,128)S(1)}, u32[]{:S(2)}, u32[]{:S(2)}) collective-permute-start(f32[1,3]{1,0:T(1,128)S(1)} %add.126), channel_id=1, source_target_pairs={{0,32},{32,64},{64,96},{96,0},{1,33},{33,65},{65,97},{97,1},{2,34}... | collective-permute-start | bytes 44 | tf_op jit(solution)/shard_map/ppermute | solution.py:25
  97.5 5.0 %collective-permute-start.32 = (f32[1,3]{1,0:T(1,128)S(1)}, f32[1,3]{1,0:T(1,128)S(1)}, u32[]{:S(2)}, u32[]{:S(2)}) collective-permute-start(f32[1,3]{1,0:T(1,128)S(1)} %add.126), channel_id=1, source_target_pairs={{0,64},{32,96},{64,0},{96,32},{1,65},{33,97},{65,1},{97,33},{2,66}... | collective-permute-start | bytes 44 | tf_op jit(solution)/shard_map/ppermute | solution.py:25
  99.3 3.8 %collective-permute-start.33 = (f32[1,3]{1,0:T(1,128)S(1)}, f32[1,3]{1,0:T(1,128)S(1)}, u32[]{:S(2)}, u32[]{:S(2)}) collective-permute-start(f32[1,3]{1,0:T(1,128)S(1)} %add.126), channel_id=1, source_target_pairs={{0,96},{32,0},{64,32},{96,64},{1,97},{33,1},{65,33},{97,65},{2,98}... | collective-permute-start | bytes 44 | tf_op jit(solution)/shard_map/ppermute | solution.py:25

commit v7 on v6

--- a/solution.py
+++ b/solution.py
@@ -201,7 +201,7 @@
     texts = [t_own, t_low, t_high, s_own, s_low, s_high, t_far]
     weights = [weights_a, weights_b]
     tiles_c = place(2, [(3, j) for j in range(7)] + [(i, 6) for i in range(3)])
-    weights_c, sums_c, pi_far, pt_far = block(
+    weights_c, sums_c, pi_far = block(
         scalars,
         images,
         texts,
@@ -209,8 +209,8 @@
         where,
         tiles_c,
         None,
-        [(0, 0, "image", 3, tuple(range(7)), None), (1, 0, "text", 6, (0, 1, 2, 3), None)],
-        [1, 1],
+        [(0, 0, "image", 3, tuple(range(7)), None)],
+        [1],
     )
     weights_c, s_far = fence(weights_c, s_far)
     texts = texts + [s_far]
@@ -224,14 +224,15 @@
     *weights, ps_far, value = fence(*weights, narrow(ps_far), value)
     ps_far = send(ps_far, "c", SWAP)
     value = value + send(value, "c", SWAP)
-    pi_far, ps_near = block(
+    pi_far, ps_near, pt_far = block(
         None,
         images,
         texts,
         weights,
         where,
-        jobs=[(0, 0, "image", 3, (7,), 0)] + [(1, n, "text", j, (3,), 1) for n, j in enumerate((4, 5, 3))],
-        outs=[1, 3],
+        jobs=[(0, 0, "image", 3, (7,), 0), (2, 0, "text", 6, (0, 1, 2, 3), None)]
+        + [(1, n, "text", j, (3,), 1) for n, j in enumerate((4, 5, 3))],
+        outs=[1, 3, 1],
         before=[pi_far, ps_near],
     )
     ps_near = narrow(ps_near)

time: 104 us -> 104 us (level)
  waiting for transfers between devices: 36.1 us -> 32.4 us
  starting transfers between devices: 36 us -> 39 us
    ppermute x34, waiting for transfers between devices: 36.1 us -> 32.4 us  [send(): return lax.ppermute(value, axis, pairs)]
    ppermute x34, starting transfers between devices: 36 us -> 39 us  [send(): return lax.ppermute(value, axis, pairs)]
where the time goes in v7:
time: 104 us; the launch traced here: 103 us
  starting transfers between devices  39 us (38%)
  waiting for transfers between devices  32.4 us (31%)
  Pallas kernels  22.4 us (22%)
  other arithmetic  6.05 us (6%)
  between operations  2.34 us (2%)
    ppermute x34, starting transfers between devices, send(): return lax.ppermute(value, axis, pairs)  39 us
    ppermute x34, waiting for transfers between devices, send(): return lax.ppermute(value, axis, pairs)  32.4 us
    pallas_call x7, Pallas kernels, block(): pl.pallas_call(functools.partial(block_kernel, len(images), len(texts), l...  22.4 us
  transfers between devices with their start and end apart: 34, of which 14 were waited for; matrix products, arithmetic and copies ran while one was open for 3% of the time, Pallas kernels for 19%

profile of v7, /device:TPU:6, one launch (start us, length us, event | category | flops | bytes accessed | tf_op | source)
XLA Modules:
  0.0 102.9 jit_solution(15687222063093357976)
XLA Ops:
  0.6 1.1 %pad_maximum_fusion.1 = bf16[256,1152]{1,0:T(8,128)(2,1)S(1)} fusion(bf16[128,1152]{1,0:T(8,128)(2,1)} %param.5, bf16[128,1152]{1,0:T(8,128)(2,1)} %param.4), kind=kLoop, calls=%fused_computation.20 | loop fusion | flops 1179648 | bytes 1179648 | tf_op jit(solution)/shard_map/concatenate | solution.py:145
  1.7 0.2 fusion
  1.9 0.2 fusion.4
  2.2 2.0 %collective-permute-start = (bf16[128,1152]{1,0:T(8,128)(2,1)S(1)}, bf16[128,1152]{1,0:T(8,128)(2,1)S(1)}, u32[]{:S(2)}, u32[]{:S(2)}) collective-permute-start(bf16[128,1152]{1,0:T(8,128)(2,1)S(1)} %get-tuple-element.195), channel_id=1, source_target_pairs={{0,2},{2,0},{4,6},{6,4},{1,3},{3,1},{5,7},{7,5},{8,10},{10,8},{12,... | collective-permute-start | bytes 884744 | tf_op jit(solution)/shard_map/ppermute | solution.py:25
  4.2 2.5 %collective-permute-start.1 = (bf16[128,1152]{1,0:T(8,128)(2,1)S(1)}, bf16[128,1152]{1,0:T(8,128)(2,1)S(1)}, u32[]{:S(2)}, u32[]{:S(2)}) collective-permute-start(bf16[128,1152]{1,0:T(8,128)(2,1)S(1)} %get-tuple-element.194), channel_id=1, source_target_pairs={{2,4},{4,2},{6,0},{0,6},{3,5},{5,3},{7,1},{1,7},{10,12},{12,10},{1... | collective-permute-start | bytes 884744 | tf_op jit(solution)/shard_map/ppermute | solution.py:25
  6.7 4.5 %collective-permute-done = bf16[128,1152]{1,0:T(8,128)(2,1)S(1)} collective-permute-done((bf16[128,1152]{1,0:T(8,128)(2,1)S(1)}, bf16[128,1152]{1,0:T(8,128)(2,1)S(1)}, u32[]{:S(2)}, u32[]{:S(2)}) %collective-permute-start) | collective-permute-done | bytes 294944 | tf_op jit(solution)/shard_map/ppermute | solution.py:25
  11.2 0.5 collective-permute-start.2
  11.8 1.5 %collective-permute-start.3 = (bf16[256,1152]{1,0:T(8,128)(2,1)S(1)}, bf16[256,1152]{1,0:T(8,128)(2,1)S(1)}, u32[]{:S(2)}, u32[]{:S(2)}) collective-permute-start(bf16[256,1152]{1,0:T(8,128)(2,1)S(1)} %pad_maximum_fusion.2.refs_1_.refs_0_), channel_id=1, source_target_pairs={{0,24},{8,0},{16,8},{24,16},{1,25},{9,1},{17,9},{25,17},{2,26},{10... | collective-permute-start | bytes 1769480 | tf_op jit(solution)/shard_map/ppermute | solution.py:25
  13.3 0.5 collective-permute-done.1
  13.9 1.6 %collective-permute-start.4 = (bf16[256,1152]{1,0:T(8,128)(2,1)S(1)}, bf16[256,1152]{1,0:T(8,128)(2,1)S(1)}, u32[]{:S(2)}, u32[]{:S(2)}) collective-permute-start(bf16[256,1152]{1,0:T(8,128)(2,1)S(1)} %pad_maximum_fusion.3.refs_2_.refs_4_.refs_5_), channel_id=1, source_target_pairs={{0,32},{32,64},{64,96},{96,0},{1,33},{33,65},{65,97},{97,1},{2,34}... | collective-permute-start | bytes 1769480 | tf_op jit(solution)/shard_map/ppermute | solution.py:25
  15.6 1.7 %collective-permute-start.5 = (bf16[256,1152]{1,0:T(8,128)(2,1)S(1)}, bf16[256,1152]{1,0:T(8,128)(2,1)S(1)}, u32[]{:S(2)}, u32[]{:S(2)}) collective-permute-start(bf16[256,1152]{1,0:T(8,128)(2,1)S(1)} %pad_maximum_fusion.3.refs_2_.refs_4_.refs_5_), channel_id=1, source_target_pairs={{0,96},{32,0},{64,32},{96,64},{1,97},{33,1},{65,33},{97,65},{2,98}... | collective-permute-start | bytes 1769480 | tf_op jit(solution)/shard_map/ppermute | solution.py:25
  18.6 1.0 %shard_map.67 = (bf16[1,256,256]{2,1,0:T(8,128)(2,1)S(1)}, f32[3,8,256]{2,1,0:T(8,128)S(1)}) custom-call(f32[2]{0:T(128)S(1)} %pad_maximum_fusion.4.refs_0_, bf16[256,1152]{1,0:T(8,128)(2,1)S(1)} %pad_maximum_fusion.2.refs_1_.refs_0_, bf16[256,1152]{1,0:T(8,128)(2,1)S(1)} %pad_maximum_fusion.3.refs_2_.refs_4_.refs_5_), custom_call_target="tpu_custom_call" | custom-call | flops 1 | bytes 1 | tf_op jit(solution)/shard_map/pallas_call | solution.py:113
  19.7 6.0 %collective-permute-done.2.refs_2_.refs_1_ = bf16[256,1152]{1,0:T(8,128)(2,1)S(1)} collective-permute-done((bf16[256,1152]{1,0:T(8,128)(2,1)S(1)}, bf16[256,1152]{1,0:T(8,128)(2,1)S(1)}, u32[]{:S(2)}, u32[]{:S(2)}) %collective-permute-start.2) | collective-permute-done | bytes 589856 | tf_op jit(solution)/shard_map/ppermute | solution.py:25
  25.7 1.5 %collective-permute-done.3.refs_3_.refs_2_ = bf16[256,1152]{1,0:T(8,128)(2,1)S(1)} collective-permute-done((bf16[256,1152]{1,0:T(8,128)(2,1)S(1)}, bf16[256,1152]{1,0:T(8,128)(2,1)S(1)}, u32[]{:S(2)}, u32[]{:S(2)}) %collective-permute-start.3) | collective-permute-done | bytes 589856 | tf_op jit(solution)/shard_map/ppermute | solution.py:25
  27.2 1.9 %collective-permute-done.4.refs_5_.refs_6_ = bf16[256,1152]{1,0:T(8,128)(2,1)S(1)} collective-permute-done((bf16[256,1152]{1,0:T(8,128)(2,1)S(1)}, bf16[256,1152]{1,0:T(8,128)(2,1)S(1)}, u32[]{:S(2)}, u32[]{:S(2)}) %collective-permute-start.4) | collective-permute-done | bytes 589856 | tf_op jit(solution)/shard_map/ppermute | solution.py:25
  29.4 1.2 %collective-permute-start.8 = (bf16[128,1152]{1,0:T(8,128)(2,1)S(1)}, bf16[128,1152]{1,0:T(8,128)(2,1)S(1)}, u32[]{:S(2)}, u32[]{:S(2)}) collective-permute-start(bf16[128,1152]{1,0:T(8,128)(2,1)S(1)} %slice.75), channel_id=1, source_target_pairs={{0,8},{8,16},{16,24},{24,0},{1,9},{9,17},{17,25},{25,1},{2,10},{10... | collective-permute-start | bytes 884744 | tf_op jit(solution)/shard_map/ppermute | solution.py:25
  30.7 1.0 collective-permute-start.9
  31.6 1.6 %collective-permute-start.10 = (bf16[128,1152]{1,0:T(8,128)(2,1)S(1)}, bf16[128,1152]{1,0:T(8,128)(2,1)S(1)}, u32[]{:S(2)}, u32[]{:S(2)}) collective-permute-start(bf16[128,1152]{1,0:T(8,128)(2,1)S(1)} %slice.77), channel_id=1, source_target_pairs={{0,32},{32,64},{64,96},{96,0},{1,33},{33,65},{65,97},{97,1},{2,34}... | collective-permute-start | bytes 884744 | tf_op jit(solution)/shard_map/ppermute | solution.py:25
  33.2 1.7 %collective-permute-start.11 = (bf16[128,1152]{1,0:T(8,128)(2,1)S(1)}, bf16[128,1152]{1,0:T(8,128)(2,1)S(1)}, u32[]{:S(2)}, u32[]{:S(2)}) collective-permute-start(bf16[128,1152]{1,0:T(8,128)(2,1)S(1)} %slice.78), channel_id=1, source_target_pairs={{0,96},{32,0},{64,32},{96,64},{1,97},{33,1},{65,33},{97,65},{2,98}... | collective-permute-start | bytes 884744 | tf_op jit(solution)/shard_map/ppermute | solution.py:25
  34.9 3.3 %shard_map.68 = (bf16[11,256,256]{2,1,0:T(8,128)(2,1)S(1)}, f32[3,8,256]{2,1,0:T(8,128)S(1)}) custom-call(f32[2]{0:T(128)S(1)} %pad_maximum_fusion.4.refs_0_, bf16[256,1152]{1,0:T(8,128)(2,1)S(1)} %pad_maximum_fusion.2.refs_1_.refs_0_, bf16[256,1152]{1,0:T(8,128)(2,1)S(1)} %collective-permute-done.2.refs_2_.refs_1_, ...), custom_call_target="tpu_custom_call" | custom-call | flops 1 | bytes 1 | tf_op jit(solution)/shard_map/pallas_call | solution.py:113
  38.3 0.1 fusion.5
  38.4 3.7 %shard_map.69 = (bf16[6,256,256]{2,1,0:T(8,128)(2,1)S(1)}, f32[3,8,256]{2,1,0:T(8,128)S(1)}, f32[768,1152]{1,0:T(8,128)S(1)}) custom-call(f32[2]{0:T(128)S(1)} %pad_maximum_fusion.4.refs_0_, bf16[256,1152]{1,0:T(8,128)(2,1)S(1)} %pad_maximum_fusion.2.refs_1_.refs_0_, bf16[256,1152]{1,0:T(8,128)(2,1)S(1)} %collective-permute-done.2.refs_2_.refs_1_, ...), custom_call_target="tpu_custom_call" | custom-call | flops 1 | bytes 1 | tf_op jit(solution)/shard_map/pallas_call | solution.py:113
  42.2 0.3 collective-permute-start.13
  42.5 4.0 %shard_map.70 = (bf16[10,256,256]{2,1,0:T(8,128)(2,1)S(1)}, f32[3,8,256]{2,1,0:T(8,128)S(1)}, f32[256,1152]{1,0:T(8,128)S(1)}) custom-call(f32[2]{0:T(128)S(1)} %pad_maximum_fusion.4.refs_0_, bf16[256,1152]{1,0:T(8,128)(2,1)S(1)} %pad_maximum_fusion.2.refs_1_.refs_0_, bf16[256,1152]{1,0:T(8,128)(2,1)S(1)} %collective-permute-done.2.refs_2_.refs_1_, ...), custom_call_target="tpu_custom_call" | custom-call | flops 1 | bytes 1 | tf_op jit(solution)/shard_map/pallas_call | solution.py:113
  46.5 2.5 %shard_map.71 = (bf16[4,256,256]{2,1,0:T(8,128)(2,1)S(1)}, f32[3,8,256]{2,1,0:T(8,128)S(1)}, f32[256,1152]{1,0:T(8,128)S(1)}) custom-call(f32[2]{0:T(128)S(1)} %pad_maximum_fusion.4.refs_0_, bf16[256,1152]{1,0:T(8,128)(2,1)S(1)} %pad_maximum_fusion.2.refs_1_.refs_0_, bf16[256,1152]{1,0:T(8,128)(2,1)S(1)} %collective-permute-done.2.refs_2_.refs_1_, ...), custom_call_target="tpu_custom_call" | custom-call | flops 1 | bytes 1 | tf_op jit(solution)/shard_map/pallas_call | solution.py:113
  49.1 0.1 add_reduce_fusion
  49.2 0.5 collective-permute-start.14
  49.7 1.6 %shard_map.72 = (f32[256,1152]{1,0:T(8,128)S(1)}, f32[768,1152]{1,0:T(8,128)S(1)}, f32[256,1152]{1,0:T(8,128)S(1)}) custom-call(bf16[256,1152]{1,0:T(8,128)(2,1)S(1)} %pad_maximum_fusion.2.refs_1_.refs_0_, bf16[256,1152]{1,0:T(8,128)(2,1)S(1)} %collective-permute-done.2.refs_2_.refs_1_, bf16[256,1152]{1,0:T(8,128)(2,1)S(1)} %collective-permute-done.3.refs_3_.refs_2_, ...), custom_call_target="tpu_custom_call" | custom-call | flops 1 | bytes 1 | tf_op jit(solution)/shard_map/pallas_call | solution.py:113
  51.4 0.2 convert_element_type.78
  51.6 0.1 collective-permute-start.15
  51.7 1.1 %collective-permute-done.15 = f32[1,3]{1,0:T(1,128)S(1)} collective-permute-done((f32[1,3]{1,0:T(1,128)S(1)}, f32[1,3]{1,0:T(1,128)S(1)}, u32[]{:S(2)}, u32[]{:S(2)}) %collective-permute-start.15) | collective-permute-done | bytes 44 | tf_op jit(solution)/shard_map/ppermute | solution.py:25
  52.8 0.2 add_convert_fusion.4
  53.0 0.3 collective-permute-start.20
  53.3 0.1 fusion.7
  53.4 0.9 collective-permute-start.16
  54.3 2.4 %collective-permute-start.17 = (f16[128,1152]{1,0:T(8,128)(2,1)S(1)}, f16[128,1152]{1,0:T(8,128)(2,1)S(1)}, u32[]{:S(2)}, u32[]{:S(2)}) collective-permute-start(f16[128,1152]{1,0:T(8,128)(2,1)S(1)} %get-tuple-element.192), channel_id=1, source_target_pairs={{0,8},{8,16},{16,24},{24,0},{1,9},{9,17},{17,25},{25,1},{2,10},{10... | collective-permute-start | bytes 884744 | tf_op jit(solution)/shard_map/ppermute | solution.py:25
  56.7 0.1 fusion.6
  56.8 2.7 %collective-permute-start.18 = (f16[128,1152]{1,0:T(8,128)(2,1)S(1)}, f16[128,1152]{1,0:T(8,128)(2,1)S(1)}, u32[]{:S(2)}, u32[]{:S(2)}) collective-permute-start(f16[128,1152]{1,0:T(8,128)(2,1)S(1)} %get-tuple-element.191), channel_id=1, source_target_pairs={{0,96},{32,0},{64,32},{96,64},{1,97},{33,1},{65,33},{97,65},{2,98}... | collective-permute-start | bytes 884744 | tf_op jit(solution)/shard_map/ppermute | solution.py:25
  59.4 6.3 %shard_map.73 = (f32[256,1152]{1,0:T(8,128)S(1)}, f32[256,1152]{1,0:T(8,128)S(1)}, f32[256,1152]{1,0:T(8,128)S(1)}, f32[256,1152]{1,0:T(8,128)S(1)}, f32[256,1152]{1,0:T(8,128)S(1)}, /*index=5*/f32[256,1152]{1,0:T(8,128)S(1)}) custom-call(bf16[256,1152]{1,0:T(8,128)(2,1)S(1)} %pad_maximum_fusion.2.refs_1_.refs_0_, ...), custom_call_target="tpu_custom_call" | custom-call | flops 1 | bytes 1 | tf_op jit(solution)/shard_map/pallas_call | solution.py:113
  65.8 0.4 convert_add_fusion.2
  66.2 2.8 %collective-permute-done.19 = f16[128,1152]{1,0:T(8,128)(2,1)S(1)} collective-permute-done((f16[128,1152]{1,0:T(8,128)(2,1)S(1)}, f16[128,1152]{1,0:T(8,128)(2,1)S(1)}, u32[]{:S(2)}, u32[]{:S(2)}) %collective-permute-start.19) | collective-permute-done | bytes 294944 | tf_op jit(solution)/shard_map/ppermute | solution.py:25
  69.0 0.2 add_convert_fusion.2
  69.3 0.2 add_convert_fusion
  69.6 3.2 %collective-permute-start.22 = (f16[256,1152]{1,0:T(8,128)(2,1)S(1)}, f16[256,1152]{1,0:T(8,128)(2,1)S(1)}, u32[]{:S(2)}, u32[]{:S(2)}) collective-permute-start(f16[256,1152]{1,0:T(8,128)(2,1)S(1)} %get-tuple-element.158), channel_id=1, source_target_pairs={{0,8},{8,16},{16,24},{24,0},{1,9},{9,17},{17,25},{25,1},{2,10},{10... | collective-permute-start | bytes 1769480 | tf_op jit(solution)/shard_map/ppermute | solution.py:25
  72.8 0.5 collective-permute-start.23
  73.3 1.6 %collective-permute-start.24 = (f16[256,1152]{1,0:T(8,128)(2,1)S(1)}, f16[256,1152]{1,0:T(8,128)(2,1)S(1)}, u32[]{:S(2)}, u32[]{:S(2)}) collective-permute-start(f16[256,1152]{1,0:T(8,128)(2,1)S(1)} %get-tuple-element.160), channel_id=1, source_target_pairs={{0,32},{32,64},{64,96},{96,0},{1,33},{33,65},{65,97},{97,1},{2,34}... | collective-permute-start | bytes 1769480 | tf_op jit(solution)/shard_map/ppermute | solution.py:25
  74.8 1.1 %collective-permute-start.25 = (f32[1,3]{1,0:T(1,128)S(1)}, f32[1,3]{1,0:T(1,128)S(1)}, u32[]{:S(2)}, u32[]{:S(2)}) collective-permute-start(f32[1,3]{1,0:T(1,128)S(1)} %add.109), channel_id=1, source_target_pairs={{0,2},{2,0},{4,6},{6,4},{1,3},{3,1},{5,7},{7,5},{8,10},{10,8},{12,... | collective-permute-start | bytes 44 | tf_op jit(solution)/shard_map/ppermute | solution.py:25
  75.9 2.5 %collective-permute-done.25 = f32[1,3]{1,0:T(1,128)S(1)} collective-permute-done((f32[1,3]{1,0:T(1,128)S(1)}, f32[1,3]{1,0:T(1,128)S(1)}, u32[]{:S(2)}, u32[]{:S(2)}) %collective-permute-start.25) | collective-permute-done | bytes 44 | tf_op jit(solution)/shard_map/ppermute | solution.py:25
  78.4 3.2 %collective-permute-start.26 = (f32[1,3]{1,0:T(1,128)S(1)}, f32[1,3]{1,0:T(1,128)S(1)}, u32[]{:S(2)}, u32[]{:S(2)}) collective-permute-start(f32[1,3]{1,0:T(1,128)S(1)} %add.117), channel_id=1, source_target_pairs={{2,4},{4,2},{6,0},{0,6},{3,5},{5,3},{7,1},{1,7},{10,12},{12,10},{1... | collective-permute-start | bytes 44 | tf_op jit(solution)/shard_map/ppermute | solution.py:25
  81.6 1.6 %collective-permute-done.26 = f32[1,3]{1,0:T(1,128)S(1)} collective-permute-done((f32[1,3]{1,0:T(1,128)S(1)}, f32[1,3]{1,0:T(1,128)S(1)}, u32[]{:S(2)}, u32[]{:S(2)}) %collective-permute-start.26) | collective-permute-done | bytes 44 | tf_op jit(solution)/shard_map/ppermute | solution.py:25
  83.1 3.5 %collective-permute-done.27 = f32[1,3]{1,0:T(1,128)S(1)} collective-permute-done((f32[1,3]{1,0:T(1,128)S(1)}, f32[1,3]{1,0:T(1,128)S(1)}, u32[]{:S(2)}, u32[]{:S(2)}) %collective-permute-start.27) | collective-permute-done | bytes 44 | tf_op jit(solution)/shard_map/ppermute | solution.py:25
  86.7 1.4 %collective-permute-done.24 = f16[256,1152]{1,0:T(8,128)(2,1)S(1)} collective-permute-done((f16[256,1152]{1,0:T(8,128)(2,1)S(1)}, f16[256,1152]{1,0:T(8,128)(2,1)S(1)}, u32[]{:S(2)}, u32[]{:S(2)}) %collective-permute-start.24) | collective-permute-done | bytes 589856 | tf_op jit(solution)/shard_map/ppermute | solution.py:25
  88.1 0.2 convert_add_fusion.1
  88.3 0.3 convert_add_fusion
  88.6 3.3 %collective-permute-start.29 = (f16[128,1152]{1,0:T(8,128)(2,1)S(1)}, f16[128,1152]{1,0:T(8,128)(2,1)S(1)}, u32[]{:S(2)}, u32[]{:S(2)}) collective-permute-start(f16[128,1152]{1,0:T(8,128)(2,1)S(1)} %slice_convert_fusion), channel_id=1, source_target_pairs={{2,4},{4,2},{6,0},{0,6},{3,5},{5,3},{7,1},{1,7},{10,12},{12,10},{1... | collective-permute-start | bytes 884744 | tf_op jit(solution)/shard_map/ppermute | solution.py:25
  91.9 0.4 collective-permute-start.30
  92.3 4.4 %collective-permute-done.30 = f32[1,3]{1,0:T(1,128)S(1)} collective-permute-done((f32[1,3]{1,0:T(1,128)S(1)}, f32[1,3]{1,0:T(1,128)S(1)}, u32[]{:S(2)}, u32[]{:S(2)}) %collective-permute-start.30) | collective-permute-done | bytes 44 | tf_op jit(solution)/shard_map/ppermute | solution.py:25
  96.7 1.8 %collective-permute-start.32 = (f32[1,3]{1,0:T(1,128)S(1)}, f32[1,3]{1,0:T(1,128)S(1)}, u32[]{:S(2)}, u32[]{:S(2)}) collective-permute-start(f32[1,3]{1,0:T(1,128)S(1)} %add.126), channel_id=1, source_target_pairs={{0,64},{32,96},{64,0},{96,32},{1,65},{33,97},{65,1},{97,33},{2,66}... | collective-permute-start | bytes 44 | tf_op jit(solution)/shard_map/ppermute | solution.py:25
  98.4 1.4 %collective-permute-start.33 = (f32[1,3]{1,0:T(1,128)S(1)}, f32[1,3]{1,0:T(1,128)S(1)}, u32[]{:S(2)}, u32[]{:S(2)}) collective-permute-start(f32[1,3]{1,0:T(1,128)S(1)} %add.126), channel_id=1, source_target_pairs={{0,96},{32,0},{64,32},{96,64},{1,97},{33,1},{65,33},{97,65},{2,98}... | collective-permute-start | bytes 44 | tf_op jit(solution)/shard_map/ppermute | solution.py:25
  99.9 0.3 multiply_reduce_fusion
  100.2 1.3 %subtract_multiply_fusion = (f32[128,1152]{1,0:T(8,128)}, f32[128,1152]{1,0:T(8,128)}) fusion(f32[256,1152]{1,0:T(8,128)S(1)} %get-tuple-element.189, f16[128,1152]{1,0:T(8,128)(2,1)S(1)} %collective-permute-done.29, f32[256,1152]{1,0:T(8,128)S(1)} %convert_add_fusion, f32[128]{0:T(128)S(1)} %get-tuple-element.196, f32[128]{0:T(128)S(1)} %get-tuple-element.179, ...), kind=kLoop, calls=%fused_computation.23 | loop fusion | flops 1769472 | bytes 4130820 | tf_op jit(solution)/shard_map/mul | solution.py:40
  101.6 0.1 collective-permute-done.32
  101.7 0.6 collective-permute-done.33
  102.3 0.6 fusion.3
  (54 shorter events, 1.0 us)
Async XLA Ops:
  2.2 9.0 %collective-permute-start = (bf16[128,1152]{1,0:T(8,128)(2,1)S(1)}, bf16[128,1152]{1,0:T(8,128)(2,1)S(1)}, u32[]{:S(2)}, u32[]{:S(2)}) collective-permute-start(bf16[128,1152]{1,0:T(8,128)(2,1)S(1)} %get-tuple-element.195), channel_id=1, source_target_pairs={{0,2},{2,0},{4,6},{6,4},{1,3},{3,1},{5,7},{7,5},{8,10},{10,8},{12,... | collective-permute-start | bytes 884744 | tf_op jit(solution)/shard_map/ppermute | solution.py:25
  4.2 9.7 %collective-permute-start.1 = (bf16[128,1152]{1,0:T(8,128)(2,1)S(1)}, bf16[128,1152]{1,0:T(8,128)(2,1)S(1)}, u32[]{:S(2)}, u32[]{:S(2)}) collective-permute-start(bf16[128,1152]{1,0:T(8,128)(2,1)S(1)} %get-tuple-element.194), channel_id=1, source_target_pairs={{2,4},{4,2},{6,0},{0,6},{3,5},{5,3},{7,1},{1,7},{10,12},{12,10},{1... | collective-permute-start | bytes 884744 | tf_op jit(solution)/shard_map/ppermute | solution.py:25
  6.7 10.5 %collective-permute-start.6 = (bf16[128,1152]{1,0:T(8,128)(2,1)S(1)}, bf16[128,1152]{1,0:T(8,128)(2,1)S(1)}, u32[]{:S(2)}, u32[]{:S(2)}) collective-permute-start(bf16[128,1152]{1,0:T(8,128)(2,1)S(1)} %get-tuple-element.194), channel_id=1, source_target_pairs={{0,1},{1,0},{2,3},{3,2},{4,5},{5,4},{6,7},{7,6},{8,9},{9,8},{10,11... | collective-permute-start | bytes 884744 | tf_op jit(solution)/shard_map/ppermute | solution.py:25
  11.2 14.5 %collective-permute-start.2 = (bf16[256,1152]{1,0:T(8,128)(2,1)S(1)}, bf16[256,1152]{1,0:T(8,128)(2,1)S(1)}, u32[]{:S(2)}, u32[]{:S(2)}) collective-permute-start(bf16[256,1152]{1,0:T(8,128)(2,1)S(1)} %pad_maximum_fusion.2.refs_1_.refs_0_), channel_id=1, source_target_pairs={{0,8},{8,16},{16,24},{24,0},{1,9},{9,17},{17,25},{25,1},{2,10},{10... | collective-permute-start | bytes 1769480 | tf_op jit(solution)/shard_map/ppermute | solution.py:25
  11.8 15.4 %collective-permute-start.3 = (bf16[256,1152]{1,0:T(8,128)(2,1)S(1)}, bf16[256,1152]{1,0:T(8,128)(2,1)S(1)}, u32[]{:S(2)}, u32[]{:S(2)}) collective-permute-start(bf16[256,1152]{1,0:T(8,128)(2,1)S(1)} %pad_maximum_fusion.2.refs_1_.refs_0_), channel_id=1, source_target_pairs={{0,24},{8,0},{16,8},{24,16},{1,25},{9,1},{17,9},{25,17},{2,26},{10... | collective-permute-start | bytes 1769480 | tf_op jit(solution)/shard_map/ppermute | solution.py:25
  13.9 15.2 %collective-permute-start.4 = (bf16[256,1152]{1,0:T(8,128)(2,1)S(1)}, bf16[256,1152]{1,0:T(8,128)(2,1)S(1)}, u32[]{:S(2)}, u32[]{:S(2)}) collective-permute-start(bf16[256,1152]{1,0:T(8,128)(2,1)S(1)} %pad_maximum_fusion.3.refs_2_.refs_4_.refs_5_), channel_id=1, source_target_pairs={{0,32},{32,64},{64,96},{96,0},{1,33},{33,65},{65,97},{97,1},{2,34}... | collective-permute-start | bytes 1769480 | tf_op jit(solution)/shard_map/ppermute | solution.py:25
  15.6 13.6 %collective-permute-start.5 = (bf16[256,1152]{1,0:T(8,128)(2,1)S(1)}, bf16[256,1152]{1,0:T(8,128)(2,1)S(1)}, u32[]{:S(2)}, u32[]{:S(2)}) collective-permute-start(bf16[256,1152]{1,0:T(8,128)(2,1)S(1)} %pad_maximum_fusion.3.refs_2_.refs_4_.refs_5_), channel_id=1, source_target_pairs={{0,96},{32,0},{64,32},{96,64},{1,97},{33,1},{65,33},{97,65},{2,98}... | collective-permute-start | bytes 1769480 | tf_op jit(solution)/shard_map/ppermute | solution.py:25
  17.2 2.5 %collective-permute-start.7 = (bf16[128,1152]{1,0:T(8,128)(2,1)S(1)}, bf16[128,1152]{1,0:T(8,128)(2,1)S(1)}, u32[]{:S(2)}, u32[]{:S(2)}) collective-permute-start(bf16[128,1152]{1,0:T(8,128)(2,1)S(1)} %collective-permute-done.1), channel_id=1, source_target_pairs={{0,1},{1,0},{2,3},{3,2},{4,5},{5,4},{6,7},{7,6},{8,9},{9,8},{10,11... | collective-permute-start | bytes 884744 | tf_op jit(solution)/shard_map/ppermute | solution.py:25
  29.3 9.0 %collective-permute-start.12 = (bf16[512,1152]{1,0:T(8,128)(2,1)S(1)}, bf16[512,1152]{1,0:T(8,128)(2,1)S(1)}, u32[]{:S(2)}, u32[]{:S(2)}) collective-permute-start(bf16[512,1152]{1,0:T(8,128)(2,1)S(1)} %pad_maximum_fusion), channel_id=1, source_target_pairs={{0,1},{1,0},{2,3},{3,2},{4,5},{5,4},{6,7},{7,6},{8,9},{9,8},{10,11... | collective-permute-start | bytes 3538952 | tf_op jit(solution)/shard_map/ppermute | solution.py:25
  29.4 12.6 %collective-permute-start.8 = (bf16[128,1152]{1,0:T(8,128)(2,1)S(1)}, bf16[128,1152]{1,0:T(8,128)(2,1)S(1)}, u32[]{:S(2)}, u32[]{:S(2)}) collective-permute-start(bf16[128,1152]{1,0:T(8,128)(2,1)S(1)} %slice.75), channel_id=1, source_target_pairs={{0,8},{8,16},{16,24},{24,0},{1,9},{9,17},{17,25},{25,1},{2,10},{10... | collective-permute-start | bytes 884744 | tf_op jit(solution)/shard_map/ppermute | solution.py:25
  30.7 11.4 %collective-permute-start.9 = (bf16[128,1152]{1,0:T(8,128)(2,1)S(1)}, bf16[128,1152]{1,0:T(8,128)(2,1)S(1)}, u32[]{:S(2)}, u32[]{:S(2)}) collective-permute-start(bf16[128,1152]{1,0:T(8,128)(2,1)S(1)} %slice.76), channel_id=1, source_target_pairs={{0,24},{8,0},{16,8},{24,16},{1,25},{9,1},{17,9},{25,17},{2,26},{10... | collective-permute-start | bytes 884744 | tf_op jit(solution)/shard_map/ppermute | solution.py:25
  31.6 10.5 %collective-permute-start.10 = (bf16[128,1152]{1,0:T(8,128)(2,1)S(1)}, bf16[128,1152]{1,0:T(8,128)(2,1)S(1)}, u32[]{:S(2)}, u32[]{:S(2)}) collective-permute-start(bf16[128,1152]{1,0:T(8,128)(2,1)S(1)} %slice.77), channel_id=1, source_target_pairs={{0,32},{32,64},{64,96},{96,0},{1,33},{33,65},{65,97},{97,1},{2,34}... | collective-permute-start | bytes 884744 | tf_op jit(solution)/shard_map/ppermute | solution.py:25
  33.2 8.9 %collective-permute-start.11 = (bf16[128,1152]{1,0:T(8,128)(2,1)S(1)}, bf16[128,1152]{1,0:T(8,128)(2,1)S(1)}, u32[]{:S(2)}, u32[]{:S(2)}) collective-permute-start(bf16[128,1152]{1,0:T(8,128)(2,1)S(1)} %slice.78), channel_id=1, source_target_pairs={{0,96},{32,0},{64,32},{96,64},{1,97},{33,1},{65,33},{97,65},{2,98}... | collective-permute-start | bytes 884744 | tf_op jit(solution)/shard_map/ppermute | solution.py:25
  42.2 4.4 %collective-permute-start.13 = (bf16[256,1152]{1,0:T(8,128)(2,1)S(1)}, bf16[256,1152]{1,0:T(8,128)(2,1)S(1)}, u32[]{:S(2)}, u32[]{:S(2)}) collective-permute-start(bf16[256,1152]{1,0:T(8,128)(2,1)S(1)} %constant_dynamic-update-slice_fusion.4.refs_11_.refs_10_), channel_id=1, source_target_pairs={{0,1},{1,0},{2,3},{3,2},{4,5},{5,4},{6,7},{7,6},{8,9},{9,8},{10,11... | collective-permute-start | bytes 1769480 | tf_op jit(solution)/shard_map/ppermute | solution.py:25
  49.2 3.6 %collective-permute-start.14 = (f16[256,1152]{1,0:T(8,128)(2,1)S(1)}, f16[256,1152]{1,0:T(8,128)(2,1)S(1)}, u32[]{:S(2)}, u32[]{:S(2)}) collective-permute-start(f16[256,1152]{1,0:T(8,128)(2,1)S(1)} %convert_element_type.74), channel_id=1, source_target_pairs={{0,1},{1,0},{2,3},{3,2},{4,5},{5,4},{6,7},{7,6},{8,9},{9,8},{10,11... | collective-permute-start | bytes 1769480 | tf_op jit(solution)/shard_map/ppermute | solution.py:25
  51.6 1.2 %collective-permute-start.15 = (f32[1,3]{1,0:T(1,128)S(1)}, f32[1,3]{1,0:T(1,128)S(1)}, u32[]{:S(2)}, u32[]{:S(2)}) collective-permute-start(f32[1,3]{1,0:T(1,128)S(1)} %bitcast.4), channel_id=1, source_target_pairs={{0,1},{1,0},{2,3},{3,2},{4,5},{5,4},{6,7},{7,6},{8,9},{9,8},{10,11... | collective-permute-start | bytes 44 | tf_op jit(solution)/shard_map/ppermute | solution.py:25
  53.0 12.8 %collective-permute-start.20 = (f16[768,1152]{1,0:T(8,128)(2,1)S(1)}, f16[768,1152]{1,0:T(8,128)(2,1)S(1)}, u32[]{:S(2)}, u32[]{:S(2)}) collective-permute-start(f16[768,1152]{1,0:T(8,128)(2,1)S(1)} %convert_element_type.78), channel_id=1, source_target_pairs={{0,1},{1,0},{2,3},{3,2},{4,5},{5,4},{6,7},{7,6},{8,9},{9,8},{10,11... | collective-permute-start | bytes 5308424 | tf_op jit(solution)/shard_map/ppermute | solution.py:25
  53.4 12.8 %collective-permute-start.16 = (f16[128,1152]{1,0:T(8,128)(2,1)S(1)}, f16[128,1152]{1,0:T(8,128)(2,1)S(1)}, u32[]{:S(2)}, u32[]{:S(2)}) collective-permute-start(f16[128,1152]{1,0:T(8,128)(2,1)S(1)} %get-tuple-element.193), channel_id=1, source_target_pairs={{0,24},{8,0},{16,8},{24,16},{1,25},{9,1},{17,9},{25,17},{2,26},{10... | collective-permute-start | bytes 884744 | tf_op jit(solution)/shard_map/ppermute | solution.py:25
  54.3 11.9 %collective-permute-start.17 = (f16[128,1152]{1,0:T(8,128)(2,1)S(1)}, f16[128,1152]{1,0:T(8,128)(2,1)S(1)}, u32[]{:S(2)}, u32[]{:S(2)}) collective-permute-start(f16[128,1152]{1,0:T(8,128)(2,1)S(1)} %get-tuple-element.192), channel_id=1, source_target_pairs={{0,8},{8,16},{16,24},{24,0},{1,9},{9,17},{17,25},{25,1},{2,10},{10... | collective-permute-start | bytes 884744 | tf_op jit(solution)/shard_map/ppermute | solution.py:25
  56.8 9.5 %collective-permute-start.18 = (f16[128,1152]{1,0:T(8,128)(2,1)S(1)}, f16[128,1152]{1,0:T(8,128)(2,1)S(1)}, u32[]{:S(2)}, u32[]{:S(2)}) collective-permute-start(f16[128,1152]{1,0:T(8,128)(2,1)S(1)} %get-tuple-element.191), channel_id=1, source_target_pairs={{0,96},{32,0},{64,32},{96,64},{1,97},{33,1},{65,33},{97,65},{2,98}... | collective-permute-start | bytes 884744 | tf_op jit(solution)/shard_map/ppermute | solution.py:25
  59.4 9.6 %collective-permute-start.19 = (f16[128,1152]{1,0:T(8,128)(2,1)S(1)}, f16[128,1152]{1,0:T(8,128)(2,1)S(1)}, u32[]{:S(2)}, u32[]{:S(2)}) collective-permute-start(f16[128,1152]{1,0:T(8,128)(2,1)S(1)} %get-tuple-element.190), channel_id=1, source_target_pairs={{0,32},{32,64},{64,96},{96,0},{1,33},{33,65},{65,97},{97,1},{2,34}... | collective-permute-start | bytes 884744 | tf_op jit(solution)/shard_map/ppermute | solution.py:25
  69.5 17.2 %collective-permute-start.21 = (f16[256,1152]{1,0:T(8,128)(2,1)S(1)}, f16[256,1152]{1,0:T(8,128)(2,1)S(1)}, u32[]{:S(2)}, u32[]{:S(2)}) collective-permute-start(f16[256,1152]{1,0:T(8,128)(2,1)S(1)} %get-tuple-element.157), channel_id=1, source_target_pairs={{0,24},{8,0},{16,8},{24,16},{1,25},{9,1},{17,9},{25,17},{2,26},{10... | collective-permute-start | bytes 1769480 | tf_op jit(solution)/shard_map/ppermute | solution.py:25
  69.6 17.1 %collective-permute-start.22 = (f16[256,1152]{1,0:T(8,128)(2,1)S(1)}, f16[256,1152]{1,0:T(8,128)(2,1)S(1)}, u32[]{:S(2)}, u32[]{:S(2)}) collective-permute-start(f16[256,1152]{1,0:T(8,128)(2,1)S(1)} %get-tuple-element.158), channel_id=1, source_target_pairs={{0,8},{8,16},{16,24},{24,0},{1,9},{9,17},{17,25},{25,1},{2,10},{10... | collective-permute-start | bytes 1769480 | tf_op jit(solution)/shard_map/ppermute | solution.py:25
  72.8 13.9 %collective-permute-start.23 = (f16[256,1152]{1,0:T(8,128)(2,1)S(1)}, f16[256,1152]{1,0:T(8,128)(2,1)S(1)}, u32[]{:S(2)}, u32[]{:S(2)}) collective-permute-start(f16[256,1152]{1,0:T(8,128)(2,1)S(1)} %get-tuple-element.159), channel_id=1, source_target_pairs={{0,96},{32,0},{64,32},{96,64},{1,97},{33,1},{65,33},{97,65},{2,98}... | collective-permute-start | bytes 1769480 | tf_op jit(solution)/shard_map/ppermute | solution.py:25
  73.3 14.8 %collective-permute-start.24 = (f16[256,1152]{1,0:T(8,128)(2,1)S(1)}, f16[256,1152]{1,0:T(8,128)(2,1)S(1)}, u32[]{:S(2)}, u32[]{:S(2)}) collective-permute-start(f16[256,1152]{1,0:T(8,128)(2,1)S(1)} %get-tuple-element.160), channel_id=1, source_target_pairs={{0,32},{32,64},{64,96},{96,0},{1,33},{33,65},{65,97},{97,1},{2,34}... | collective-permute-start | bytes 1769480 | tf_op jit(solution)/shard_map/ppermute | solution.py:25
  74.8 3.5 %collective-permute-start.25 = (f32[1,3]{1,0:T(1,128)S(1)}, f32[1,3]{1,0:T(1,128)S(1)}, u32[]{:S(2)}, u32[]{:S(2)}) collective-permute-start(f32[1,3]{1,0:T(1,128)S(1)} %add.109), channel_id=1, source_target_pairs={{0,2},{2,0},{4,6},{6,4},{1,3},{3,1},{5,7},{7,5},{8,10},{10,8},{12,... | collective-permute-start | bytes 44 | tf_op jit(solution)/shard_map/ppermute | solution.py:25
  78.4 4.8 %collective-permute-start.26 = (f32[1,3]{1,0:T(1,128)S(1)}, f32[1,3]{1,0:T(1,128)S(1)}, u32[]{:S(2)}, u32[]{:S(2)}) collective-permute-start(f32[1,3]{1,0:T(1,128)S(1)} %add.117), channel_id=1, source_target_pairs={{2,4},{4,2},{6,0},{0,6},{3,5},{5,3},{7,1},{1,7},{10,12},{12,10},{1... | collective-permute-start | bytes 44 | tf_op jit(solution)/shard_map/ppermute | solution.py:25
  83.1 3.5 %collective-permute-start.27 = (f32[1,3]{1,0:T(1,128)S(1)}, f32[1,3]{1,0:T(1,128)S(1)}, u32[]{:S(2)}, u32[]{:S(2)}) collective-permute-start(f32[1,3]{1,0:T(1,128)S(1)} %add.118), channel_id=1, source_target_pairs={{0,8},{8,0},{16,24},{24,16},{1,9},{9,1},{17,25},{25,17},{2,10},{10... | collective-permute-start | bytes 44 | tf_op jit(solution)/shard_map/ppermute | solution.py:25
  88.6 11.3 %collective-permute-start.29 = (f16[128,1152]{1,0:T(8,128)(2,1)S(1)}, f16[128,1152]{1,0:T(8,128)(2,1)S(1)}, u32[]{:S(2)}, u32[]{:S(2)}) collective-permute-start(f16[128,1152]{1,0:T(8,128)(2,1)S(1)} %slice_convert_fusion), channel_id=1, source_target_pairs={{2,4},{4,2},{6,0},{0,6},{3,5},{5,3},{7,1},{1,7},{10,12},{12,10},{1... | collective-permute-start | bytes 884744 | tf_op jit(solution)/shard_map/ppermute | solution.py:25
  91.9 8.0 %collective-permute-start.28 = (f16[128,1152]{1,0:T(8,128)(2,1)S(1)}, f16[128,1152]{1,0:T(8,128)(2,1)S(1)}, u32[]{:S(2)}, u32[]{:S(2)}) collective-permute-start(f16[128,1152]{1,0:T(8,128)(2,1)S(1)} %slice_convert_fusion.1), channel_id=1, source_target_pairs={{0,2},{2,0},{4,6},{6,4},{1,3},{3,1},{5,7},{7,5},{8,10},{10,8},{12,... | collective-permute-start | bytes 884744 | tf_op jit(solution)/shard_map/ppermute | solution.py:25
  91.9 4.8 %collective-permute-start.30 = (f32[1,3]{1,0:T(1,128)S(1)}, f32[1,3]{1,0:T(1,128)S(1)}, u32[]{:S(2)}, u32[]{:S(2)}) collective-permute-start(f32[1,3]{1,0:T(1,128)S(1)} %add.119), channel_id=1, source_target_pairs={{8,16},{16,8},{24,0},{0,24},{9,17},{17,9},{25,1},{1,25},{10,18},{1... | collective-permute-start | bytes 44 | tf_op jit(solution)/shard_map/ppermute | solution.py:25
  96.6 4.9 %collective-permute-start.31 = (f32[1,3]{1,0:T(1,128)S(1)}, f32[1,3]{1,0:T(1,128)S(1)}, u32[]{:S(2)}, u32[]{:S(2)}) collective-permute-start(f32[1,3]{1,0:T(1,128)S(1)} %add.126), channel_id=1, source_target_pairs={{0,32},{32,64},{64,96},{96,0},{1,33},{33,65},{65,97},{97,1},{2,34}... | collective-permute-start | bytes 44 | tf_op jit(solution)/shard_map/ppermute | solution.py:25
  96.7 5.0 %collective-permute-start.32 = (f32[1,3]{1,0:T(1,128)S(1)}, f32[1,3]{1,0:T(1,128)S(1)}, u32[]{:S(2)}, u32[]{:S(2)}) collective-permute-start(f32[1,3]{1,0:T(1,128)S(1)} %add.126), channel_id=1, source_target_pairs={{0,64},{32,96},{64,0},{96,32},{1,65},{33,97},{65,1},{97,33},{2,66}... | collective-permute-start | bytes 44 | tf_op jit(solution)/shard_map/ppermute | solution.py:25
  98.4 3.8 %collective-permute-start.33 = (f32[1,3]{1,0:T(1,128)S(1)}, f32[1,3]{1,0:T(1,128)S(1)}, u32[]{:S(2)}, u32[]{:S(2)}) collective-permute-start(f32[1,3]{1,0:T(1,128)S(1)} %add.126), channel_id=1, source_target_pairs={{0,96},{32,0},{64,32},{96,64},{1,97},{33,1},{65,33},{97,65},{2,98}... | collective-permute-start | bytes 44 | tf_op jit(solution)/shard_map/ppermute | solution.py:25
